TPU v7x, 256 devices: a whole 4x4x8 slice. The times are simulated.
256 devices in a mesh: grp: 8 (over x_lo, y), tile: 32 (over x_hi, z, core).
Axes of the slice: x: 4 (x_hi: 2, x_lo: 2; x = x_hi * 2 + x_lo), y: 4, z: 8, core: 2. Of those that a mesh axis runs over, the one named last changes fastest.
Arguments:
- acts: bfloat16 [2048, 5120], P(('grp', 'tile')), may hold values from -6 to 6
- grads: bfloat16 [2048, 20480], P(('grp', 'tile')), may hold values from -6 to 6
- basis_in: bfloat16 [5120, 2560], P(None, 'tile'), may hold values from -0.078125 to 0.078125
- basis_out: bfloat16 [20480, 10240], P('grp', 'tile'), may hold values from -0.0390625 to 0.0390625
- tenant: int32 [8], replicated, may hold values from 0 to 1, as said below
Outputs:
- held_out: float32 [2, 10240, 2560], P(None, ('tile', 'grp'))
Inputs may be any that keep to these rules, and one draw needn't show every extreme that they name: Each tenant owns exactly 4 of the sequences.
All inputs are finite; a program needn't handle non-finite values.
Results may differ from a plain program's by a relative error of at most 0.017.
Values may be sent and summed in bfloat16 or wider, within the bound.
No kernel may reach another device: no remote copies, remote signals or barrier semaphores. Data moves between devices by JAX's collectives and lax.ppermute only.
A program may use at most 128 MiB of HBM per device.

v0:
```python
import jax
import jax.numpy as jnp
from jax import lax
from jax.sharding import PartitionSpec as P

SEQ_GRP = 1
TENANTS = 2


def shards(acts, grads, basis_in, basis_out, tenant):
    groups = lax.axis_size("grp")
    group_index = lax.axis_index("grp")
    input_cols = jnp.dot(
        lax.all_gather(acts, "tile", axis=0, tiled=True),
        basis_in,
        preferred_element_type=jnp.float32,
    ).astype(jnp.bfloat16)
    rotated_in = lax.all_gather(input_cols, "tile", axis=1, tiled=True)
    group_tokens = rotated_in.shape[0]
    owned_cols = basis_out.shape[1]
    whole_grads = lax.all_gather(grads, "tile", axis=0, tiled=True)
    rotated_out = jnp.dot(
        whole_grads,
        lax.all_gather(basis_out, "grp", axis=0, tiled=True),
        preferred_element_type=jnp.float32,
    )
    rotated_out = rotated_out.astype(jnp.bfloat16)
    seq_len = group_tokens // SEQ_GRP
    left = rotated_out.reshape(SEQ_GRP, seq_len, owned_cols)
    right = rotated_in.reshape(SEQ_GRP, seq_len, rotated_in.shape[1])
    corr = jnp.einsum("slr,slc->src", left, right, preferred_element_type=jnp.float32)
    square = corr * corr
    own_tenants = lax.dynamic_slice_in_dim(tenant, group_index * SEQ_GRP, SEQ_GRP)
    owners = (own_tenants[:, None] == jnp.arange(TENANTS, dtype=jnp.int32)[None, :]).astype(
        jnp.float32
    )
    group_part = jnp.einsum("sk,src->krc", owners, square)
    sums = lax.psum_scatter(
        group_part.astype(jnp.bfloat16), "grp", scatter_dimension=1, tiled=True
    ).astype(jnp.float32)
    total = jnp.sum(sums, axis=0)
    seq_count = SEQ_GRP * groups
    scale = 1.0 / float((seq_count - seq_count // TENANTS) * seq_len)
    return (total[None] - sums) * scale


def solution(mesh):
    return jax.shard_map(
        shards,
        mesh=mesh,
        in_specs=(
            P(("grp", "tile"), None),
            P(("grp", "tile"), None),
            P(None, "tile"),
            P("grp", "tile"),
            P(),
        ),
        out_specs=P(None, ("tile", "grp"), None),
        check_vma=False,
    )
```

profile of v0, /device:TPU:1, one launch (start us, length us, event | category | flops | bytes accessed | tf_op | source)
XLA Modules:
  0.0 481.1 jit_solution(2832983357224209007)
XLA Ops:
  6.5 0.0 copy-start
  6.5 0.0 copy-start.1
  6.5 0.0 all-gather.9.cloned.1.call-start
  6.5 0.7 all-gather.9.cloned.1.call-update
  7.3 0.0 all-gather.5.cloned.1.call-start
  7.3 0.7 all-gather.5.cloned.1.call-update
  8.0 0.0 all-gather.7.cloned.1.call-start
  8.1 0.7 all-gather.7.cloned.1.call-update
  8.7 0.0 all-gather.11.cloned.1.call-start
  8.8 87.3 %all-gather.9.cloned.1.call-done = bf16[256,5120]{1,0:T(8,128)(2,1)} async-done(((bf16[8,5120]{1,0:T(8,128)(2,1)}), bf16[256,5120]{1,0:T(8,128)(2,1)}) %all-gather.9.cloned.1.call-update) | async-done | bytes 2621456 | tf_op jit(solution)/shard_map/all_gather | solution.py:14
  96.1 0.0 copy-done
  96.1 3.3 convolution_convert_fusion.1
  99.4 0.0 all-gather.11.cloned.1.call-update
  99.4 0.0 reduce-scatter.4.cloned.1.call-start
  99.5 0.0 copy-done.1
  99.5 0.6 dynamic_slice.3
  100.1 0.6 compare_convert_fusion
  100.8 104.0 %all-gather.5.cloned.1.call-done = bf16[256,20480]{1,0:T(8,128)(2,1)} async-done(((bf16[8,20480]{1,0:T(8,128)(2,1)}), bf16[256,20480]{1,0:T(8,128)(2,1)}) %all-gather.5.cloned.1.call-update) | async-done | bytes 10485776 | tf_op jit(solution)/shard_map/all_gather | solution.py:21
  204.8 136.9 %all-gather.7.cloned.1.call-done = bf16[20480,320]{0,1:T(8,128)(2,1)} async-done(((bf16[2560,320]{0,1:T(8,128)(2,1)}), bf16[20480,320]{0,1:T(8,128)(2,1)}) %all-gather.7.cloned.1.call-update) | async-done | bytes 13107216 | tf_op jit(solution)/shard_map/all_gather | solution.py:24
  341.7 15.8 %convolution_convert_fusion = bf16[256,320]{1,0:T(8,128)(2,1)S(1)} fusion(bf16[256,20480]{1,0:T(8,128)(2,1)} %all-gather.5.cloned.1.call-done, bf16[20480,320]{0,1:T(8,128)(2,1)} %all-gather.7.cloned.1.call-done), kind=kOutput, calls=%fused_computation.2 | convolution fusion | flops 3355525120 | bytes 23756800 | tf_op jit(solution)/shard_map/dot_general | solution.py:22
  357.4 64.4 %all-gather.11.cloned.1.call-done = bf16[256,2560]{0,1:T(8,128)(2,1)} async-done(((bf16[256,80]{0,1:T(8,128)(2,1)}), bf16[256,2560]{0,1:T(8,128)(2,1)}) %all-gather.11.cloned.1.call-update) | async-done | bytes 1310736 | tf_op jit(solution)/shard_map/all_gather | solution.py:18
  421.9 2.1 convolution_multiply_fusion
  424.0 0.6 multiply_convert_fusion
  424.6 3.4 copy.6
  428.0 2.2 copy.8
  430.1 0.0 reduce-scatter.4.cloned.1.call-update
  430.2 42.1 %reduce-scatter.4.cloned.1.call-done = bf16[40,5120]{1,0:T(8,128)(2,1)} async-done(((bf16[320,5120]{1,0:T(8,128)(2,1)}), bf16[40,5120]{1,0:T(8,128)(2,1)}) %reduce-scatter.4.cloned.1.call-update) | async-done | bytes 409616
  472.2 1.3 reshape.23
  473.5 0.1 convert_reduce_fusion
  473.6 1.0 fusion
Async XLA Ops:
  6.5 89.6 %copy-start = (bf16[5120,80]{0,1:T(8,128)(2,1)S(1)}, bf16[5120,80]{0,1:T(8,128)(2,1)}, u32[]{:S(2)}) copy-start(bf16[5120,80]{0,1:T(8,128)(2,1)} %param.7) | copy-start | bytes 2457604
  6.5 93.0 %copy-start.1 = (s32[8]{0:T(128)S(1)}, s32[8]{0:T(128)}, u32[]{:S(2)}) copy-start(s32[8]{0:T(128)} %param.9) | copy-start | bytes 100
  6.5 89.6 %all-gather.9.cloned.1.call-start = ((), (), s32[]{:S(2)}) async-start(), calls=%async_computation.3 | async-start | bytes 2703360 | tf_op jit(solution)/shard_map/all_gather | solution.py:14
  7.3 197.5 %all-gather.5.cloned.1.call-start = ((), (), s32[]{:S(2)}) async-start(), calls=%async_computation.1 | async-start | bytes 10813440 | tf_op jit(solution)/shard_map/all_gather | solution.py:21
  8.0 333.7 %all-gather.7.cloned.1.call-start = ((), (), s32[]{:S(2)}) async-start(), calls=%async_computation.2 | async-start | bytes 14745600 | tf_op jit(solution)/shard_map/all_gather | solution.py:24
  8.7 413.1 %all-gather.11.cloned.1.call-start = ((), (), s32[]{:S(2)}) async-start(), calls=%async_computation.4 | async-start | bytes 1351680 | tf_op jit(solution)/shard_map/all_gather | solution.py:18
  99.4 372.8 %reduce-scatter.4.cloned.1.call-start = ((), (), s32[]{:S(2)}) async-start(), calls=%async_computation.5 | async-start | bytes 3686400
Sparse Core Ops, SparseCore 0:
  10.1 85.9 all-gather.8
  98.9 105.8 all-gather.4
  206.6 135.0 all-gather.6
  344.3 77.5 all-gather.10
  430.3 41.8 reduce-scatter.3
where the time goes:
time: 484 us; the launch traced here: 481 us
  waiting for transfers between devices  437 us (90%)
  matrix products  21.2 us (4%)
  between operations  13.2 us (3%)
  local copies, waits for them, and re-layouts  7.48 us (2%)
    all_gather x1, waiting for transfers between devices, shards(): lax.all_gather(basis_out, 'grp', axis=0, tiled=True)  137 us
    all_gather x1, waiting for transfers between devices, shards(): whole_grads = lax.all_gather(grads, 'tile', axis=0, tiled=True)  104 us
    all_gather x1, waiting for transfers between devices, shards(): lax.all_gather(acts, 'tile', axis=0, tiled=True)  87.3 us
    all_gather x1, waiting for transfers between devices, shards(): rotated_in = lax.all_gather(input_cols, 'tile', axis=1, tiled=True)  64.4 us
    unnamed x6, waiting for transfers between devices  44.2 us
    dot_general x1, matrix products, shards(): jnp.dot(whole_grads, lax.all_gather(basis_out, 'grp', axis=0, tiled=True)...  15.8 us
  transfers between devices with their start and end apart: 5, of which 5 were waited for; matrix products, arithmetic and copies ran while one was open for 4% of the time, Pallas kernels for 0%

commit v1 on v0

v1 whole, which is shorter than its diff:
```python
import jax
import jax.numpy as jnp
import numpy as np
from jax import lax
from jax.sharding import Mesh, PartitionSpec as P

SEQ_GRP = 1
TENANTS = 2
AXES = ("xl", "y", "xh", "z", "core")
SIZES = (2, 4, 2, 8, 2)
GRP = ("xl", "y")
PLANE = ("xl", "y", "xh")
BF16, F32 = jnp.bfloat16, jnp.float32


def shift(x, axis, step):
    count = SIZES[AXES.index(axis)]
    return lax.ppermute(x, axis, [(i, (i + step) % count) for i in range(count)])


def swapped(x, axis):
    other = shift(x, axis, 1)
    first = lax.axis_index(axis) == 0
    return jnp.stack([jnp.where(first, x, other), jnp.where(first, other, x)])


def shards(acts, grads, basis_in, basis_out, tenant):
    tokens, hidden = grads.shape
    model = acts.shape[1]
    own_in, own_out = basis_in.shape[1], basis_out.shape[1]
    groups, planes = 8, 16
    rows = hidden // planes

    sent = grads.reshape(tokens, planes, rows).transpose(1, 0, 2)
    panel = lax.all_to_all(sent, PLANE, 0, 0).reshape(planes * tokens, rows)

    halves = basis_out.T.reshape(own_out, 2, rows).transpose(1, 0, 2)
    mine = lax.all_to_all(halves, "xh", 0, 0)
    weights = jnp.stack([mine, shift(mine, "core", 1)], axis=1)
    weights = weights.reshape(2, 2 * own_out, rows)

    every = lax.all_gather(acts, "z", axis=0, tiled=True)
    pair = basis_in.T
    pair = swapped(pair, "xh")
    pair = swapped(pair, "core")
    cols = pair.transpose(1, 0, 2, 3).reshape(4 * own_in, model)
    rotated = lax.dot_general(
        cols, every, (((1,), (1,)), ((), ())), preferred_element_type=F32
    ).astype(BF16)
    blocks = lax.all_to_all(
        rotated.reshape(4, own_in, 8 * tokens), ("xh", "core"), 0, 0
    )
    blocks = blocks.transpose(1, 0, 2).reshape(own_in, 32 * tokens)
    spread = jnp.broadcast_to(blocks[None], (32,) + blocks.shape)
    rotated_in = lax.all_to_all(spread, ("xh", "z", "core"), 0, 0)
    rotated_in = rotated_in.reshape(32 * own_in, 32 * tokens)

    up, down = [panel], [panel]
    for _ in range(3):
        up.append(shift(up[-1], "z", 1))
        down.append(shift(down[-1], "z", -1))
    half = panel.shape[0] // 2
    last = jnp.concatenate(
        [shift(up[3][:half], "z", 1), shift(down[3][half:], "z", -1)], axis=0
    )

    def partial(parts):
        left = jnp.stack([p.reshape(groups, 2 * tokens, rows) for p in parts], axis=1)
        left = left.reshape(groups * len(parts) * 2 * tokens, rows)
        out = jnp.stack(
            [
                lax.dot_general(
                    left,
                    weights[h],
                    (((1,), (1,)), ((), ())),
                    preferred_element_type=F32,
                ).astype(BF16)
                for h in range(2)
            ]
        )
        out = out.reshape(planes, len(parts) * 2 * tokens, 2 * own_out)
        got = lax.all_to_all(out, ("xh", "xl", "y"), 0, 0)
        return jnp.sum(got.astype(F32), axis=0).astype(BF16)

    first = partial([panel, up[1], down[1], up[2], down[2]])
    second = partial([up[3], down[3], last])
    mixed = jnp.concatenate([first, second], axis=0)
    other = shift(mixed[:, own_out:], "core", 1)
    both = jnp.stack([mixed[:, :own_out], other]).reshape(2, 8, 2, tokens, own_out)

    core_rel, slot, half_x, row = np.unravel_index(
        np.arange(32 * tokens), (2, 8, 2, tokens)
    )
    offset = np.array([0, 7, 1, 6, 2, 5, 3, 4])[slot]
    core_of = (lax.axis_index("core") + core_rel) % 2
    z_of = (lax.axis_index("z") + offset) % 8
    source = ((half_x * 2 + core_of) * 8 + z_of) * tokens + row
    pick = (jnp.arange(32 * tokens)[:, None] == source[None, :]).astype(BF16)
    rolled = jnp.dot(
        rotated_in, pick, preferred_element_type=F32
    ).astype(BF16)

    left = both.reshape(32 * tokens, own_out)
    corr = lax.dot_general(
        left, rolled, (((0,), (1,)), ((), ())), preferred_element_type=F32
    )
    square = (corr * corr).astype(BF16)
    parts = lax.all_to_all(
        square.reshape(groups, own_out // groups, square.shape[1]), GRP, 0, 0
    ).astype(F32)
    sums = jnp.stack(
        [
            jnp.sum(jnp.where((tenant == k)[:, None, None], parts, 0.0), axis=0)
            for k in range(TENANTS)
        ]
    )
    total = jnp.sum(sums, axis=0)
    seq_count = SEQ_GRP * groups
    scale = 1.0 / float((seq_count - seq_count // TENANTS) * 32 * tokens)
    return (total[None] - sums) * scale


def solution(mesh):
    fine = Mesh(mesh.devices.reshape(SIZES), AXES)
    tile = ("xh", "z", "core")
    return jax.shard_map(
        shards,
        mesh=fine,
        in_specs=(
            P(AXES, None),
            P(AXES, None),
            P(None, tile),
            P(GRP, tile),
            P(),
        ),
        out_specs=P(None, tile + GRP, None),
        check_vma=False,
    )
```

time: 484 us -> 248 us (0.51)
  waiting for transfers between devices: 437 us -> 92.6 us
  starting transfers between devices: 0.16 us -> 97.7 us
  blocking collectives: 0 us -> 22.5 us
  between operations: 13.2 us -> 0.35 us
  matrix products: 21.2 us -> 12.6 us
  local copies, waits for them, and re-layouts: 7.48 us -> 14.6 us
    all_gather x4 -> x0, waiting for transfers between devices: 393 us -> none  [the longest x1 137 us: shards(): lax.all_gather(basis_out, 'grp', axis=0, tiled=True)]
    all_to_all x0 -> x7, waiting for transfers between devices: none -> 84.2 us  [the longest x1 32.2 us: shards(): rotated_in = lax.all_to_all(spread, ('xh', 'z', 'core'), 0, 0)]
    all_to_all x0 -> x7, starting transfers between devices: none -> 71.4 us  [the longest x2 36.8 us: partial(): got = lax.all_to_all(out, ('xh', 'xl', 'y'), 0, 0)]
    unnamed x6 -> x0, waiting for transfers between devices: 44.2 us -> none
    ppermute x0 -> x12, starting transfers between devices: none -> 26.3 us  [shift(): lax.ppermute(x, axis, [(i, (i + step) % count) for i in range(count)])]
    all_gather x0 -> x1, blocking collectives: none -> 22.5 us  [shards(): every = lax.all_gather(acts, 'z', axis=0, tiled=True)]
    dot_general x3 -> x6, matrix products: 21.2 us -> 12.6 us  [the longest x4 7.83 us: partial(): lax.dot_general(left, weights[h], (((1,), (1,)), ((), ())), preferred_ele...]
    ppermute x0 -> x12, waiting for transfers between devices: none -> 8.45 us  [shift(): lax.ppermute(x, axis, [(i, (i + step) % count) for i in range(count)])]
  transfers between devices with their start and end apart: 5 -> 19, of which waited for: 5 -> 9; matrix products, arithmetic and copies ran while one was open for 4% -> 10% of each run, Pallas kernels for 0% -> 0%
where the time goes in v1:
time: 248 us; the launch traced here: 247 us
  starting transfers between devices  97.7 us (39%)
  waiting for transfers between devices  92.6 us (37%)
  blocking collectives  22.5 us (9%)
  local copies, waits for them, and re-layouts  14.6 us (6%)
  matrix products  12.6 us (5%)
  other arithmetic  6.99 us (3%)
    all_to_all x2, starting transfers between devices, partial(): got = lax.all_to_all(out, ('xh', 'xl', 'y'), 0, 0)  36.8 us
    all_to_all x1, waiting for transfers between devices, shards(): rotated_in = lax.all_to_all(spread, ('xh', 'z', 'core'), 0, 0)  32.2 us
    all_to_all x2, waiting for transfers between devices, partial(): got = lax.all_to_all(out, ('xh', 'xl', 'y'), 0, 0)  27 us
    ppermute x12, starting transfers between devices, shift(): lax.ppermute(x, axis, [(i, (i + step) % count) for i in range(count)])  26.3 us
    all_gather x1, blocking collectives, shards(): every = lax.all_gather(acts, 'z', axis=0, tiled=True)  22.5 us
    all_to_all x1, waiting for transfers between devices, shards(): lax.all_to_all(square.reshape(groups, own_out // groups, square.shape[1])...  21.2 us
    all_to_all x1, starting transfers between devices, shards(): rotated_in = lax.all_to_all(spread, ('xh', 'z', 'core'), 0, 0)  10.6 us
    all_to_all x1, starting transfers between devices, shards(): lax.all_to_all(rotated.reshape(4, own_in, 8 * tokens), ('xh', 'core'), 0, 0)  8.77 us
  transfers between devices with their start and end apart: 19, of which 9 were waited for; matrix products, arithmetic and copies ran while one was open for 10% of the time, Pallas kernels for 0%

profile of v1, /device:TPU:1, one launch (start us, length us, event | category | flops | bytes accessed | tf_op | source)
XLA Modules:
  0.0 247.3 jit_solution(17646098395686545451)
XLA Ops:
  0.0 7.6 %all-to-all-start = ((bf16[16,8,1280]{2,1,0:T(8,128)(2,1)}), bf16[16,8,1280]{2,1,0:T(8,128)(2,1)S(1)}, u32[]{:S(2)}, u32[]{:S(2)}) async-start(bf16[16,8,1280]{2,1,0:T(8,128)(2,1)} %bitcast.91), calls=%async_computation | async-start | bytes 655360 | tf_op jit(solution)/shard_map/all_to_all | solution.py:35
  7.6 2.9 %collective-permute-start.10 = (bf16[80,5120]{1,0:T(8,128)(2,1)}, bf16[80,5120]{1,0:T(8,128)(2,1)}, u32[]{:S(2)}, u32[]{:S(2)}) collective-permute-start(bf16[80,5120]{1,0:T(8,128)(2,1)} %bitcast.88), channel_id=1, source_target_pairs={{0,16},{16,0},{1,17},{17,1},{2,18},{18,2},{3,19},{19,3},{4,20},{20... | collective-permute-start | bytes 2457608 | tf_op jit(solution)/shard_map/ppermute | solution.py:18
  10.5 3.8 %reshape.54 = bf16[320,2,1280]{2,1,0:T(2,128)(2,1)S(1)} reshape(bf16[320,2560]{1,0:T(8,128)(2,1)} %bitcast.76) | data formatting | bytes 3276800 | tf_op jit(solution)/shard_map/reshape | solution.py:37
  14.3 1.4 copy.17
  15.6 3.8 %all-to-all-start.1 = ((bf16[2,320,1280]{2,1,0:T(8,128)(2,1)}), bf16[2,320,1280]{2,1,0:T(8,128)(2,1)S(1)}, u32[]{:S(2)}, u32[]{:S(2)}) async-start(bf16[2,320,1280]{2,1,0:T(8,128)(2,1)} %copy.17), calls=%async_computation.1 | async-start | bytes 3276800 | tf_op jit(solution)/shard_map/all_to_all | solution.py:38
  19.5 1.7 collective-permute-start
  21.2 4.0 %collective-permute-start.1 = (bf16[128,1280]{1,0:T(8,128)(2,1)S(1)}, bf16[128,1280]{1,0:T(8,128)(2,1)}, u32[]{:S(2)}, u32[]{:S(2)}) collective-permute-start(bf16[128,1280]{1,0:T(8,128)(2,1)S(1)} %bitcast.83), channel_id=1, source_target_pairs={{0,14},{2,0},{4,2},{6,4},{8,6},{10,8},{12,10},{14,12},{1,15},{3,1}... | collective-permute-start | bytes 983048 | tf_op jit(solution)/shard_map/ppermute | solution.py:18
  25.2 22.5 %all_gather.3 = bf16[64,5120]{1,0:T(8,128)(2,1)S(1)} all-gather(bf16[8,5120]{1,0:T(8,128)(2,1)S(1)} %copy-done.7), channel_id=1, replica_groups=mesh['xl'=2,'y'=4,'xh'=2,'z'=8,'core'=2] {'z'}, dimensions={0}, use_global_device_ids=true | all-gather | bytes 737280 | tf_op jit(solution)/shard_map/all_gather | solution.py:42
  47.7 0.8 constant_dynamic-update-slice_fusion.4
  48.5 2.0 collective-permute-start.2
  50.4 0.7 collective-permute-start.3
  51.2 1.7 constant_dynamic-update-slice_fusion.3
  52.9 1.7 constant_dynamic-update-slice_fusion.2
  54.6 8.4 %collective-permute-start.4 = (bf16[2,320,1280]{2,1,0:T(8,128)(2,1)S(1)}, bf16[2,320,1280]{2,1,0:T(8,128)(2,1)S(1)}, u32[]{:S(2)}, u32[]{:S(2)}) collective-permute-start(bf16[2,320,1280]{2,1,0:T(8,128)(2,1)S(1)} %all-to-all-done.1), channel_id=1, source_target_pairs={{0,1},{1,0},{2,3},{3,2},{4,5},{5,4},{6,7},{7,6},{8,9},{9,8},{10,11... | collective-permute-start | bytes 4915208 | tf_op jit(solution)/shard_map/ppermute | solution.py:18
  63.0 1.3 select_bitcast_fusion.3
  64.3 1.4 collective-permute-start.6
  65.7 0.1 collective-permute-start.5
  65.9 0.2 pad_maximum_fusion.3
  66.0 2.3 collective-permute-start.11
  68.3 3.8 %collective-permute-done.6 = bf16[128,1280]{1,0:T(8,128)(2,1)S(1)} collective-permute-done((bf16[128,1280]{1,0:T(8,128)(2,1)S(1)}, bf16[128,1280]{1,0:T(8,128)(2,1)S(1)}, u32[]{:S(2)}, u32[]{:S(2)}) %collective-permute-start.6) | collective-permute-done | bytes 327712 | tf_op jit(solution)/shard_map/ppermute | solution.py:18
  72.1 2.1 collective-permute-start.8
  74.3 0.3 collective-permute-start.7
  74.5 1.7 constant_dynamic-update-slice_fusion.1
  76.2 0.4 collective-permute-done.8
  76.7 3.2 %collective-permute-done.7 = bf16[64,1280]{1,0:T(8,128)(2,1)S(1)} collective-permute-done((bf16[64,1280]{1,0:T(8,128)(2,1)S(1)}, bf16[64,1280]{1,0:T(8,128)(2,1)S(1)}, u32[]{:S(2)}, u32[]{:S(2)}) %collective-permute-start.7) | collective-permute-done | bytes 163872 | tf_op jit(solution)/shard_map/ppermute | solution.py:18
  79.9 0.1 pad_maximum_fusion.4
  80.0 0.3 fusion.3
  80.4 1.0 fusion.7
  81.3 0.2 copy-done.2
  81.5 0.5 copy-done
  82.0 1.0 fusion.6
  83.0 0.2 select_bitcast_fusion.1
  83.2 0.3 pad_maximum_fusion
  83.5 1.1 convolution_convert_fusion.5
  84.6 0.1 reshape.59
  84.7 0.6 copy.19
  85.4 8.8 %all-to-all-start.4 = ((bf16[4,80,64]{1,2,0:T(8,128)(2,1)}), bf16[4,80,64]{1,2,0:T(8,128)(2,1)S(1)}, u32[]{:S(2)}, u32[]{:S(2)}) async-start(bf16[4,80,64]{1,2,0:T(8,128)(2,1)} %copy.19), calls=%async_computation.4 | async-start | bytes 131072 | tf_op jit(solution)/shard_map/all_to_all | solution.py:50
  94.1 1.1 pad_maximum_fusion.5
  95.2 3.7 %all-to-all-done.4 = bf16[4,80,64]{1,2,0:T(8,128)(2,1)S(1)} async-done(((bf16[4,80,64]{1,2,0:T(8,128)(2,1)}), bf16[4,80,64]{1,2,0:T(8,128)(2,1)S(1)}, u32[]{:S(2)}, u32[]{:S(2)}) %all-to-all-start.4) | async-done | bytes 40992 | tf_op jit(solution)/shard_map/all_to_all | solution.py:50
  98.9 32.8 %all-to-all-start.3 = ((bf16[16,48,640]{2,1,0:T(8,128)(2,1)}), bf16[16,48,640]{2,1,0:T(8,128)(2,1)S(1)}, u32[]{:S(2)}, u32[]{:S(2)}) async-start(bf16[16,48,640]{2,1,0:T(8,128)(2,1)} %bitcast.24), calls=%async_computation.3 | async-start | bytes 1966080 | tf_op jit(solution)/shard_map/all_to_all | solution.py:82
  131.7 0.8 constant_dynamic-update-slice_fusion
  132.5 3.0 %fusion.5 = bf16[1,640,640]{2,1,0:T(8,128)(2,1)S(1)} fusion(bf16[640,1280]{1,0:T(8,128)(2,1)} %bitcast.8, bf16[640,1280]{1,0:T(8,128)(2,1)S(1)} %bitcast.81), kind=kOutput, calls=%fused_computation.19 | convolution fusion | flops 1048985600 | bytes 4096000 | tf_op jit(solution)/shard_map/dot_general | solution.py:72
  135.5 2.9 %fusion.4 = bf16[1,640,640]{2,1,0:T(8,128)(2,1)S(1)} fusion(bf16[640,1280]{1,0:T(8,128)(2,1)} %bitcast.8, bf16[640,1280]{1,0:T(8,128)(2,1)S(1)} %bitcast.79), kind=kOutput, calls=%fused_computation.18 | convolution fusion | flops 1048985600 | bytes 4096000 | tf_op jit(solution)/shard_map/dot_general | solution.py:72
  138.4 1.4 pad_maximum_fusion.2
  139.8 6.5 %all-to-all-done.3 = bf16[16,48,640]{2,1,0:T(8,128)(2,1)S(1)} async-done(((bf16[16,48,640]{2,1,0:T(8,128)(2,1)}), bf16[16,48,640]{2,1,0:T(8,128)(2,1)S(1)}, u32[]{:S(2)}, u32[]{:S(2)}) %all-to-all-start.3) | async-done | bytes 983072 | tf_op jit(solution)/shard_map/all_to_all | solution.py:82
  146.3 3.9 %all-to-all-start.2 = ((bf16[16,80,640]{2,1,0:T(8,128)(2,1)}), bf16[16,80,640]{2,1,0:T(8,128)(2,1)S(1)}, u32[]{:S(2)}, u32[]{:S(2)}) async-start(bf16[16,80,640]{2,1,0:T(8,128)(2,1)} %bitcast.17), calls=%async_computation.2 | async-start | bytes 3276800 | tf_op jit(solution)/shard_map/all_to_all | solution.py:82
  150.3 0.1 copy.20
  150.4 20.5 %all-to-all-done.2 = bf16[16,80,640]{2,1,0:T(8,128)(2,1)S(1)} async-done(((bf16[16,80,640]{2,1,0:T(8,128)(2,1)}), bf16[16,80,640]{2,1,0:T(8,128)(2,1)S(1)}, u32[]{:S(2)}, u32[]{:S(2)}) %all-to-all-start.2) | async-done | bytes 1638432 | tf_op jit(solution)/shard_map/all_to_all | solution.py:82
  170.9 1.2 broadcast_in_dim.32
  172.1 10.6 %all-to-all-start.5 = ((bf16[32,80,256]{2,1,0:T(8,128)(2,1)}), bf16[32,80,256]{2,1,0:T(8,128)(2,1)}, u32[]{:S(2)}, u32[]{:S(2)}) async-start(bf16[32,80,256]{2,1,0:T(8,128)(2,1)} %broadcast_in_dim.32), calls=%async_computation.5 | async-start | bytes 2621440 | tf_op jit(solution)/shard_map/all_to_all | solution.py:55
  182.7 0.0 copy-start.8
  182.7 0.0 copy-start.9
  182.7 0.0 copy-start.10
  182.7 0.1 reduce_sum.53
  182.8 0.2 reduce_sum.52
  183.1 0.1 fusion.12
  183.2 0.4 collective-permute-start.9
  183.6 1.0 collective-permute-done.9
  184.6 32.2 %all-to-all-done.5 = bf16[32,80,256]{2,1,0:T(8,128)(2,1)} async-done(((bf16[32,80,256]{2,1,0:T(8,128)(2,1)}), bf16[32,80,256]{2,1,0:T(8,128)(2,1)}, u32[]{:S(2)}, u32[]{:S(2)}) %all-to-all-start.5) | async-done | bytes 1310752 | tf_op jit(solution)/shard_map/all_to_all | solution.py:55
  216.9 3.6 %fusion = bf16[320,2560]{1,0:T(8,128)(2,1)} fusion(bf16[256,320]{1,0:T(8,128)(2,1)S(1)} %bitcast.94, bf16[2560,256]{1,0:T(8,128)(2,1)} %bitcast.38, s32[256]{0:T(256)S(1)} %fusion.18), kind=kOutput, calls=%fused_computation.3 | convolution fusion | flops 757334016 | bytes 3113984 | tf_op jit(solution)/shard_map/dot_general | solution.py:104
  220.5 3.9 %all-to-all-start.6 = ((bf16[8,40,2560]{2,1,0:T(8,128)(2,1)}), bf16[8,40,2560]{2,1,0:T(8,128)(2,1)S(1)}, u32[]{:S(2)}, u32[]{:S(2)}) async-start(bf16[8,40,2560]{2,1,0:T(8,128)(2,1)} %bitcast.39), calls=%async_computation.6 | async-start | bytes 3276800 | tf_op jit(solution)/shard_map/all_to_all | solution.py:108
  224.4 21.2 %all-to-all-done.6 = bf16[8,40,2560]{2,1,0:T(8,128)(2,1)S(1)} async-done(((bf16[8,40,2560]{2,1,0:T(8,128)(2,1)}), bf16[8,40,2560]{2,1,0:T(8,128)(2,1)S(1)}, u32[]{:S(2)}, u32[]{:S(2)}) %all-to-all-start.6) | async-done | bytes 1638432 | tf_op jit(solution)/shard_map/all_to_all | solution.py:108
  245.6 0.6 fusion.1
  246.3 1.0 fusion.8
  (38 shorter events, 0.2 us)
Async XLA Ops:
  0.0 15.6 %all-to-all-start = ((bf16[16,8,1280]{2,1,0:T(8,128)(2,1)}), bf16[16,8,1280]{2,1,0:T(8,128)(2,1)S(1)}, u32[]{:S(2)}, u32[]{:S(2)}) async-start(bf16[16,8,1280]{2,1,0:T(8,128)(2,1)} %bitcast.91), calls=%async_computation | async-start | bytes 655360 | tf_op jit(solution)/shard_map/all_to_all | solution.py:35
  7.6 55.4 %collective-permute-start.10 = (bf16[80,5120]{1,0:T(8,128)(2,1)}, bf16[80,5120]{1,0:T(8,128)(2,1)}, u32[]{:S(2)}, u32[]{:S(2)}) collective-permute-start(bf16[80,5120]{1,0:T(8,128)(2,1)} %bitcast.88), channel_id=1, source_target_pairs={{0,16},{16,0},{1,17},{17,1},{2,18},{18,2},{3,19},{19,3},{4,20},{20... | collective-permute-start | bytes 2457608 | tf_op jit(solution)/shard_map/ppermute | solution.py:18
  15.6 9.6 %copy-start.7 = (bf16[8,5120]{1,0:T(8,128)(2,1)S(1)}, bf16[8,5120]{1,0:T(8,128)(2,1)}, u32[]{:S(2)}) copy-start(bf16[8,5120]{1,0:T(8,128)(2,1)} %param.9) | copy-start | bytes 245764
  15.6 39.0 %all-to-all-start.1 = ((bf16[2,320,1280]{2,1,0:T(8,128)(2,1)}), bf16[2,320,1280]{2,1,0:T(8,128)(2,1)S(1)}, u32[]{:S(2)}, u32[]{:S(2)}) async-start(bf16[2,320,1280]{2,1,0:T(8,128)(2,1)} %copy.17), calls=%async_computation.1 | async-start | bytes 3276800 | tf_op jit(solution)/shard_map/all_to_all | solution.py:38
  19.4 43.6 %copy-start.4 = (bf16[5120,80]{0,1:T(8,128)(2,1)S(1)}, bf16[5120,80]{0,1:T(8,128)(2,1)}, u32[]{:S(2)}) copy-start(bf16[5120,80]{0,1:T(8,128)(2,1)} %param.11) | copy-start | bytes 2457604
  19.5 29.0 %collective-permute-start = (bf16[128,1280]{1,0:T(8,128)(2,1)S(1)}, bf16[128,1280]{1,0:T(8,128)(2,1)}, u32[]{:S(2)}, u32[]{:S(2)}) collective-permute-start(bf16[128,1280]{1,0:T(8,128)(2,1)S(1)} %bitcast.82), channel_id=1, source_target_pairs={{0,2},{2,4},{4,6},{6,8},{8,10},{10,12},{12,14},{14,0},{1,3},{3,5},... | collective-permute-start | bytes 983048 | tf_op jit(solution)/shard_map/ppermute | solution.py:18
  21.2 29.2 %collective-permute-start.1 = (bf16[128,1280]{1,0:T(8,128)(2,1)S(1)}, bf16[128,1280]{1,0:T(8,128)(2,1)}, u32[]{:S(2)}, u32[]{:S(2)}) collective-permute-start(bf16[128,1280]{1,0:T(8,128)(2,1)S(1)} %bitcast.83), channel_id=1, source_target_pairs={{0,14},{2,0},{4,2},{6,4},{8,6},{10,8},{12,10},{14,12},{1,15},{3,1}... | collective-permute-start | bytes 983048 | tf_op jit(solution)/shard_map/ppermute | solution.py:18
  48.5 17.3 %collective-permute-start.2 = (bf16[128,1280]{1,0:T(8,128)(2,1)}, bf16[128,1280]{1,0:T(8,128)(2,1)}, u32[]{:S(2)}, u32[]{:S(2)}) collective-permute-start(bf16[128,1280]{1,0:T(8,128)(2,1)} %collective-permute-done), channel_id=1, source_target_pairs={{0,2},{2,4},{4,6},{6,8},{8,10},{10,12},{12,14},{14,0},{1,3},{3,5},... | collective-permute-start | bytes 983048 | tf_op jit(solution)/shard_map/ppermute | solution.py:18
  50.4 13.9 %collective-permute-start.3 = (bf16[128,1280]{1,0:T(8,128)(2,1)}, bf16[128,1280]{1,0:T(8,128)(2,1)S(1)}, u32[]{:S(2)}, u32[]{:S(2)}) collective-permute-start(bf16[128,1280]{1,0:T(8,128)(2,1)} %collective-permute-done.1), channel_id=1, source_target_pairs={{0,14},{2,0},{4,2},{6,4},{8,6},{10,8},{12,10},{14,12},{1,15},{3,1}... | collective-permute-start | bytes 983048 | tf_op jit(solution)/shard_map/ppermute | solution.py:18
  54.6 25.4 %collective-permute-start.4 = (bf16[2,320,1280]{2,1,0:T(8,128)(2,1)S(1)}, bf16[2,320,1280]{2,1,0:T(8,128)(2,1)S(1)}, u32[]{:S(2)}, u32[]{:S(2)}) collective-permute-start(bf16[2,320,1280]{2,1,0:T(8,128)(2,1)S(1)} %all-to-all-done.1), channel_id=1, source_target_pairs={{0,1},{1,0},{2,3},{3,2},{4,5},{5,4},{6,7},{7,6},{8,9},{9,8},{10,11... | collective-permute-start | bytes 4915208 | tf_op jit(solution)/shard_map/ppermute | solution.py:18
  64.3 1.7 copy-start.5
  64.3 7.8 %collective-permute-start.6 = (bf16[128,1280]{1,0:T(8,128)(2,1)S(1)}, bf16[128,1280]{1,0:T(8,128)(2,1)S(1)}, u32[]{:S(2)}, u32[]{:S(2)}) collective-permute-start(bf16[128,1280]{1,0:T(8,128)(2,1)S(1)} %collective-permute-done.3), channel_id=1, source_target_pairs={{0,14},{2,0},{4,2},{6,4},{8,6},{10,8},{12,10},{14,12},{1,15},{3,1}... | collective-permute-start | bytes 983048 | tf_op jit(solution)/shard_map/ppermute | solution.py:18
  65.7 8.5 %collective-permute-start.5 = (bf16[128,1280]{1,0:T(8,128)(2,1)}, bf16[128,1280]{1,0:T(8,128)(2,1)S(1)}, u32[]{:S(2)}, u32[]{:S(2)}) collective-permute-start(bf16[128,1280]{1,0:T(8,128)(2,1)} %collective-permute-done.2), channel_id=1, source_target_pairs={{0,2},{2,4},{4,6},{6,8},{8,10},{10,12},{12,14},{14,0},{1,3},{3,5},... | collective-permute-start | bytes 983048 | tf_op jit(solution)/shard_map/ppermute | solution.py:18
  66.0 16.9 %collective-permute-start.11 = (bf16[2,80,5120]{2,1,0:T(8,128)(2,1)S(1)}, bf16[2,80,5120]{2,1,0:T(8,128)(2,1)S(1)}, u32[]{:S(2)}, u32[]{:S(2)}) collective-permute-start(bf16[2,80,5120]{2,1,0:T(8,128)(2,1)S(1)} %pad_maximum_fusion.3), channel_id=1, source_target_pairs={{0,1},{1,0},{2,3},{3,2},{4,5},{5,4},{6,7},{7,6},{8,9},{9,8},{10,11... | collective-permute-start | bytes 4915208 | tf_op jit(solution)/shard_map/ppermute | solution.py:18
  72.1 4.5 %collective-permute-start.8 = (bf16[64,1280]{1,0:T(8,128)(2,1)S(1)}, bf16[64,1280]{1,0:T(8,128)(2,1)S(1)}, u32[]{:S(2)}, u32[]{:S(2)}) collective-permute-start(bf16[64,1280]{1,0:T(8,128)(2,1)S(1)} %slice.31), channel_id=1, source_target_pairs={{0,14},{2,0},{4,2},{6,4},{8,6},{10,8},{12,10},{14,12},{1,15},{3,1}... | collective-permute-start | bytes 491528 | tf_op jit(solution)/shard_map/ppermute | solution.py:18
  74.3 5.6 %collective-permute-start.7 = (bf16[64,1280]{1,0:T(8,128)(2,1)S(1)}, bf16[64,1280]{1,0:T(8,128)(2,1)S(1)}, u32[]{:S(2)}, u32[]{:S(2)}) collective-permute-start(bf16[64,1280]{1,0:T(8,128)(2,1)S(1)} %slice.30), channel_id=1, source_target_pairs={{0,2},{2,4},{4,6},{6,8},{8,10},{10,12},{12,14},{14,0},{1,3},{3,5},... | collective-permute-start | bytes 491528 | tf_op jit(solution)/shard_map/ppermute | solution.py:18
  80.3 1.2 copy-start.2
  80.3 1.7 copy-start
  85.4 13.5 %all-to-all-start.4 = ((bf16[4,80,64]{1,2,0:T(8,128)(2,1)}), bf16[4,80,64]{1,2,0:T(8,128)(2,1)S(1)}, u32[]{:S(2)}, u32[]{:S(2)}) async-start(bf16[4,80,64]{1,2,0:T(8,128)(2,1)} %copy.19), calls=%async_computation.4 | async-start | bytes 131072 | tf_op jit(solution)/shard_map/all_to_all | solution.py:50
  94.1 37.6 %copy-start.6 = (bf16[128,1280]{1,0:T(8,128)(2,1)S(1)}, bf16[128,1280]{1,0:T(8,128)(2,1)}, u32[]{:S(2)}) copy-start(bf16[128,1280]{1,0:T(8,128)(2,1)} %copy-done.5) | copy-start | bytes 983044
  95.2 37.3 %copy-start.3 = (bf16[1,2,320,1280]{3,2,1,0:T(8,128)(2,1)S(1)}, bf16[1,2,320,1280]{3,2,1,0:T(8,128)(2,1)}, u32[]{:S(2)}) copy-start(bf16[1,2,320,1280]{3,2,1,0:T(8,128)(2,1)} %copy-done.2) | copy-start | bytes 4915204
  98.9 47.4 %all-to-all-start.3 = ((bf16[16,48,640]{2,1,0:T(8,128)(2,1)}), bf16[16,48,640]{2,1,0:T(8,128)(2,1)S(1)}, u32[]{:S(2)}, u32[]{:S(2)}) async-start(bf16[16,48,640]{2,1,0:T(8,128)(2,1)} %bitcast.24), calls=%async_computation.3 | async-start | bytes 1966080 | tf_op jit(solution)/shard_map/all_to_all | solution.py:82
  132.5 3.0 %copy-start.1 = (bf16[1,2,320,1280]{3,2,1,0:T(8,128)(2,1)S(1)}, bf16[1,2,320,1280]{3,2,1,0:T(8,128)(2,1)}, u32[]{:S(2)}) copy-start(bf16[1,2,320,1280]{3,2,1,0:T(8,128)(2,1)} %copy-done) | copy-start | bytes 4915204
  146.3 24.6 %all-to-all-start.2 = ((bf16[16,80,640]{2,1,0:T(8,128)(2,1)}), bf16[16,80,640]{2,1,0:T(8,128)(2,1)S(1)}, u32[]{:S(2)}, u32[]{:S(2)}) async-start(bf16[16,80,640]{2,1,0:T(8,128)(2,1)} %bitcast.17), calls=%async_computation.2 | async-start | bytes 3276800 | tf_op jit(solution)/shard_map/all_to_all | solution.py:82
  172.1 44.8 %all-to-all-start.5 = ((bf16[32,80,256]{2,1,0:T(8,128)(2,1)}), bf16[32,80,256]{2,1,0:T(8,128)(2,1)}, u32[]{:S(2)}, u32[]{:S(2)}) async-start(bf16[32,80,256]{2,1,0:T(8,128)(2,1)} %broadcast_in_dim.32), calls=%async_computation.5 | async-start | bytes 2621440 | tf_op jit(solution)/shard_map/all_to_all | solution.py:55
  182.7 0.9 copy-start.8
  182.7 0.9 copy-start.9
  182.7 0.9 copy-start.10
  182.7 0.9 copy-start.11
  183.2 1.4 collective-permute-start.9
  220.5 3.9 %copy-start.12 = (s32[8]{0:T(128)S(1)}, s32[8]{0:T(128)}, u32[]{:S(2)}) copy-start(s32[8]{0:T(128)} %param.13) | copy-start | bytes 100
  220.5 25.1 %all-to-all-start.6 = ((bf16[8,40,2560]{2,1,0:T(8,128)(2,1)}), bf16[8,40,2560]{2,1,0:T(8,128)(2,1)S(1)}, u32[]{:S(2)}, u32[]{:S(2)}) async-start(bf16[8,40,2560]{2,1,0:T(8,128)(2,1)} %bitcast.39), calls=%async_computation.6 | async-start | bytes 3276800 | tf_op jit(solution)/shard_map/all_to_all | solution.py:108

commit v2 on v1

v2 whole, which is shorter than its diff:
```python
import jax
import jax.numpy as jnp
import numpy as np
from jax import lax
from jax.sharding import Mesh, PartitionSpec as P

SEQ_GRP = 1
TENANTS = 2
AXES = ("xl", "y", "xh", "z", "core")
SIZES = (2, 4, 2, 8, 2)
GRP = ("xl", "y")
PLANE = ("xl", "y", "xh")
BF16, F32 = jnp.bfloat16, jnp.float32
SLOTS = (0, 7, 1, 6, 2, 5, 3, 4)


def shift(x, axis, step):
    count = SIZES[AXES.index(axis)]
    return lax.ppermute(x, axis, [(i, (i + step) % count) for i in range(count)])


def after(x, *earlier):
    return lax.optimization_barrier((x,) + earlier)[0]


def ordered(x, other, axis):
    first = lax.axis_index(axis) == 0
    return jnp.stack([jnp.where(first, x, other), jnp.where(first, other, x)])


def rows_dot(a, b):
    return lax.dot_general(
        a, b, (((1,), (1,)), ((), ())), preferred_element_type=F32
    ).astype(BF16)


def shards(acts, grads, basis_in, basis_out, tenant):
    tokens, hidden = grads.shape
    model = acts.shape[1]
    own_in, own_out = basis_in.shape[1], basis_out.shape[1]
    groups, planes = 8, 16
    rows = hidden // planes
    xh, z = lax.axis_index("xh"), lax.axis_index("z")

    acts_x = shift(acts, "xh", 1)
    sent = grads.reshape(tokens, planes, rows).transpose(1, 0, 2)
    panel = lax.all_to_all(sent, PLANE, 0, 0).reshape(planes * tokens, rows)

    out_cols = basis_out.T
    keep = lax.dynamic_slice_in_dim(out_cols, xh * rows, rows, axis=1)
    give = lax.dynamic_slice_in_dim(out_cols, (1 - xh) * rows, rows, axis=1)

    pair = ordered(acts, acts_x, "xh").reshape(2 * tokens, model)
    give = after(give, panel)
    panel = after(panel, pair)
    every = lax.all_gather(pair, "z", axis=0, tiled=True)
    in_cols = basis_in.T
    in_other = shift(in_cols, "core", 1)

    keep_c = shift(keep, "core", 1)
    got = shift(give, "xh", 1)

    def partial(parts):
        left = jnp.stack([p.reshape(groups, 2 * tokens, rows) for p in parts], axis=1)
        left = left.reshape(groups * len(parts) * 2 * tokens, rows)
        out = jnp.stack([rows_dot(left, weights[h]) for h in range(2)])
        return out.reshape(planes, len(parts) * 2 * tokens, 2 * own_out)

    def home(out):
        back = lax.all_to_all(out, ("xh", "xl", "y"), 0, 0)
        return jnp.sum(back.astype(F32), axis=0).astype(BF16)

    up, down = [panel], [panel]
    for _ in range(2):
        up.append(shift(up[-1], "z", 1))
        down.append(shift(down[-1], "z", -1))
    got = after(got, up[1], down[1])
    got_c = shift(got, "core", 1)
    weights = ordered(
        jnp.concatenate([keep, keep_c]), jnp.concatenate([got, got_c]), "xh"
    )
    out_first = partial([panel, up[1], down[1], up[2], down[2]])
    up.append(shift(after(up[2], out_first), "z", 1))
    down.append(shift(after(down[2], out_first), "z", -1))
    half = panel.shape[0] // 2
    last = jnp.concatenate(
        [shift(up[3][:half], "z", 1), shift(down[3][half:], "z", -1)], axis=0
    )
    first = home(out_first)

    r = rows_dot(jnp.concatenate([in_cols, in_other]), every)
    r = r.reshape(2, own_in, 16 * tokens)
    r = jnp.where(lax.axis_index("core") == 0, r, r[::-1])
    r = r.reshape(2 * own_in, 16 * tokens)
    far = shift(r, "z", 4)
    duo = jnp.stack([r, far])
    below, above, two = shift(duo, "z", 1), shift(duo, "z", -1), shift(duo, "z", 2)
    ring = [r, above[0], two[1], below[1], far, above[1], two[0], below[0]]
    r = lax.dynamic_slice_in_dim(jnp.stack(ring + ring[:7]), (8 - z) % 8, 8, axis=0)
    r = r.reshape(16 * own_in, 16 * tokens)
    slot, half_x, row = np.unravel_index(np.arange(16 * tokens), (8, 2, tokens))
    z_of = (z + np.array(SLOTS)[slot]) % 8
    source = (z_of * 2 + half_x) * tokens + row
    pick = (jnp.arange(16 * tokens)[:, None] == source[None, :]).astype(BF16)
    r = jnp.dot(r, pick, preferred_element_type=F32).astype(BF16)
    r = ordered(r, shift(r, "xh", 1), "xh").reshape(32 * own_in, 16 * tokens)
    rotated_in = jnp.concatenate([r, shift(r, "core", 1)], axis=1)

    second = home(after(partial([up[3], down[3], last]), first))
    mixed = jnp.concatenate([first, second], axis=0)
    other = shift(mixed[:, own_out:], "core", 1)
    left = jnp.concatenate([mixed[:, :own_out], other], axis=0)

    corr = lax.dot_general(
        left, rotated_in, (((0,), (1,)), ((), ())), preferred_element_type=F32
    )
    square = (corr * corr).astype(BF16)
    parts = lax.all_to_all(
        square.reshape(groups, own_out // groups, square.shape[1]), GRP, 0, 0
    ).astype(F32)
    sums = jnp.stack(
        [
            jnp.sum(jnp.where((tenant == k)[:, None, None], parts, 0.0), axis=0)
            for k in range(TENANTS)
        ]
    )
    total = jnp.sum(sums, axis=0)
    seq_count = SEQ_GRP * groups
    scale = 1.0 / float((seq_count - seq_count // TENANTS) * 32 * tokens)
    return (total[None] - sums) * scale


def solution(mesh):
    fine = Mesh(mesh.devices.reshape(SIZES), AXES)
    tile = ("xh", "z", "core")
    return jax.shard_map(
        shards,
        mesh=fine,
        in_specs=(
            P(AXES, None),
            P(AXES, None),
            P(None, tile),
            P(GRP, tile),
            P(),
        ),
        out_specs=P(None, tile + GRP, None),
        check_vma=False,
    )
```

time: 248 us -> 161 us (0.65)
  waiting for transfers between devices: 92.6 us -> 52.4 us
  starting transfers between devices: 97.7 us -> 69.4 us
  blocking collectives: 22.5 us -> 0 us
  between operations: 0.35 us -> 13.8 us
  local copies, waits for them, and re-layouts: 14.6 us -> 4.31 us
    all_to_all x5 -> x2, waiting for transfers between devices: 63 us -> 4.99 us  [home(): back = lax.all_to_all(out, ('xh', 'xl', 'y'), 0, 0)]
    all_to_all x5 -> x2, starting transfers between devices: 59.9 us -> 8.65 us  [home(): back = lax.all_to_all(out, ('xh', 'xl', 'y'), 0, 0)]
    ppermute x12 -> x20, starting transfers between devices: 26.3 us -> 49.4 us  [shift(): lax.ppermute(x, axis, [(i, (i + step) % count) for i in range(count)])]
    all_gather x1 -> x0, blocking collectives: 22.5 us -> none  [shards(): every = lax.all_gather(acts, 'z', axis=0, tiled=True)]
    ppermute x12 -> x20, waiting for transfers between devices: 8.45 us -> 26.2 us  [shift(): lax.ppermute(x, axis, [(i, (i + step) % count) for i in range(count)])]
    unnamed x30 -> x33, local copies, waits for them, and re-layouts: 6.73 us -> 0.33 us
    reshape x3 -> x0, local copies, waits for them, and re-layouts: 4.51 us -> none  [the longest x1 3.78 us: shards(): halves = basis_out.T.reshape(own_out, 2, rows).transpose(1, 0, 2)]
    dot_general x6 -> x7, matrix products: 12.6 us -> 14.9 us  [the longest x5 12.6 us: rows_dot(): lax.dot_general(a, b, (((1,), (1,)), ((), ())), preferred_element_type=F32)]
  transfers between devices with their start and end apart: 19 -> 25, of which waited for: 9 -> 10; matrix products, arithmetic and copies ran while one was open for 10% -> 13% of each run, Pallas kernels for 0% -> 0%
where the time goes in v2:
time: 161 us; the launch traced here: 160 us
  starting transfers between devices  69.4 us (43%)
  waiting for transfers between devices  52.4 us (33%)
  matrix products  14.9 us (9%)
  between operations  13.8 us (9%)
  other arithmetic  5.54 us (3%)
  local copies, waits for them, and re-layouts  4.31 us (3%)
    ppermute x20, starting transfers between devices, shift(): lax.ppermute(x, axis, [(i, (i + step) % count) for i in range(count)])  49.4 us
    ppermute x20, waiting for transfers between devices, shift(): lax.ppermute(x, axis, [(i, (i + step) % count) for i in range(count)])  26.2 us
    all_to_all x1, waiting for transfers between devices, shards(): lax.all_to_all(square.reshape(groups, own_out // groups, square.shape[1])...  21.2 us
    dot_general x5, matrix products, rows_dot(): lax.dot_general(a, b, (((1,), (1,)), ((), ())), preferred_element_type=F32)  12.6 us
    all_to_all x2, starting transfers between devices, home(): back = lax.all_to_all(out, ('xh', 'xl', 'y'), 0, 0)  8.65 us
    all_to_all x1, starting transfers between devices, shards(): panel = lax.all_to_all(sent, PLANE, 0, 0).reshape(planes * tokens, rows)  7.58 us
    all_to_all x2, waiting for transfers between devices, home(): back = lax.all_to_all(out, ('xh', 'xl', 'y'), 0, 0)  4.99 us
    all_to_all x1, starting transfers between devices, shards(): lax.all_to_all(square.reshape(groups, own_out // groups, square.shape[1])...  3.71 us
  transfers between devices with their start and end apart: 25, of which 10 were waited for; matrix products, arithmetic and copies ran while one was open for 13% of the time, Pallas kernels for 0%

profile of v2, /device:TPU:1, one launch (start us, length us, event | category | flops | bytes accessed | tf_op | source)
XLA Modules:
  0.0 160.4 jit_solution(17238318642016427964)
XLA Ops:
  6.5 7.6 %all-to-all-start = ((bf16[16,8,1280]{2,1,0:T(8,128)(2,1)}), bf16[16,8,1280]{2,1,0:T(8,128)(2,1)S(1)}, u32[]{:S(2)}, u32[]{:S(2)}) async-start(bf16[16,8,1280]{2,1,0:T(8,128)(2,1)} %bitcast.78), calls=%async_computation | async-start | bytes 655360 | tf_op jit(solution)/shard_map/all_to_all | solution.py:47
  14.1 0.0 all-gather.2.cloned.1.call-start
  14.2 3.0 %collective-permute-start = (bf16[8,5120]{1,0:T(8,128)(2,1)}, bf16[8,5120]{1,0:T(8,128)(2,1)S(1)}, u32[]{:S(2)}, u32[]{:S(2)}) collective-permute-start(bf16[8,5120]{1,0:T(8,128)(2,1)} %param.8), channel_id=1, source_target_pairs={{0,16},{16,0},{1,17},{17,1},{2,18},{18,2},{3,19},{19,3},{4,20},{20... | collective-permute-start | bytes 245768 | tf_op jit(solution)/shard_map/ppermute | solution.py:19
  17.1 1.5 dynamic-slice_bitcast_fusion.1
  18.7 3.6 %collective-permute-done = bf16[8,5120]{1,0:T(8,128)(2,1)S(1)} collective-permute-done((bf16[8,5120]{1,0:T(8,128)(2,1)}, bf16[8,5120]{1,0:T(8,128)(2,1)S(1)}, u32[]{:S(2)}, u32[]{:S(2)}) %collective-permute-start) | collective-permute-done | bytes 81952 | tf_op jit(solution)/shard_map/ppermute | solution.py:19
  22.3 0.0 all-to-all-done
  22.3 1.2 collective-permute-start.6
  23.5 0.7 maximum_bitcast_fusion
  24.2 1.6 %collective-permute-start.1 = (bf16[128,1280]{1,0:T(8,128)(2,1)S(1)}, bf16[128,1280]{1,0:T(8,128)(2,1)S(1)}, u32[]{:S(2)}, u32[]{:S(2)}) collective-permute-start(bf16[128,1280]{1,0:T(8,128)(2,1)S(1)} %bitcast.62), channel_id=1, source_target_pairs={{0,2},{2,4},{4,6},{6,8},{8,10},{10,12},{12,14},{14,0},{1,3},{3,5},... | collective-permute-start | bytes 983048 | tf_op jit(solution)/shard_map/ppermute | solution.py:19
  25.8 3.3 %collective-permute-start.5 = (bf16[320,1280]{1,0:T(8,128)(2,1)S(1)}, bf16[320,1280]{1,0:T(8,128)(2,1)}, u32[]{:S(2)}, u32[]{:S(2)}) collective-permute-start(bf16[320,1280]{1,0:T(8,128)(2,1)S(1)} %get-tuple-element.19), channel_id=1, source_target_pairs={{0,1},{1,0},{2,3},{3,2},{4,5},{5,4},{6,7},{7,6},{8,9},{9,8},{10,11... | collective-permute-start | bytes 2457608 | tf_op jit(solution)/shard_map/ppermute | solution.py:19
  29.1 0.0 collective-permute-start.13
  29.1 0.0 all-gather.2.cloned.1.call-update
  29.1 3.7 %collective-permute-start.2 = (bf16[128,1280]{1,0:T(8,128)(2,1)S(1)}, bf16[128,1280]{1,0:T(8,128)(2,1)S(1)}, u32[]{:S(2)}, u32[]{:S(2)}) collective-permute-start(bf16[128,1280]{1,0:T(8,128)(2,1)S(1)} %bitcast.63), channel_id=1, source_target_pairs={{0,14},{2,0},{4,2},{6,4},{8,6},{10,8},{12,10},{14,12},{1,15},{3,1}... | collective-permute-start | bytes 983048 | tf_op jit(solution)/shard_map/ppermute | solution.py:19
  32.9 1.8 %collective-permute-done.1 = bf16[128,1280]{1,0:T(8,128)(2,1)S(1)} collective-permute-done((bf16[128,1280]{1,0:T(8,128)(2,1)S(1)}, bf16[128,1280]{1,0:T(8,128)(2,1)S(1)}, u32[]{:S(2)}, u32[]{:S(2)}) %collective-permute-start.1) | collective-permute-done | bytes 327712 | tf_op jit(solution)/shard_map/ppermute | solution.py:19
  34.7 0.0 collective-permute-start.3
  34.8 4.7 %collective-permute-done.2 = bf16[128,1280]{1,0:T(8,128)(2,1)S(1)} collective-permute-done((bf16[128,1280]{1,0:T(8,128)(2,1)S(1)}, bf16[128,1280]{1,0:T(8,128)(2,1)S(1)}, u32[]{:S(2)}, u32[]{:S(2)}) %collective-permute-start.2) | collective-permute-done | bytes 327712 | tf_op jit(solution)/shard_map/ppermute | solution.py:19
  39.4 3.4 %collective-permute-start.4 = (bf16[128,1280]{1,0:T(8,128)(2,1)S(1)}, bf16[128,1280]{1,0:T(8,128)(2,1)}, u32[]{:S(2)}, u32[]{:S(2)}) collective-permute-start(bf16[128,1280]{1,0:T(8,128)(2,1)S(1)} %collective-permute-done.2), channel_id=1, source_target_pairs={{0,14},{2,0},{4,2},{6,4},{8,6},{10,8},{12,10},{14,12},{1,15},{3,1}... | collective-permute-start | bytes 983048 | tf_op jit(solution)/shard_map/ppermute | solution.py:19
  42.9 1.7 %collective-permute-start.7 = (bf16[320,1280]{1,0:T(8,128)(2,1)S(1)}, bf16[320,1280]{1,0:T(8,128)(2,1)S(1)}, u32[]{:S(2)}, u32[]{:S(2)}) collective-permute-start(bf16[320,1280]{1,0:T(8,128)(2,1)S(1)} %collective-permute-done.6), channel_id=1, source_target_pairs={{0,1},{1,0},{2,3},{3,2},{4,5},{5,4},{6,7},{7,6},{8,9},{9,8},{10,11... | collective-permute-start | bytes 2457608 | tf_op jit(solution)/shard_map/ppermute | solution.py:19
  44.5 0.0 collective-permute-done.3
  44.6 8.9 %collective-permute-done.4 = bf16[128,1280]{1,0:T(8,128)(2,1)} collective-permute-done((bf16[128,1280]{1,0:T(8,128)(2,1)S(1)}, bf16[128,1280]{1,0:T(8,128)(2,1)}, u32[]{:S(2)}, u32[]{:S(2)}) %collective-permute-start.4) | collective-permute-done | bytes 327712 | tf_op jit(solution)/shard_map/ppermute | solution.py:19
  53.5 1.0 constant_dynamic-update-slice_fusion
  54.5 0.1 constant_dynamic-update-slice_fusion.6
  54.6 0.1 constant_dynamic-update-slice_fusion.5
  54.7 3.2 %fusion.10 = bf16[1,640,640]{2,1,0:T(8,128)(2,1)S(1)} fusion(bf16[640,1280]{1,0:T(8,128)(2,1)S(1)} %bitcast.82, bf16[640,1280]{1,0:T(8,128)(2,1)S(1)} %constant_dynamic-update-slice_fusion.5, pred[]{:T(512)S(6)} %eq.32, bf16[320,1280]{1,0:T(8,128)(2,1)} %collective-permute-done.5, bf16[320,1280]{1,0:T(8,128)(2,1)S(1)} %get-tuple-element.19), kind=kOutput, calls=%fused_computation.20 | convolution fusion | flops 1053081600 | bytes 5734401 | tf_op jit(solution)/shard_map/dot_general | solution.py:32
  57.9 2.7 %fusion.11 = bf16[1,640,640]{2,1,0:T(8,128)(2,1)S(1)} fusion(bf16[640,1280]{1,0:T(8,128)(2,1)S(1)} %bitcast.83, bf16[640,1280]{1,0:T(8,128)(2,1)S(1)} %constant_dynamic-update-slice_fusion.5, pred[]{:T(512)S(6)} %eq.32, bf16[320,1280]{1,0:T(8,128)(2,1)} %collective-permute-done.5, bf16[320,1280]{1,0:T(8,128)(2,1)S(1)} %get-tuple-element.19), kind=kOutput, calls=%fused_computation.21 | convolution fusion | flops 1053081600 | bytes 5734401 | tf_op jit(solution)/shard_map/dot_general | solution.py:32
  60.6 0.0 copy-start.3
  60.6 0.0 copy-start.4
  60.6 0.0 copy-start.5
  60.6 1.4 pad_maximum_fusion.1
  62.0 2.1 %collective-permute-start.8 = (bf16[128,1280]{1,0:T(8,128)(2,1)S(1)}, bf16[128,1280]{1,0:T(8,128)(2,1)S(1)}, u32[]{:S(2)}, u32[]{:S(2)}) collective-permute-start(bf16[128,1280]{1,0:T(8,128)(2,1)S(1)} %collective-permute-done.3), channel_id=1, source_target_pairs={{0,2},{2,4},{4,6},{6,8},{8,10},{10,12},{12,14},{14,0},{1,3},{3,5},... | collective-permute-start | bytes 983048 | tf_op jit(solution)/shard_map/ppermute | solution.py:19
  64.1 0.5 collective-permute-start.9
  64.7 4.1 %all-to-all-start.1 = ((bf16[16,80,640]{2,1,0:T(8,128)(2,1)}), bf16[16,80,640]{2,1,0:T(8,128)(2,1)S(1)}, u32[]{:S(2)}, u32[]{:S(2)}) async-start(bf16[16,80,640]{2,1,0:T(8,128)(2,1)} %bitcast.16), calls=%async_computation.1 | async-start | bytes 3276800 | tf_op jit(solution)/shard_map/all_to_all | solution.py:70
  68.8 3.4 %collective-permute-done.8 = bf16[128,1280]{1,0:T(8,128)(2,1)S(1)} collective-permute-done((bf16[128,1280]{1,0:T(8,128)(2,1)S(1)}, bf16[128,1280]{1,0:T(8,128)(2,1)S(1)}, u32[]{:S(2)}, u32[]{:S(2)}) %collective-permute-start.8) | collective-permute-done | bytes 327712 | tf_op jit(solution)/shard_map/ppermute | solution.py:19
  72.2 0.7 slice.40
  72.8 0.9 collective-permute-start.10
  73.7 0.7 slice.41
  74.4 1.8 %collective-permute-start.11 = (bf16[64,1280]{1,0:T(8,128)(2,1)}, bf16[64,1280]{1,0:T(8,128)(2,1)S(1)}, u32[]{:S(2)}, u32[]{:S(2)}) collective-permute-start(bf16[64,1280]{1,0:T(8,128)(2,1)} %slice.41), channel_id=1, source_target_pairs={{0,14},{2,0},{4,2},{6,4},{8,6},{10,8},{12,10},{14,12},{1,15},{3,1}... | collective-permute-start | bytes 491528 | tf_op jit(solution)/shard_map/ppermute | solution.py:19
  76.2 2.4 %fusion.14 = bf16[160,128]{1,0:T(8,128)(2,1)S(1)} fusion(bf16[128,5120]{1,0:T(8,128)(2,1)} %all-gather.2.cloned.1.call-done, bf16[80,5120]{1,0:T(8,128)(2,1)} %collective-permute-done.13, bf16[80,5120]{1,0:T(8,128)(2,1)} %bitcast.86), kind=kOutput, calls=%fused_computation.26 | convolution fusion | flops 213012480 | bytes 2990080 | tf_op jit(solution)/shard_map/dot_general | solution.py:32
  78.6 5.2 %collective-permute-start.14 = (bf16[160,128]{1,0:T(8,128)(2,1)S(1)}, bf16[160,128]{1,0:T(8,128)(2,1)S(1)}, u32[]{:S(2)}, u32[]{:S(2)}) collective-permute-start(bf16[160,128]{1,0:T(8,128)(2,1)S(1)} %bitcast.73), channel_id=1, source_target_pairs={{0,8},{2,10},{4,12},{6,14},{8,0},{10,2},{12,4},{14,6},{1,9},{3,11}... | collective-permute-start | bytes 122888 | tf_op jit(solution)/shard_map/ppermute | solution.py:19
  83.8 1.8 %collective-permute-done.14 = bf16[160,128]{1,0:T(8,128)(2,1)S(1)} collective-permute-done((bf16[160,128]{1,0:T(8,128)(2,1)S(1)}, bf16[160,128]{1,0:T(8,128)(2,1)S(1)}, u32[]{:S(2)}, u32[]{:S(2)}) %collective-permute-start.14) | collective-permute-done | bytes 40992 | tf_op jit(solution)/shard_map/ppermute | solution.py:19
  85.6 0.3 collective-permute-start.15
  85.9 2.3 %collective-permute-start.16 = (bf16[2,160,128]{2,1,0:T(8,128)(2,1)S(1)}, bf16[2,160,128]{2,1,0:T(8,128)(2,1)S(1)}, u32[]{:S(2)}, u32[]{:S(2)}) collective-permute-start(bf16[2,160,128]{2,1,0:T(8,128)(2,1)S(1)} %pad_maximum_fusion.7), channel_id=1, source_target_pairs={{0,4},{2,6},{4,8},{6,10},{8,12},{10,14},{12,0},{14,2},{1,5},{3,7},... | collective-permute-start | bytes 245768 | tf_op jit(solution)/shard_map/ppermute | solution.py:19
  88.2 1.4 collective-permute-start.17
  89.6 0.1 pad_maximum_fusion.2
  89.7 2.2 %fusion.12 = bf16[1,384,640]{2,1,0:T(8,128)(2,1)S(1)} fusion(bf16[384,1280]{1,0:T(8,128)(2,1)S(1)} %bitcast.67, bf16[640,1280]{1,0:T(8,128)(2,1)S(1)} %copy-done.1, pred[]{:T(512)S(6)} %eq.32, bf16[320,1280]{1,0:T(8,128)(2,1)} %collective-permute-done.5, bf16[320,1280]{1,0:T(8,128)(2,1)S(1)} %get-tuple-element.19), kind=kOutput, calls=%fused_computation.24 | convolution fusion | flops 633487360 | bytes 4751361 | tf_op jit(solution)/shard_map/dot_general | solution.py:32
  92.0 1.1 collective-permute-done.17
  93.3 0.2 convolution_convert_fusion
  93.5 2.8 %collective-permute-start.18 = (bf16[1280,128]{1,0:T(8,128)(2,1)S(1)}, bf16[1280,128]{1,0:T(8,128)(2,1)S(1)}, u32[]{:S(2)}, u32[]{:S(2)}) collective-permute-start(bf16[1280,128]{1,0:T(8,128)(2,1)S(1)} %convolution_convert_fusion), channel_id=1, source_target_pairs={{0,16},{16,0},{1,17},{17,1},{2,18},{18,2},{3,19},{19,3},{4,20},{20... | collective-permute-start | bytes 983048 | tf_op jit(solution)/shard_map/ppermute | solution.py:19
  96.4 2.2 %fusion.13 = bf16[1,384,640]{2,1,0:T(8,128)(2,1)S(1)} fusion(bf16[384,1280]{1,0:T(8,128)(2,1)S(1)} %bitcast.68, bf16[640,1280]{1,0:T(8,128)(2,1)S(1)} %copy-done.1, pred[]{:T(512)S(6)} %eq.32, bf16[320,1280]{1,0:T(8,128)(2,1)} %collective-permute-done.5, bf16[320,1280]{1,0:T(8,128)(2,1)S(1)} %get-tuple-element.19), kind=kOutput, calls=%fused_computation.25 | convolution fusion | flops 633487360 | bytes 4751361 | tf_op jit(solution)/shard_map/dot_general | solution.py:32
  98.5 1.1 pad_maximum_fusion.3
  99.6 0.2 reduce_sum.52
  99.8 4.6 %all-to-all-start.2 = ((bf16[16,48,640]{2,1,0:T(8,128)(2,1)}), bf16[16,48,640]{2,1,0:T(8,128)(2,1)S(1)}, u32[]{:S(2)}, u32[]{:S(2)}) async-start(bf16[16,48,640]{2,1,0:T(8,128)(2,1)} %bitcast.23), calls=%async_computation.2 | async-start | bytes 1966080 | tf_op jit(solution)/shard_map/all_to_all | solution.py:70
  104.5 0.1 pad_maximum_fusion.4
  104.6 6.7 %collective-permute-start.19 = (bf16[2560,128]{1,0:T(8,128)(2,1)S(1)}, bf16[2560,128]{1,0:T(8,128)(2,1)S(1)}, u32[]{:S(2)}, u32[]{:S(2)}) collective-permute-start(bf16[2560,128]{1,0:T(8,128)(2,1)S(1)} %bitcast.71), channel_id=1, source_target_pairs={{0,1},{1,0},{2,3},{3,2},{4,5},{5,4},{6,7},{7,6},{8,9},{9,8},{10,11... | collective-permute-start | bytes 1966088 | tf_op jit(solution)/shard_map/ppermute | solution.py:19
  111.3 5.0 %all-to-all-done.2 = bf16[16,48,640]{2,1,0:T(8,128)(2,1)S(1)} async-done(((bf16[16,48,640]{2,1,0:T(8,128)(2,1)}), bf16[16,48,640]{2,1,0:T(8,128)(2,1)S(1)}, u32[]{:S(2)}, u32[]{:S(2)}) %all-to-all-start.2) | async-done | bytes 983072 | tf_op jit(solution)/shard_map/all_to_all | solution.py:70
  116.3 0.1 reduce_sum.53
  116.4 0.1 fusion.21
  116.5 7.4 %collective-permute-start.12 = (bf16[128,320]{1,0:T(8,128)(2,1)S(1)}, bf16[128,320]{1,0:T(8,128)(2,1)S(1)}, u32[]{:S(2)}, u32[]{:S(2)}) collective-permute-start(bf16[128,320]{1,0:T(8,128)(2,1)S(1)} %get-tuple-element.24), channel_id=1, source_target_pairs={{0,1},{1,0},{2,3},{3,2},{4,5},{5,4},{6,7},{7,6},{8,9},{9,8},{10,11... | collective-permute-start | bytes 245768 | tf_op jit(solution)/shard_map/ppermute | solution.py:19
  124.0 0.9 collective-permute-done.12
  124.9 2.0 %fusion = bf16[320,2560]{1,0:T(8,128)(2,1)} fusion(bf16[2560,128]{1,0:T(8,128)(2,1)S(1)} %collective-permute-done.19, bf16[2560,128]{1,0:T(8,128)(2,1)S(1)} %bitcast.72, bf16[128,320]{1,0:T(8,128)(2,1)S(1)} %collective-permute-done.12, bf16[128,320]{1,0:T(8,128)(2,1)S(1)} %get-tuple-element.23), kind=kOutput, calls=%fused_computation.3 | convolution fusion | flops 424017920 | bytes 3112960 | tf_op jit(solution)/shard_map/dot_general | solution.py:114
  126.9 3.7 %all-to-all-start.3 = ((bf16[8,40,2560]{2,1,0:T(8,128)(2,1)}), bf16[8,40,2560]{2,1,0:T(8,128)(2,1)S(1)}, u32[]{:S(2)}, u32[]{:S(2)}) async-start(bf16[8,40,2560]{2,1,0:T(8,128)(2,1)} %bitcast.33), calls=%async_computation.3 | async-start | bytes 3276800 | tf_op jit(solution)/shard_map/all_to_all | solution.py:118
  130.7 21.2 %all-to-all-done.3 = bf16[8,40,2560]{2,1,0:T(8,128)(2,1)S(1)} async-done(((bf16[8,40,2560]{2,1,0:T(8,128)(2,1)}), bf16[8,40,2560]{2,1,0:T(8,128)(2,1)S(1)}, u32[]{:S(2)}, u32[]{:S(2)}) %all-to-all-start.3) | async-done | bytes 1638432 | tf_op jit(solution)/shard_map/all_to_all | solution.py:118
  151.9 0.6 fusion.1
  152.6 1.0 fusion.17
  (52 shorter events, 0.5 us)
Async XLA Ops:
  6.5 15.7 %all-to-all-start = ((bf16[16,8,1280]{2,1,0:T(8,128)(2,1)}), bf16[16,8,1280]{2,1,0:T(8,128)(2,1)S(1)}, u32[]{:S(2)}, u32[]{:S(2)}) async-start(bf16[16,8,1280]{2,1,0:T(8,128)(2,1)} %bitcast.78), calls=%async_computation | async-start | bytes 655360 | tf_op jit(solution)/shard_map/all_to_all | solution.py:47
  14.1 62.1 %all-gather.2.cloned.1.call-start = ((), (), s32[]{:S(2)}) async-start(), calls=%async_computation.4 | async-start | bytes 1474560 | tf_op jit(solution)/shard_map/all_gather | solution.py:56
  14.2 8.1 %collective-permute-start = (bf16[8,5120]{1,0:T(8,128)(2,1)}, bf16[8,5120]{1,0:T(8,128)(2,1)S(1)}, u32[]{:S(2)}, u32[]{:S(2)}) collective-permute-start(bf16[8,5120]{1,0:T(8,128)(2,1)} %param.8), channel_id=1, source_target_pairs={{0,16},{16,0},{1,17},{17,1},{2,18},{18,2},{3,19},{19,3},{4,20},{20... | collective-permute-start | bytes 245768 | tf_op jit(solution)/shard_map/ppermute | solution.py:19
  17.1 5.1 %copy-start.2 = (bf16[8,5120]{1,0:T(8,128)(2,1)S(1)}, bf16[8,5120]{1,0:T(8,128)(2,1)}, u32[]{:S(2)}) copy-start(bf16[8,5120]{1,0:T(8,128)(2,1)} %param.8) | copy-start | bytes 245764
  22.3 20.6 %collective-permute-start.6 = (bf16[320,1280]{1,0:T(8,128)(2,1)S(1)}, bf16[320,1280]{1,0:T(8,128)(2,1)S(1)}, u32[]{:S(2)}, u32[]{:S(2)}) collective-permute-start(bf16[320,1280]{1,0:T(8,128)(2,1)S(1)} %get-tuple-element.12), channel_id=1, source_target_pairs={{0,16},{16,0},{1,17},{17,1},{2,18},{18,2},{3,19},{19,3},{4,20},{20... | collective-permute-start | bytes 2457608 | tf_op jit(solution)/shard_map/ppermute | solution.py:19
  24.2 10.6 %collective-permute-start.1 = (bf16[128,1280]{1,0:T(8,128)(2,1)S(1)}, bf16[128,1280]{1,0:T(8,128)(2,1)S(1)}, u32[]{:S(2)}, u32[]{:S(2)}) collective-permute-start(bf16[128,1280]{1,0:T(8,128)(2,1)S(1)} %bitcast.62), channel_id=1, source_target_pairs={{0,2},{2,4},{4,6},{6,8},{8,10},{10,12},{12,14},{14,0},{1,3},{3,5},... | collective-permute-start | bytes 983048 | tf_op jit(solution)/shard_map/ppermute | solution.py:19
  25.8 28.9 %collective-permute-start.5 = (bf16[320,1280]{1,0:T(8,128)(2,1)S(1)}, bf16[320,1280]{1,0:T(8,128)(2,1)}, u32[]{:S(2)}, u32[]{:S(2)}) collective-permute-start(bf16[320,1280]{1,0:T(8,128)(2,1)S(1)} %get-tuple-element.19), channel_id=1, source_target_pairs={{0,1},{1,0},{2,3},{3,2},{4,5},{5,4},{6,7},{7,6},{8,9},{9,8},{10,11... | collective-permute-start | bytes 2457608 | tf_op jit(solution)/shard_map/ppermute | solution.py:19
  29.1 47.1 %collective-permute-start.13 = (bf16[80,5120]{1,0:T(8,128)(2,1)}, bf16[80,5120]{1,0:T(8,128)(2,1)}, u32[]{:S(2)}, u32[]{:S(2)}) collective-permute-start(bf16[80,5120]{1,0:T(8,128)(2,1)} %bitcast.85), channel_id=1, source_target_pairs={{0,1},{1,0},{2,3},{3,2},{4,5},{5,4},{6,7},{7,6},{8,9},{9,8},{10,11... | collective-permute-start | bytes 2457608 | tf_op jit(solution)/shard_map/ppermute | solution.py:19
  29.1 10.3 %collective-permute-start.2 = (bf16[128,1280]{1,0:T(8,128)(2,1)S(1)}, bf16[128,1280]{1,0:T(8,128)(2,1)S(1)}, u32[]{:S(2)}, u32[]{:S(2)}) collective-permute-start(bf16[128,1280]{1,0:T(8,128)(2,1)S(1)} %bitcast.63), channel_id=1, source_target_pairs={{0,14},{2,0},{4,2},{6,4},{8,6},{10,8},{12,10},{14,12},{1,15},{3,1}... | collective-permute-start | bytes 983048 | tf_op jit(solution)/shard_map/ppermute | solution.py:19
  34.7 9.8 %collective-permute-start.3 = (bf16[128,1280]{1,0:T(8,128)(2,1)S(1)}, bf16[128,1280]{1,0:T(8,128)(2,1)S(1)}, u32[]{:S(2)}, u32[]{:S(2)}) collective-permute-start(bf16[128,1280]{1,0:T(8,128)(2,1)S(1)} %collective-permute-done.1), channel_id=1, source_target_pairs={{0,2},{2,4},{4,6},{6,8},{8,10},{10,12},{12,14},{14,0},{1,3},{3,5},... | collective-permute-start | bytes 983048 | tf_op jit(solution)/shard_map/ppermute | solution.py:19
  39.4 14.1 %collective-permute-start.4 = (bf16[128,1280]{1,0:T(8,128)(2,1)S(1)}, bf16[128,1280]{1,0:T(8,128)(2,1)}, u32[]{:S(2)}, u32[]{:S(2)}) collective-permute-start(bf16[128,1280]{1,0:T(8,128)(2,1)S(1)} %collective-permute-done.2), channel_id=1, source_target_pairs={{0,14},{2,0},{4,2},{6,4},{8,6},{10,8},{12,10},{14,12},{1,15},{3,1}... | collective-permute-start | bytes 983048 | tf_op jit(solution)/shard_map/ppermute | solution.py:19
  42.9 11.7 %collective-permute-start.7 = (bf16[320,1280]{1,0:T(8,128)(2,1)S(1)}, bf16[320,1280]{1,0:T(8,128)(2,1)S(1)}, u32[]{:S(2)}, u32[]{:S(2)}) collective-permute-start(bf16[320,1280]{1,0:T(8,128)(2,1)S(1)} %collective-permute-done.6), channel_id=1, source_target_pairs={{0,1},{1,0},{2,3},{3,2},{4,5},{5,4},{6,7},{7,6},{8,9},{9,8},{10,11... | collective-permute-start | bytes 2457608 | tf_op jit(solution)/shard_map/ppermute | solution.py:19
  54.7 3.3 %copy-start = (bf16[640,1280]{1,0:T(8,128)(2,1)}, bf16[640,1280]{1,0:T(8,128)(2,1)S(1)}, u32[]{:S(2)}) copy-start(bf16[640,1280]{1,0:T(8,128)(2,1)S(1)} %constant_dynamic-update-slice_fusion.5) | copy-start | bytes 4915204
  60.6 4.1 %copy-start.3 = (s32[128]{0:T(128)S(1)}, s32[128]{0:T(128)}, u32[]{:S(2)}) copy-start(s32[128]{0:T(128)} %constant.60.clone) | copy-start | bytes 1540
  60.6 4.1 %copy-start.4 = (s32[128]{0:T(128)S(1)}, s32[128]{0:T(128)}, u32[]{:S(2)}) copy-start(s32[128]{0:T(128)} %constant.61.clone) | copy-start | bytes 1540
  60.6 4.1 %copy-start.5 = (s32[128]{0:T(128)S(1)}, s32[128]{0:T(128)}, u32[]{:S(2)}) copy-start(s32[128]{0:T(128)} %constant.62.clone) | copy-start | bytes 1540
  62.0 10.1 %collective-permute-start.8 = (bf16[128,1280]{1,0:T(8,128)(2,1)S(1)}, bf16[128,1280]{1,0:T(8,128)(2,1)S(1)}, u32[]{:S(2)}, u32[]{:S(2)}) collective-permute-start(bf16[128,1280]{1,0:T(8,128)(2,1)S(1)} %collective-permute-done.3), channel_id=1, source_target_pairs={{0,2},{2,4},{4,6},{6,8},{8,10},{10,12},{12,14},{14,0},{1,3},{3,5},... | collective-permute-start | bytes 983048 | tf_op jit(solution)/shard_map/ppermute | solution.py:19
  64.1 9.6 %collective-permute-start.9 = (bf16[128,1280]{1,0:T(8,128)(2,1)}, bf16[128,1280]{1,0:T(8,128)(2,1)S(1)}, u32[]{:S(2)}, u32[]{:S(2)}) collective-permute-start(bf16[128,1280]{1,0:T(8,128)(2,1)} %collective-permute-done.4), channel_id=1, source_target_pairs={{0,14},{2,0},{4,2},{6,4},{8,6},{10,8},{12,10},{14,12},{1,15},{3,1}... | collective-permute-start | bytes 983048 | tf_op jit(solution)/shard_map/ppermute | solution.py:19
  64.7 34.9 %all-to-all-start.1 = ((bf16[16,80,640]{2,1,0:T(8,128)(2,1)}), bf16[16,80,640]{2,1,0:T(8,128)(2,1)S(1)}, u32[]{:S(2)}, u32[]{:S(2)}) async-start(bf16[16,80,640]{2,1,0:T(8,128)(2,1)} %bitcast.16), calls=%async_computation.1 | async-start | bytes 3276800 | tf_op jit(solution)/shard_map/all_to_all | solution.py:70
  72.8 16.7 %collective-permute-start.10 = (bf16[64,1280]{1,0:T(8,128)(2,1)}, bf16[64,1280]{1,0:T(8,128)(2,1)S(1)}, u32[]{:S(2)}, u32[]{:S(2)}) collective-permute-start(bf16[64,1280]{1,0:T(8,128)(2,1)} %slice.40), channel_id=1, source_target_pairs={{0,2},{2,4},{4,6},{6,8},{8,10},{10,12},{12,14},{14,0},{1,3},{3,5},... | collective-permute-start | bytes 491528 | tf_op jit(solution)/shard_map/ppermute | solution.py:19
  74.4 15.2 %collective-permute-start.11 = (bf16[64,1280]{1,0:T(8,128)(2,1)}, bf16[64,1280]{1,0:T(8,128)(2,1)S(1)}, u32[]{:S(2)}, u32[]{:S(2)}) collective-permute-start(bf16[64,1280]{1,0:T(8,128)(2,1)} %slice.41), channel_id=1, source_target_pairs={{0,14},{2,0},{4,2},{6,4},{8,6},{10,8},{12,10},{14,12},{1,15},{3,1}... | collective-permute-start | bytes 491528 | tf_op jit(solution)/shard_map/ppermute | solution.py:19
  78.6 11.1 %copy-start.1 = (bf16[640,1280]{1,0:T(8,128)(2,1)S(1)}, bf16[640,1280]{1,0:T(8,128)(2,1)}, u32[]{:S(2)}) copy-start(bf16[640,1280]{1,0:T(8,128)(2,1)} %copy-done) | copy-start | bytes 4915204
  78.6 6.9 %collective-permute-start.14 = (bf16[160,128]{1,0:T(8,128)(2,1)S(1)}, bf16[160,128]{1,0:T(8,128)(2,1)S(1)}, u32[]{:S(2)}, u32[]{:S(2)}) collective-permute-start(bf16[160,128]{1,0:T(8,128)(2,1)S(1)} %bitcast.73), channel_id=1, source_target_pairs={{0,8},{2,10},{4,12},{6,14},{8,0},{10,2},{12,4},{14,6},{1,9},{3,11}... | collective-permute-start | bytes 122888 | tf_op jit(solution)/shard_map/ppermute | solution.py:19
  85.6 6.3 %collective-permute-start.15 = (bf16[2,160,128]{2,1,0:T(8,128)(2,1)S(1)}, bf16[2,160,128]{2,1,0:T(8,128)(2,1)S(1)}, u32[]{:S(2)}, u32[]{:S(2)}) collective-permute-start(bf16[2,160,128]{2,1,0:T(8,128)(2,1)S(1)} %pad_maximum_fusion.7), channel_id=1, source_target_pairs={{0,14},{2,0},{4,2},{6,4},{8,6},{10,8},{12,10},{14,12},{1,15},{3,1}... | collective-permute-start | bytes 245768 | tf_op jit(solution)/shard_map/ppermute | solution.py:19
  85.9 6.0 %collective-permute-start.16 = (bf16[2,160,128]{2,1,0:T(8,128)(2,1)S(1)}, bf16[2,160,128]{2,1,0:T(8,128)(2,1)S(1)}, u32[]{:S(2)}, u32[]{:S(2)}) collective-permute-start(bf16[2,160,128]{2,1,0:T(8,128)(2,1)S(1)} %pad_maximum_fusion.7), channel_id=1, source_target_pairs={{0,4},{2,6},{4,8},{6,10},{8,12},{10,14},{12,0},{14,2},{1,5},{3,7},... | collective-permute-start | bytes 245768 | tf_op jit(solution)/shard_map/ppermute | solution.py:19
  88.2 4.8 %collective-permute-start.17 = (bf16[2,160,128]{2,1,0:T(8,128)(2,1)S(1)}, bf16[2,160,128]{2,1,0:T(8,128)(2,1)S(1)}, u32[]{:S(2)}, u32[]{:S(2)}) collective-permute-start(bf16[2,160,128]{2,1,0:T(8,128)(2,1)S(1)} %pad_maximum_fusion.7), channel_id=1, source_target_pairs={{0,2},{2,4},{4,6},{6,8},{8,10},{10,12},{12,14},{14,0},{1,3},{3,5},... | collective-permute-start | bytes 245768 | tf_op jit(solution)/shard_map/ppermute | solution.py:19
  93.5 10.9 %collective-permute-start.18 = (bf16[1280,128]{1,0:T(8,128)(2,1)S(1)}, bf16[1280,128]{1,0:T(8,128)(2,1)S(1)}, u32[]{:S(2)}, u32[]{:S(2)}) collective-permute-start(bf16[1280,128]{1,0:T(8,128)(2,1)S(1)} %convolution_convert_fusion), channel_id=1, source_target_pairs={{0,16},{16,0},{1,17},{17,1},{2,18},{18,2},{3,19},{19,3},{4,20},{20... | collective-permute-start | bytes 983048 | tf_op jit(solution)/shard_map/ppermute | solution.py:19
  99.8 16.5 %all-to-all-start.2 = ((bf16[16,48,640]{2,1,0:T(8,128)(2,1)}), bf16[16,48,640]{2,1,0:T(8,128)(2,1)S(1)}, u32[]{:S(2)}, u32[]{:S(2)}) async-start(bf16[16,48,640]{2,1,0:T(8,128)(2,1)} %bitcast.23), calls=%async_computation.2 | async-start | bytes 1966080 | tf_op jit(solution)/shard_map/all_to_all | solution.py:70
  104.6 19.4 %collective-permute-start.19 = (bf16[2560,128]{1,0:T(8,128)(2,1)S(1)}, bf16[2560,128]{1,0:T(8,128)(2,1)S(1)}, u32[]{:S(2)}, u32[]{:S(2)}) collective-permute-start(bf16[2560,128]{1,0:T(8,128)(2,1)S(1)} %bitcast.71), channel_id=1, source_target_pairs={{0,1},{1,0},{2,3},{3,2},{4,5},{5,4},{6,7},{7,6},{8,9},{9,8},{10,11... | collective-permute-start | bytes 1966088 | tf_op jit(solution)/shard_map/ppermute | solution.py:19
  116.5 8.4 %collective-permute-start.12 = (bf16[128,320]{1,0:T(8,128)(2,1)S(1)}, bf16[128,320]{1,0:T(8,128)(2,1)S(1)}, u32[]{:S(2)}, u32[]{:S(2)}) collective-permute-start(bf16[128,320]{1,0:T(8,128)(2,1)S(1)} %get-tuple-element.24), channel_id=1, source_target_pairs={{0,1},{1,0},{2,3},{3,2},{4,5},{5,4},{6,7},{7,6},{8,9},{9,8},{10,11... | collective-permute-start | bytes 245768 | tf_op jit(solution)/shard_map/ppermute | solution.py:19
  126.9 3.7 %copy-start.6 = (s32[8]{0:T(128)S(1)}, s32[8]{0:T(128)}, u32[]{:S(2)}) copy-start(s32[8]{0:T(128)} %param.12) | copy-start | bytes 100
  126.9 25.0 %all-to-all-start.3 = ((bf16[8,40,2560]{2,1,0:T(8,128)(2,1)}), bf16[8,40,2560]{2,1,0:T(8,128)(2,1)S(1)}, u32[]{:S(2)}, u32[]{:S(2)}) async-start(bf16[8,40,2560]{2,1,0:T(8,128)(2,1)} %bitcast.33), calls=%async_computation.3 | async-start | bytes 3276800 | tf_op jit(solution)/shard_map/all_to_all | solution.py:118
Sparse Core Ops, SparseCore 0:
  29.3 37.5 all-gather.1

commit v3 on v2

v3 whole, which is shorter than its diff:
```python
import jax
import jax.numpy as jnp
import numpy as np
from jax import lax
from jax.experimental import pallas as pl
from jax.experimental.pallas import tpu as pltpu
from jax.sharding import Mesh, PartitionSpec as P

SEQ_GRP = 1
TENANTS = 2
AXES = ("xl", "y", "xh", "z", "core")
SIZES = (2, 4, 2, 8, 2)
GRP = ("xl", "y")
BF16, F32 = jnp.bfloat16, jnp.float32


def shift(x, axis, step=1):
    count = SIZES[AXES.index(axis)]
    return lax.ppermute(x, axis, [(i, (i + step) % count) for i in range(count)])


def stage(*arrays):
    return lax.optimization_barrier(arrays)


def ordered(x, other, axis):
    first = lax.axis_index(axis) == 0
    return jnp.concatenate([jnp.where(first, x, other), jnp.where(first, other, x)])


def rows_dot(a, b):
    return lax.dot_general(
        a, b, (((1,), (1,)), ((), ())), preferred_element_type=F32
    ).astype(BF16)


def product_kernel(spans, xh_ref, *refs):
    out_ref, left, right, sems = refs[-4:]
    sources, pieces = refs[: len(spans)], refs[len(spans) : -4]
    copies, row = [], 0
    for k, (ref, (first, rows)) in enumerate(zip(sources, spans)):
        copies.append(
            pltpu.make_async_copy(
                ref.at[pl.ds(first, rows)], left.at[pl.ds(row, rows)], sems.at[k]
            )
        )
        row += rows
    row = 0
    for k, ref in enumerate(pieces, len(spans)):
        place = right.at[pl.ds(row, ref.shape[0])]
        copies.append(pltpu.make_async_copy(ref, place, sems.at[k]))
        row += ref.shape[0]
    for copy in copies:
        copy.start()
    groups, cols = out_ref.shape[1], out_ref.shape[3]
    step = 16
    waited = 0
    for half, ready in enumerate((len(spans) + 2, len(copies))):
        for copy in copies[waited:ready]:
            copy.wait()
        waited = ready
        out = lax.dot_general(
            left[...],
            right[half * cols : (half + 1) * cols],
            (((1,), (1,)), ((), ())),
            preferred_element_type=F32,
        ).astype(BF16)
        side = (xh_ref[0] + half) % 2
        for slot in range(left.shape[0] // (groups * step)):
            for group in range(groups):
                row = (slot * groups + group) * step
                out_ref[side, group, slot * step : (slot + 1) * step] = out[
                    row : row + step
                ]


def product(parts, pieces, xh):
    arrays = [p[0] for p in parts]
    depth = arrays[0].shape[1]
    total = sum(p[2] for p in parts)
    cols = sum(p.shape[0] for p in pieces)
    spans = [p[1:] for p in parts]
    return pl.pallas_call(
        lambda *refs: product_kernel(spans, *refs),
        out_shape=jax.ShapeDtypeStruct((2, 8, total // 8, cols // 2), BF16),
        in_specs=[pl.BlockSpec(memory_space=pltpu.SMEM)]
        + [pl.BlockSpec(memory_space=pl.ANY)] * (len(parts) + len(pieces)),
        out_specs=pl.BlockSpec(memory_space=pltpu.VMEM),
        scratch_shapes=[
            pltpu.VMEM((total, depth), BF16),
            pltpu.VMEM((cols, depth), BF16),
            pltpu.SemaphoreType.DMA((len(parts) + len(pieces),)),
        ],
        compiler_params=pltpu.CompilerParams(vmem_limit_bytes=40 << 20),
        cost_estimate=pl.CostEstimate(
            flops=2 * total * depth * cols,
            bytes_accessed=2 * (total * depth + cols * depth + total * cols),
            transcendentals=0,
        ),
    )(xh.reshape(1).astype(jnp.int32), *arrays, *pieces)


def inputs_kernel(spans, core_ref, *refs):
    own, other, out_ref, chunks, sems = refs[-5:]
    copies = []
    for k, (ref, (first, rows)) in enumerate(zip(refs[: len(spans)], spans)):
        source = ref.at[pl.ds(first, rows)]
        copies.append(pltpu.make_async_copy(source, chunks.at[k], sems.at[k]))
    for copy in copies:
        copy.start()
    for copy in copies:
        copy.wait()
    wide = [chunks[k].astype(F32) for k in range(len(spans))]
    depth = chunks.shape[2]
    quarters = own.shape[1] // depth
    totals = [0.0, 0.0]
    for q in range(quarters):
        rows = [
            w[first : first + 8]
            for w in wide
            for first in (q * 8, (quarters + q) * 8)
        ]
        heard = jnp.concatenate(rows).astype(BF16)
        for side, cols in enumerate((own, other)):
            totals[side] += lax.dot_general(
                cols[:, q * depth : (q + 1) * depth],
                heard,
                (((1,), (1,)), ((), ())),
                preferred_element_type=F32,
            )
    for side in range(2):
        out_ref[(core_ref[0] + side) % 2] = totals[side].astype(BF16)


def inputs(parts, own, other, core):
    arrays = [p[0] for p in parts]
    spans = [p[1:] for p in parts]
    rows, depth = spans[0][1], arrays[0].shape[1]
    tokens = rows * depth // own.shape[1] * len(parts)
    return pl.pallas_call(
        lambda *refs: inputs_kernel(spans, *refs),
        out_shape=jax.ShapeDtypeStruct((2, own.shape[0], tokens), BF16),
        in_specs=[pl.BlockSpec(memory_space=pltpu.SMEM)]
        + [pl.BlockSpec(memory_space=pl.ANY)] * len(parts)
        + [pl.BlockSpec(memory_space=pltpu.VMEM)] * 2,
        out_specs=pl.BlockSpec(memory_space=pltpu.VMEM),
        scratch_shapes=[
            pltpu.VMEM((len(parts), rows, depth), BF16),
            pltpu.SemaphoreType.DMA((len(parts),)),
        ],
        compiler_params=pltpu.CompilerParams(vmem_limit_bytes=24 << 20),
        cost_estimate=pl.CostEstimate(
            flops=4 * own.size * tokens,
            bytes_accessed=4 * own.size + 2 * len(parts) * rows * depth,
            transcendentals=0,
        ),
    )(core.reshape(1).astype(jnp.int32), *arrays, own, other)


def arrange_kernel(place_ref, near, below, above, two, out_ref):
    xh, z = place_ref[0], place_ref[1]
    for steps, ref, far in (
        (0, near, 0),
        (1, above, 0),
        (2, two, 1),
        (3, below, 1),
        (4, near, 1),
        (5, above, 1),
        (6, two, 0),
        (7, below, 0),
    ):
        for side in range(2):
            out_ref[(xh + side) % 2, (z + steps) % 8] = ref[far, side]


def arrange(place, *pieces):
    return pl.pallas_call(
        arrange_kernel,
        out_shape=jax.ShapeDtypeStruct((2, 8) + pieces[0].shape[2:], BF16),
        in_specs=[pl.BlockSpec(memory_space=pltpu.SMEM)]
        + [pl.BlockSpec(memory_space=pltpu.VMEM)] * 4,
        out_specs=pl.BlockSpec(memory_space=pltpu.VMEM),
        compiler_params=pltpu.CompilerParams(vmem_limit_bytes=16 << 20),
    )(place, *pieces)


def shards(acts, grads, basis_in, basis_out, tenant):
    tokens, hidden = grads.shape
    model = acts.shape[1]
    own_in, own_out = basis_in.shape[1], basis_out.shape[1]
    groups, planes = 8, 16
    rows = hidden // planes
    xh, z, core = (lax.axis_index(a) for a in ("xh", "z", "core"))

    in_cols = basis_in.T
    in_other = shift(in_cols, "core")
    acts_x = shift(acts, "xh")
    step = lambda i: ((i // 2 + 1 - 2 * (i % 2)) % 8) * 2 + i % 2
    turn = [(i, step(i)) for i in range(16)]
    over = [(i, step(i ^ 1)) for i in range(16)]
    ring = lambda x, way=turn: lax.ppermute(x, ("z", "core"), way)
    quarters = model // rows
    tall = lambda a: a.reshape(tokens, quarters, rows).transpose(1, 0, 2).reshape(-1, rows)
    own_acts = jnp.concatenate([tall(acts), tall(acts_x)])
    acts_1 = [ring(own_acts), ring(own_acts, over)]

    sent = grads.reshape(tokens, planes, rows).transpose(1, 0, 2)
    panel = lax.all_to_all(sent, ("xl", "y", "xh"), 0, 0).reshape(planes * tokens, rows)

    out_cols = basis_out.T
    keep = lax.dynamic_slice_in_dim(out_cols, xh * rows, rows, axis=1)
    give = lax.dynamic_slice_in_dim(out_cols, (1 - xh) * rows, rows, axis=1)
    panel, keep, give, *acts_1 = stage(panel, keep, give, *acts_1)
    size, extra = panel.shape[0], own_acts.shape[0]
    keep_c = shift(keep, "core")
    turned = ring(jnp.concatenate([panel, *acts_1]))
    crossed = ring(panel, over)
    got = [shift(give[: own_out // 2], "xh")]
    give, got[0], turned, crossed = stage(give, got[0], turned, crossed)
    block_2 = ring(jnp.concatenate([turned[:size], crossed, turned[size:]]))
    got.append(shift(give[own_out // 2 :], "xh"))
    got[1], block_2 = stage(got[1], block_2)
    got_c = shift(jnp.concatenate(got), "core")
    block_3 = ring(block_2[: 2 * size + extra])
    pieces = (keep, keep_c, *got, got_c)
    parts = [(panel, 0), (turned, 0), (crossed, 0), (block_2, 0), (block_2, size)]
    out = product([(*p, size) for p in parts], pieces, xh)
    out, block_3, in_cols, in_other, *pieces = stage(
        out, block_3, in_cols, in_other, *pieces
    )

    def home(out):
        out = out.reshape(planes, out.shape[2], 2 * own_out)
        return lax.all_to_all(out, ("xh", "xl", "y"), 0, 0)

    first = home(out)
    last = ring(block_3[:size])

    parts = [
        (own_acts, 0),
        *((a, 0) for a in acts_1),
        *((turned, size + k * extra) for k in range(2)),
        *((block_2, 2 * size + k * extra) for k in range(2)),
        (block_3, 2 * size),
    ]
    r = inputs([(*p, extra) for p in parts], in_cols, in_other, core).reshape(2 * own_in, 16 * tokens)
    r = jnp.concatenate([r, shift(r, "core")], axis=1)
    z_j, xh_j, row = np.unravel_index(np.arange(16 * tokens), (8, 2, tokens))
    apart = (z_j - z) % 8
    ran = jnp.where(apart % 4 == 0, core, (apart < 4).astype(core.dtype))
    away = jnp.minimum(apart, 8 - apart)
    slot = jnp.where(away == 0, 0, jnp.where(away == 4, 7, 2 * away - 1 + (ran ^ core)))
    source = (((ran ^ core) * 8 + slot) * 2 + (xh_j ^ xh)) * tokens + row
    pick = (jnp.arange(32 * tokens)[:, None] == source[None, :]).astype(BF16)
    r = jnp.dot(r, pick, preferred_element_type=F32).astype(BF16)

    far = shift(r, "z", 4)
    cross = shift(r, "xh")
    both = [((a, b), (1 - a, (b + 4) % 8)) for a in range(2) for b in range(8)]
    far_cross = lax.ppermute(
        r, ("xh", "z"), [(a * 8 + b, c * 8 + d) for (a, b), (c, d) in both]
    )
    parts = [(block_3, 0, size), (block_3, size, size), (last, 0, size)]
    out = product(parts, pieces, xh)
    out, first, r, far, cross, far_cross = stage(out, first, r, far, cross, far_cross)
    second = home(out)

    quad = jnp.stack([jnp.stack([r, cross]), jnp.stack([far, far_cross])])
    below, above, two = shift(quad, "z", 1), shift(quad, "z", -1), shift(quad, "z", 2)
    place = jnp.stack([xh, z]).astype(jnp.int32)
    r = arrange(place, quad, below, above, two).reshape(32 * own_in, 16 * tokens)
    r = jnp.concatenate([r, shift(r, "core")], axis=1)
    side, slot, half_x, row = np.unravel_index(
        np.arange(32 * tokens), (2, 8, 2, tokens)
    )
    ran = core ^ side
    steps = np.array([0, 1, 1, 2, 2, 3, 3, 4])[slot]
    from_core = ran ^ np.where(np.isin(slot, (0, 7)), 0, (slot - 1) % 2)
    z_of = (z + (2 * ran - 1) * steps) % 8
    source = (((from_core ^ core) * 8 + z_of) * 2 + half_x) * tokens + row
    pick = (jnp.arange(32 * tokens)[:, None] == source[None, :]).astype(BF16)
    rotated_in = jnp.dot(r, pick, preferred_element_type=F32).astype(BF16)

    mixed = jnp.concatenate(
        [jnp.sum(p.astype(F32), axis=0).astype(BF16) for p in (first, second)]
    )
    left = jnp.concatenate([mixed[:, :own_out], shift(mixed[:, own_out:], "core")])

    corr = lax.dot_general(
        left, rotated_in, (((0,), (1,)), ((), ())), preferred_element_type=F32
    )
    square = (corr * corr).astype(BF16)
    parts = lax.all_to_all(
        square.reshape(groups, own_out // groups, square.shape[1]), GRP, 0, 0
    ).astype(F32)
    sums = jnp.stack(
        [
            jnp.sum(jnp.where((tenant == k)[:, None, None], parts, 0.0), axis=0)
            for k in range(TENANTS)
        ]
    )
    total = jnp.sum(sums, axis=0)
    seq_count = SEQ_GRP * groups
    scale = 1.0 / float((seq_count - seq_count // TENANTS) * 32 * tokens)
    return (total[None] - sums) * scale


def solution(mesh):
    fine = Mesh(mesh.devices.reshape(SIZES), AXES)
    tile = ("xh", "z", "core")
    return jax.shard_map(
        shards,
        mesh=fine,
        in_specs=(
            P(AXES, None),
            P(AXES, None),
            P(None, tile),
            P(GRP, tile),
            P(),
        ),
        out_specs=P(None, tile + GRP, None),
        check_vma=False,
    )
```

time: 161 us -> 156 us (0.969)
  between operations: 13.8 us -> 0.47 us
  waiting for transfers between devices: 52.4 us -> 65.5 us
  Pallas kernels: 0 us -> 12.9 us
  matrix products: 14.9 us -> 2.48 us
  starting transfers between devices: 69.4 us -> 60.4 us
  local copies, waits for them, and re-layouts: 4.31 us -> 8.64 us
    ppermute x20 -> x14, starting transfers between devices: 49.4 us -> 27.9 us  [shift(): lax.ppermute(x, axis, [(i, (i + step) % count) for i in range(count)])]
    ppermute x0 -> x8, waiting for transfers between devices: none -> 18.9 us  [the longest x7 14.3 us: shards(): ring = lambda x, way=turn: lax.ppermute(x, ('z', 'core'), way)]
    pallas_call x0 -> x4, Pallas kernels: none -> 12.9 us  [the longest x2 9.56 us: product(): pl.pallas_call(lambda *refs: product_kernel(spans, *refs), out_shape=jax....]
    dot_general x5 -> x0, matrix products: 12.6 us -> none  [rows_dot(): lax.dot_general(a, b, (((1,), (1,)), ((), ())), preferred_element_type=F32)]
    ppermute x0 -> x8, starting transfers between devices: none -> 11.2 us  [the longest x7 11.2 us: shards(): ring = lambda x, way=turn: lax.ppermute(x, ('z', 'core'), way)]
    unnamed x33 -> x56, local copies, waits for them, and re-layouts: 0.33 us -> 6.96 us
    all_to_all x3, waiting for transfers between devices: 4.99 us -> 0.01 us  [the longest x2 0.01 us: home(): return lax.all_to_all(out, ('xh', 'xl', 'y'), 0, 0)]
    another operation x7 -> x3, other arithmetic: 2.69 us -> 0.11 us  [the longest x1 0.07 us: shards(): place = jnp.stack([xh, z]).astype(jnp.int32)]
  transfers between devices with their start and end apart: 25 -> 26, of which waited for: 10 -> 14; matrix products, arithmetic and copies ran while one was open for 13% -> 3% of each run, Pallas kernels for 0% -> 8%
where the time goes in v3:
time: 156 us; the launch traced here: 155 us
  waiting for transfers between devices  65.5 us (42%)
  starting transfers between devices  60.4 us (39%)
  Pallas kernels  12.9 us (8%)
  local copies, waits for them, and re-layouts  8.64 us (6%)
  other arithmetic  4.8 us (3%)
  matrix products  2.48 us (2%)
    ppermute x14, starting transfers between devices, shift(): lax.ppermute(x, axis, [(i, (i + step) % count) for i in range(count)])  27.9 us
    ppermute x14, waiting for transfers between devices, shift(): lax.ppermute(x, axis, [(i, (i + step) % count) for i in range(count)])  25.3 us
    all_to_all x1, waiting for transfers between devices, shards(): lax.all_to_all(square.reshape(groups, own_out // groups, square.shape[1])...  21.3 us
    ppermute x7, waiting for transfers between devices, shards(): ring = lambda x, way=turn: lax.ppermute(x, ('z', 'core'), way)  14.3 us
    ppermute x7, starting transfers between devices, shards(): ring = lambda x, way=turn: lax.ppermute(x, ('z', 'core'), way)  11.2 us
    all_to_all x2, starting transfers between devices, home(): return lax.all_to_all(out, ('xh', 'xl', 'y'), 0, 0)  11 us
    pallas_call x2, Pallas kernels, product(): pl.pallas_call(lambda *refs: product_kernel(spans, *refs), out_shape=jax....  9.56 us
    unnamed x56, local copies, waits for them, and re-layouts  6.96 us
  transfers between devices with their start and end apart: 26, of which 14 were waited for; matrix products, arithmetic and copies ran while one was open for 3% of the time, Pallas kernels for 8%

profile of v3, /device:TPU:1, one launch (start us, length us, event | category | flops | bytes accessed | tf_op | source)
XLA Modules:
  0.0 155.2 jit_solution(4806274414857944403)
XLA Ops:
  0.0 3.6 %collective-permute-start = (bf16[8,5120]{1,0:T(8,128)(2,1)}, bf16[8,5120]{1,0:T(8,128)(2,1)S(1)}, u32[]{:S(2)}, u32[]{:S(2)}) collective-permute-start(bf16[8,5120]{1,0:T(8,128)(2,1)} %param.13), channel_id=1, source_target_pairs={{0,16},{16,0},{1,17},{17,1},{2,18},{18,2},{3,19},{19,3},{4,20},{20... | collective-permute-start | bytes 245768 | tf_op jit(solution)/shard_map/ppermute | solution.py:19
  3.6 4.9 %all-to-all-start = ((bf16[16,8,1280]{2,1,0:T(8,128)(2,1)}), bf16[16,8,1280]{2,1,0:T(8,128)(2,1)S(1)}, u32[]{:S(2)}, u32[]{:S(2)}) async-start(bf16[16,8,1280]{2,1,0:T(8,128)(2,1)} %bitcast.49), calls=%async_computation | async-start | bytes 655360 | tf_op jit(solution)/shard_map/all_to_all | solution.py:208
  8.5 0.9 pad_maximum_fusion.3.refs_1_
  9.4 5.7 %collective-permute-start.1 = (bf16[64,1280]{1,0:T(8,128)(2,1)S(1)}, bf16[64,1280]{1,0:T(8,128)(2,1)S(1)}, u32[]{:S(2)}, u32[]{:S(2)}) collective-permute-start(bf16[64,1280]{1,0:T(8,128)(2,1)S(1)} %pad_maximum_fusion.3.refs_1_), channel_id=1, source_target_pairs={{0,2},{1,15},{2,4},{3,1},{4,6},{5,3},{6,8},{7,5},{8,10},{9,7},{10,... | collective-permute-start | bytes 491528 | tf_op jit(solution)/shard_map/ppermute | solution.py:201
  15.0 1.5 dynamic-slice_bitcast_fusion
  16.6 1.2 collective-permute-done.1.refs_2_
  17.7 2.4 %collective-permute-done.2.refs_3_ = bf16[64,1280]{1,0:T(8,128)(2,1)S(1)} collective-permute-done((bf16[64,1280]{1,0:T(8,128)(2,1)S(1)}, bf16[64,1280]{1,0:T(8,128)(2,1)S(1)}, u32[]{:S(2)}, u32[]{:S(2)}) %collective-permute-start.2) | collective-permute-done | bytes 163872 | tf_op jit(solution)/shard_map/ppermute | solution.py:201
  20.1 0.7 copy-done.15
  20.9 2.4 %collective-permute-start.4 = (bf16[256,1280]{1,0:T(8,128)(2,1)S(1)}, bf16[256,1280]{1,0:T(8,128)(2,1)S(1)}, u32[]{:S(2)}, u32[]{:S(2)}) collective-permute-start(bf16[256,1280]{1,0:T(8,128)(2,1)S(1)} %pad_maximum_fusion.2), channel_id=1, source_target_pairs={{0,2},{1,15},{2,4},{3,1},{4,6},{5,3},{6,8},{7,5},{8,10},{9,7},{10,... | collective-permute-start | bytes 1966088 | tf_op jit(solution)/shard_map/ppermute | solution.py:201
  23.3 2.6 %collective-permute-start.3 = (bf16[160,1280]{1,0:T(8,128)(2,1)S(1)}, bf16[160,1280]{1,0:T(8,128)(2,1)S(1)}, u32[]{:S(2)}, u32[]{:S(2)}) collective-permute-start(bf16[160,1280]{1,0:T(8,128)(2,1)S(1)} %slice.24), channel_id=1, source_target_pairs={{0,16},{16,0},{1,17},{17,1},{2,18},{18,2},{3,19},{19,3},{4,20},{20... | collective-permute-start | bytes 1228808 | tf_op jit(solution)/shard_map/ppermute | solution.py:19
  25.9 8.2 %collective-permute-done.5.refs_3_ = bf16[128,1280]{1,0:T(8,128)(2,1)S(1)} collective-permute-done((bf16[128,1280]{1,0:T(8,128)(2,1)S(1)}, bf16[128,1280]{1,0:T(8,128)(2,1)S(1)}, u32[]{:S(2)}, u32[]{:S(2)}) %collective-permute-start.5) | collective-permute-done | bytes 327712 | tf_op jit(solution)/shard_map/ppermute | solution.py:201
  34.1 0.9 collective-permute-done.3.refs_8_.refs_6_
  35.0 0.1 pad_maximum_fusion
  35.1 2.5 %collective-permute-start.7 = (bf16[384,1280]{1,0:T(8,128)(2,1)S(1)}, bf16[384,1280]{1,0:T(8,128)(2,1)S(1)}, u32[]{:S(2)}, u32[]{:S(2)}) collective-permute-start(bf16[384,1280]{1,0:T(8,128)(2,1)S(1)} %pad_maximum_fusion), channel_id=1, source_target_pairs={{0,2},{1,15},{2,4},{3,1},{4,6},{5,3},{6,8},{7,5},{8,10},{9,7},{10,... | collective-permute-start | bytes 2949128 | tf_op jit(solution)/shard_map/ppermute | solution.py:201
  37.7 2.6 %collective-permute-start.6 = (bf16[160,1280]{1,0:T(8,128)(2,1)S(1)}, bf16[160,1280]{1,0:T(8,128)(2,1)S(1)}, u32[]{:S(2)}, u32[]{:S(2)}) collective-permute-start(bf16[160,1280]{1,0:T(8,128)(2,1)S(1)} %slice.25), channel_id=1, source_target_pairs={{0,16},{16,0},{1,17},{17,1},{2,18},{18,2},{3,19},{19,3},{4,20},{20... | collective-permute-start | bytes 1228808 | tf_op jit(solution)/shard_map/ppermute | solution.py:19
  40.3 0.1 collective-permute-start.8
  40.5 9.9 %collective-permute-done.6.refs_9_.refs_7_ = bf16[160,1280]{1,0:T(8,128)(2,1)S(1)} collective-permute-done((bf16[160,1280]{1,0:T(8,128)(2,1)S(1)}, bf16[160,1280]{1,0:T(8,128)(2,1)S(1)}, u32[]{:S(2)}, u32[]{:S(2)}) %collective-permute-start.6) | collective-permute-done | bytes 409632 | tf_op jit(solution)/shard_map/ppermute | solution.py:19
  50.4 0.1 pad_maximum_fusion.1
  50.5 2.5 %collective-permute-start.9 = (bf16[320,1280]{1,0:T(8,128)(2,1)S(1)}, bf16[320,1280]{1,0:T(8,128)(2,1)S(1)}, u32[]{:S(2)}, u32[]{:S(2)}) collective-permute-start(bf16[320,1280]{1,0:T(8,128)(2,1)S(1)} %pad_maximum_fusion.1), channel_id=1, source_target_pairs={{0,1},{1,0},{2,3},{3,2},{4,5},{5,4},{6,7},{7,6},{8,9},{9,8},{10,11... | collective-permute-start | bytes 2457608 | tf_op jit(solution)/shard_map/ppermute | solution.py:19
  53.0 0.1 collective-permute-start.11
  53.1 0.1 slice.28
  53.2 0.6 collective-permute-start.10
  53.8 1.2 collective-permute-done.9.refs_10_.refs_8_
  55.0 5.1 %shard_map.127 = bf16[2,8,80,640]{3,2,1,0:T(8,128)(2,1)S(1)} custom-call(s32[1]{0:T(128)} %bitcast.refs_0_, bf16[128,1280]{1,0:T(8,128)(2,1)S(1)} %bitcast.40, bf16[256,1280]{1,0:T(8,128)(2,1)S(1)} %collective-permute-done.4.refs_2_.refs_4_.refs_5_, bf16[128,1280]{1,0:T(8,128)(2,1)S(1)} %collective-permute-done.5.refs_3_, ...), custom_call_target="tpu_custom_call" | custom-call | flops 2097152000 | bytes 6553600 | tf_op jit(solution)/shard_map/pallas_call | solution.py:83
  60.1 1.1 copy-done
  61.3 0.9 copy-done.13
  62.1 2.6 %collective-permute-done.10.refs_1_.refs_2_.refs_8_ = bf16[320,1280]{1,0:T(8,128)(2,1)S(1)} collective-permute-done((bf16[320,1280]{1,0:T(8,128)(2,1)S(1)}, bf16[320,1280]{1,0:T(8,128)(2,1)S(1)}, u32[]{:S(2)}, u32[]{:S(2)}) %collective-permute-start.10) | collective-permute-done | bytes 819232 | tf_op jit(solution)/shard_map/ppermute | solution.py:201
  64.7 6.4 %all-to-all-start.1 = ((bf16[16,80,640]{2,1,0:T(8,128)(2,1)}), bf16[16,80,640]{2,1,0:T(8,128)(2,1)}, u32[]{:S(2)}, u32[]{:S(2)}) async-start(bf16[16,80,640]{2,1,0:T(8,128)(2,1)} %bitcast.37), calls=%async_computation.1 | async-start | bytes 3276800 | tf_op jit(solution)/shard_map/all_to_all | solution.py:234
  71.2 1.1 copy-done.12
  72.3 1.1 copy-done.14
  73.4 0.9 copy-done.16
  74.4 0.9 copy-done.18
  75.3 2.8 %shard_map.129 = bf16[2,80,128]{2,1,0:T(8,128)(2,1)S(1)} custom-call(s32[1]{0:T(128)} %bitcast.14.refs_0_, bf16[64,1280]{1,0:T(8,128)(2,1)S(1)} %copy-done.18, bf16[64,1280]{1,0:T(8,128)(2,1)S(1)} %collective-permute-done.1.refs_2_, bf16[64,1280]{1,0:T(8,128)(2,1)S(1)} %copy-done.16, bf16[256,1280]{1,0:T(8,128)(2,1)S(1)} %collective-permute-done.4.refs_2_.refs_4_.refs_5_, ...), custom_call_target="tpu_custom_call" | custom-call | flops 209715200 | bytes 2949120 | tf_op jit(solution)/shard_map/pallas_call | solution.py:140
  78.1 3.0 %collective-permute-start.13 = (bf16[160,128]{1,0:T(8,128)(2,1)S(1)}, bf16[160,128]{1,0:T(8,128)(2,1)S(1)}, u32[]{:S(2)}, u32[]{:S(2)}) collective-permute-start(bf16[160,128]{1,0:T(8,128)(2,1)S(1)} %bitcast.45), channel_id=1, source_target_pairs={{0,1},{1,0},{2,3},{3,2},{4,5},{5,4},{6,7},{7,6},{8,9},{9,8},{10,11... | collective-permute-start | bytes 122888 | tf_op jit(solution)/shard_map/ppermute | solution.py:19
  81.2 0.8 collective-permute-done.13
  82.0 0.2 convolution_convert_fusion.1
  82.1 5.3 %collective-permute-start.14 = (bf16[160,128]{1,0:T(8,128)(2,1)S(1)}, bf16[160,128]{1,0:T(8,128)(2,1)S(1)}, u32[]{:S(2)}, u32[]{:S(2)}) collective-permute-start(bf16[160,128]{1,0:T(8,128)(2,1)S(1)} %convolution_convert_fusion.1), channel_id=1, source_target_pairs={{0,8},{2,10},{4,12},{6,14},{8,0},{10,2},{12,4},{14,6},{1,9},{3,11}... | collective-permute-start | bytes 122888 | tf_op jit(solution)/shard_map/ppermute | solution.py:19
  87.5 3.1 %collective-permute-start.15 = (bf16[160,128]{1,0:T(8,128)(2,1)S(1)}, bf16[160,128]{1,0:T(8,128)(2,1)S(1)}, u32[]{:S(2)}, u32[]{:S(2)}) collective-permute-start(bf16[160,128]{1,0:T(8,128)(2,1)S(1)} %convolution_convert_fusion.1), channel_id=1, source_target_pairs={{0,16},{16,0},{1,17},{17,1},{2,18},{18,2},{3,19},{19,3},{4,20},{20... | collective-permute-start | bytes 122888 | tf_op jit(solution)/shard_map/ppermute | solution.py:19
  90.6 4.5 %shard_map.128 = bf16[2,8,48,640]{3,2,1,0:T(8,128)(2,1)} custom-call(s32[1]{0:T(128)} %bitcast.refs_0_, bf16[320,1280]{1,0:T(8,128)(2,1)S(1)} %collective-permute-done.10.refs_1_.refs_2_.refs_8_, bf16[320,1280]{1,0:T(8,128)(2,1)S(1)} %collective-permute-done.10.refs_1_.refs_2_.refs_8_, bf16[128,1280]{1,0:T(8,128)(2,1)S(1)} %collective-permute-done.12.refs_3_, ...), custom_call_target="tpu_custom_call" | custom-call | flops 1258291200 | bytes 5242880 | tf_op jit(solution)/shard_map/pallas_call | solution.py:83
  95.1 4.6 %collective-permute-done.16 = bf16[160,128]{1,0:T(8,128)(2,1)S(1)} collective-permute-done((bf16[160,128]{1,0:T(8,128)(2,1)S(1)}, bf16[160,128]{1,0:T(8,128)(2,1)S(1)}, u32[]{:S(2)}, u32[]{:S(2)}) %collective-permute-start.16) | collective-permute-done | bytes 40992 | tf_op jit(solution)/shard_map/ppermute | solution.py:260
  99.7 4.7 %all-to-all-start.2 = ((bf16[16,48,640]{2,1,0:T(8,128)(2,1)}), bf16[16,48,640]{2,1,0:T(8,128)(2,1)S(1)}, u32[]{:S(2)}, u32[]{:S(2)}) async-start(bf16[16,48,640]{2,1,0:T(8,128)(2,1)} %bitcast.16), calls=%async_computation.2 | async-start | bytes 1966080 | tf_op jit(solution)/shard_map/all_to_all | solution.py:234
  104.5 1.2 collective-permute-start.18
  105.6 1.6 %collective-permute-start.19 = (bf16[2,2,160,128]{3,2,1,0:T(8,128)(2,1)S(1)}, bf16[2,2,160,128]{3,2,1,0:T(8,128)(2,1)S(1)}, u32[]{:S(2)}, u32[]{:S(2)}) collective-permute-start(bf16[2,2,160,128]{3,2,1,0:T(8,128)(2,1)S(1)} %pad_maximum_fusion.4.near), channel_id=1, source_target_pairs={{0,14},{2,0},{4,2},{6,4},{8,6},{10,8},{12,10},{14,12},{1,15},{3,1}... | collective-permute-start | bytes 491528 | tf_op jit(solution)/shard_map/ppermute | solution.py:19
  107.2 0.1 pad_add_fusion.place_ref
  107.3 2.6 %collective-permute-done.18.below = bf16[2,2,160,128]{3,2,1,0:T(8,128)(2,1)S(1)} collective-permute-done((bf16[2,2,160,128]{3,2,1,0:T(8,128)(2,1)S(1)}, bf16[2,2,160,128]{3,2,1,0:T(8,128)(2,1)S(1)}, u32[]{:S(2)}, u32[]{:S(2)}) %collective-permute-start.18) | collective-permute-done | bytes 163872 | tf_op jit(solution)/shard_map/ppermute | solution.py:19
  109.9 0.2 collective-permute-done.19.above
  110.1 8.4 %collective-permute-done.20.two = bf16[2,2,160,128]{3,2,1,0:T(8,128)(2,1)S(1)} collective-permute-done((bf16[2,2,160,128]{3,2,1,0:T(8,128)(2,1)S(1)}, bf16[2,2,160,128]{3,2,1,0:T(8,128)(2,1)S(1)}, u32[]{:S(2)}, u32[]{:S(2)}) %collective-permute-start.20) | collective-permute-done | bytes 163872 | tf_op jit(solution)/shard_map/ppermute | solution.py:19
  118.5 0.6 shard_map.130
  119.1 0.0 copy-start.19
  119.1 0.0 copy-start.20
  119.1 0.0 copy-start.21
  119.2 0.0 copy-start.22
  119.2 0.0 copy-start.23
  119.2 2.0 %collective-permute-start.21 = (bf16[2560,128]{1,0:T(8,128)(2,1)S(1)}, bf16[2560,128]{1,0:T(8,128)(2,1)S(1)}, u32[]{:S(2)}, u32[]{:S(2)}) collective-permute-start(bf16[2560,128]{1,0:T(8,128)(2,1)S(1)} %bitcast.43), channel_id=1, source_target_pairs={{0,1},{1,0},{2,3},{3,2},{4,5},{5,4},{6,7},{7,6},{8,9},{9,8},{10,11... | collective-permute-start | bytes 1966088 | tf_op jit(solution)/shard_map/ppermute | solution.py:19
  121.1 1.7 %reduce_sum.52 = bf16[80,640]{1,0:T(8,128)(2,1)S(1)} reduce(bf16[16,80,640]{2,1,0:T(8,128)(2,1)} %all-to-all-done.1, bf16[]{:T(256)} %constant.88.clone.1), dimensions={0}, to_apply=%region_0.1 | reduce | flops 768000 | bytes 1740802 | tf_op jit(solution)/shard_map/reduce_sum | solution.py:285
  122.8 0.1 reduce_sum.53
  123.0 0.1 fusion.15
  123.1 0.1 collective-permute-start.17
  123.2 1.2 collective-permute-done.17
  124.5 2.3 %fusion = bf16[320,2560]{1,0:T(8,128)(2,1)} fusion(bf16[2560,128]{1,0:T(8,128)(2,1)S(1)} %collective-permute-done.21, bf16[2560,128]{1,0:T(8,128)(2,1)S(1)} %bitcast.44, bf16[128,320]{1,0:T(8,128)(2,1)S(1)} %collective-permute-done.17, bf16[128,320]{1,0:T(8,128)(2,1)S(1)} %get-tuple-element.63, s32[256]{0:T(256)S(1)} %fusion.26), kind=kOutput, calls=%fused_computation.3 | convolution fusion | flops 760283136 | bytes 3113984 | tf_op jit(solution)/shard_map/dot_general | solution.py:289
  126.8 5.4 %all-to-all-start.3 = ((bf16[8,40,2560]{2,1,0:T(8,128)(2,1)}), bf16[8,40,2560]{2,1,0:T(8,128)(2,1)S(1)}, u32[]{:S(2)}, u32[]{:S(2)}) async-start(bf16[8,40,2560]{2,1,0:T(8,128)(2,1)} %bitcast.25), calls=%async_computation.3 | async-start | bytes 3276800 | tf_op jit(solution)/shard_map/all_to_all | solution.py:293
  132.2 21.3 %all-to-all-done.3 = bf16[8,40,2560]{2,1,0:T(8,128)(2,1)S(1)} async-done(((bf16[8,40,2560]{2,1,0:T(8,128)(2,1)}), bf16[8,40,2560]{2,1,0:T(8,128)(2,1)S(1)}, u32[]{:S(2)}, u32[]{:S(2)}) %all-to-all-start.3) | async-done | bytes 1638432 | tf_op jit(solution)/shard_map/all_to_all | solution.py:293
  153.5 0.6 fusion.1
  154.2 1.0 fusion.9
  (72 shorter events, 0.4 us)
Async XLA Ops:
  0.0 8.5 %collective-permute-start = (bf16[8,5120]{1,0:T(8,128)(2,1)}, bf16[8,5120]{1,0:T(8,128)(2,1)S(1)}, u32[]{:S(2)}, u32[]{:S(2)}) collective-permute-start(bf16[8,5120]{1,0:T(8,128)(2,1)} %param.13), channel_id=1, source_target_pairs={{0,16},{16,0},{1,17},{17,1},{2,18},{18,2},{3,19},{19,3},{4,20},{20... | collective-permute-start | bytes 245768 | tf_op jit(solution)/shard_map/ppermute | solution.py:19
  3.6 16.5 %all-to-all-start = ((bf16[16,8,1280]{2,1,0:T(8,128)(2,1)}), bf16[16,8,1280]{2,1,0:T(8,128)(2,1)S(1)}, u32[]{:S(2)}, u32[]{:S(2)}) async-start(bf16[16,8,1280]{2,1,0:T(8,128)(2,1)} %bitcast.49), calls=%async_computation | async-start | bytes 655360 | tf_op jit(solution)/shard_map/all_to_all | solution.py:208
  9.4 7.2 %copy-start.17 = (bf16[64,1280]{1,0:T(8,128)(2,1)}, bf16[64,1280]{1,0:T(8,128)(2,1)S(1)}, u32[]{:S(2)}) copy-start(bf16[64,1280]{1,0:T(8,128)(2,1)S(1)} %pad_maximum_fusion.3.refs_1_) | copy-start | bytes 491524
  9.4 8.3 %collective-permute-start.1 = (bf16[64,1280]{1,0:T(8,128)(2,1)S(1)}, bf16[64,1280]{1,0:T(8,128)(2,1)S(1)}, u32[]{:S(2)}, u32[]{:S(2)}) collective-permute-start(bf16[64,1280]{1,0:T(8,128)(2,1)S(1)} %pad_maximum_fusion.3.refs_1_), channel_id=1, source_target_pairs={{0,2},{1,15},{2,4},{3,1},{4,6},{5,3},{6,8},{7,5},{8,10},{9,7},{10,... | collective-permute-start | bytes 491528 | tf_op jit(solution)/shard_map/ppermute | solution.py:201
  15.0 5.0 %collective-permute-start.2 = (bf16[64,1280]{1,0:T(8,128)(2,1)S(1)}, bf16[64,1280]{1,0:T(8,128)(2,1)S(1)}, u32[]{:S(2)}, u32[]{:S(2)}) collective-permute-start(bf16[64,1280]{1,0:T(8,128)(2,1)S(1)} %pad_maximum_fusion.3.refs_1_), channel_id=1, source_target_pairs={{0,15},{1,2},{2,1},{3,4},{4,3},{5,6},{6,5},{7,8},{8,7},{9,10},{10,... | collective-permute-start | bytes 491528 | tf_op jit(solution)/shard_map/ppermute | solution.py:201
  20.1 14.9 %copy-start.9 = (bf16[16,8,1280]{2,1,0:T(8,128)(2,1)}, bf16[16,8,1280]{2,1,0:T(8,128)(2,1)S(1)}, u32[]{:S(2)}) copy-start(bf16[16,8,1280]{2,1,0:T(8,128)(2,1)S(1)} %all-to-all-done) | copy-start | bytes 983044
  20.1 0.7 copy-start.15
  20.9 14.1 %collective-permute-start.4 = (bf16[256,1280]{1,0:T(8,128)(2,1)S(1)}, bf16[256,1280]{1,0:T(8,128)(2,1)S(1)}, u32[]{:S(2)}, u32[]{:S(2)}) collective-permute-start(bf16[256,1280]{1,0:T(8,128)(2,1)S(1)} %pad_maximum_fusion.2), channel_id=1, source_target_pairs={{0,2},{1,15},{2,4},{3,1},{4,6},{5,3},{6,8},{7,5},{8,10},{9,7},{10,... | collective-permute-start | bytes 1966088 | tf_op jit(solution)/shard_map/ppermute | solution.py:201
  23.3 11.7 %collective-permute-start.3 = (bf16[160,1280]{1,0:T(8,128)(2,1)S(1)}, bf16[160,1280]{1,0:T(8,128)(2,1)S(1)}, u32[]{:S(2)}, u32[]{:S(2)}) collective-permute-start(bf16[160,1280]{1,0:T(8,128)(2,1)S(1)} %slice.24), channel_id=1, source_target_pairs={{0,16},{16,0},{1,17},{17,1},{2,18},{18,2},{3,19},{19,3},{4,20},{20... | collective-permute-start | bytes 1228808 | tf_op jit(solution)/shard_map/ppermute | solution.py:19
  25.9 8.2 %collective-permute-start.5 = (bf16[128,1280]{1,0:T(8,128)(2,1)S(1)}, bf16[128,1280]{1,0:T(8,128)(2,1)S(1)}, u32[]{:S(2)}, u32[]{:S(2)}) collective-permute-start(bf16[128,1280]{1,0:T(8,128)(2,1)S(1)} %bitcast.39), channel_id=1, source_target_pairs={{0,15},{1,2},{2,1},{3,4},{4,3},{5,6},{6,5},{7,8},{8,7},{9,10},{10,... | collective-permute-start | bytes 983048 | tf_op jit(solution)/shard_map/ppermute | solution.py:201
  35.0 20.0 %copy-start.1 = (bf16[160,1280]{1,0:T(8,128)(2,1)}, bf16[160,1280]{1,0:T(8,128)(2,1)S(1)}, u32[]{:S(2)}) copy-start(bf16[160,1280]{1,0:T(8,128)(2,1)S(1)} %collective-permute-done.3.refs_8_.refs_6_) | copy-start | bytes 1228804
  35.1 17.9 %copy-start.11 = (bf16[5120,80]{0,1:T(8,128)(2,1)S(1)}, bf16[5120,80]{0,1:T(8,128)(2,1)}, u32[]{:S(2)}) copy-start(bf16[5120,80]{0,1:T(8,128)(2,1)} %param.15) | copy-start | bytes 2457604
  35.1 15.3 %collective-permute-start.7 = (bf16[384,1280]{1,0:T(8,128)(2,1)S(1)}, bf16[384,1280]{1,0:T(8,128)(2,1)S(1)}, u32[]{:S(2)}, u32[]{:S(2)}) collective-permute-start(bf16[384,1280]{1,0:T(8,128)(2,1)S(1)} %pad_maximum_fusion), channel_id=1, source_target_pairs={{0,2},{1,15},{2,4},{3,1},{4,6},{5,3},{6,8},{7,5},{8,10},{9,7},{10,... | collective-permute-start | bytes 2949128 | tf_op jit(solution)/shard_map/ppermute | solution.py:201
  37.7 17.3 %copy-start.10 = (bf16[16,8,1280]{2,1,0:T(8,128)(2,1)S(1)}, bf16[16,8,1280]{2,1,0:T(8,128)(2,1)}, u32[]{:S(2)}) copy-start(bf16[16,8,1280]{2,1,0:T(8,128)(2,1)} %copy-done.9) | copy-start | bytes 983044
  37.7 12.7 %collective-permute-start.6 = (bf16[160,1280]{1,0:T(8,128)(2,1)S(1)}, bf16[160,1280]{1,0:T(8,128)(2,1)S(1)}, u32[]{:S(2)}, u32[]{:S(2)}) collective-permute-start(bf16[160,1280]{1,0:T(8,128)(2,1)S(1)} %slice.25), channel_id=1, source_target_pairs={{0,16},{16,0},{1,17},{17,1},{2,18},{18,2},{3,19},{19,3},{4,20},{20... | collective-permute-start | bytes 1228808 | tf_op jit(solution)/shard_map/ppermute | solution.py:19
  40.3 13.5 %collective-permute-start.8 = (bf16[320,1280]{1,0:T(8,128)(2,1)S(1)}, bf16[320,1280]{1,0:T(8,128)(2,1)S(1)}, u32[]{:S(2)}, u32[]{:S(2)}) collective-permute-start(bf16[320,1280]{1,0:T(8,128)(2,1)S(1)} %get-tuple-element.43.refs_6_.refs_4_), channel_id=1, source_target_pairs={{0,1},{1,0},{2,3},{3,2},{4,5},{5,4},{6,7},{7,6},{8,9},{9,8},{10,11... | collective-permute-start | bytes 2457608 | tf_op jit(solution)/shard_map/ppermute | solution.py:19
  50.4 4.6 %copy-start.3 = (bf16[160,1280]{1,0:T(8,128)(2,1)}, bf16[160,1280]{1,0:T(8,128)(2,1)S(1)}, u32[]{:S(2)}) copy-start(bf16[160,1280]{1,0:T(8,128)(2,1)S(1)} %collective-permute-done.6.refs_9_.refs_7_) | copy-start | bytes 1228804
  50.5 4.5 %collective-permute-start.9 = (bf16[320,1280]{1,0:T(8,128)(2,1)S(1)}, bf16[320,1280]{1,0:T(8,128)(2,1)S(1)}, u32[]{:S(2)}, u32[]{:S(2)}) collective-permute-start(bf16[320,1280]{1,0:T(8,128)(2,1)S(1)} %pad_maximum_fusion.1), channel_id=1, source_target_pairs={{0,1},{1,0},{2,3},{3,2},{4,5},{5,4},{6,7},{7,6},{8,9},{9,8},{10,11... | collective-permute-start | bytes 2457608 | tf_op jit(solution)/shard_map/ppermute | solution.py:19
  53.0 8.2 %collective-permute-start.11 = (bf16[80,5120]{1,0:T(8,128)(2,1)S(1)}, bf16[80,5120]{1,0:T(8,128)(2,1)S(1)}, u32[]{:S(2)}, u32[]{:S(2)}) collective-permute-start(bf16[80,5120]{1,0:T(8,128)(2,1)S(1)} %bitcast.41), channel_id=1, source_target_pairs={{0,1},{1,0},{2,3},{3,2},{4,5},{5,4},{6,7},{7,6},{8,9},{9,8},{10,11... | collective-permute-start | bytes 2457608 | tf_op jit(solution)/shard_map/ppermute | solution.py:19
  53.2 11.6 %collective-permute-start.10 = (bf16[320,1280]{1,0:T(8,128)(2,1)S(1)}, bf16[320,1280]{1,0:T(8,128)(2,1)S(1)}, u32[]{:S(2)}, u32[]{:S(2)}) collective-permute-start(bf16[320,1280]{1,0:T(8,128)(2,1)S(1)} %slice.28), channel_id=1, source_target_pairs={{0,2},{1,15},{2,4},{3,1},{4,6},{5,3},{6,8},{7,5},{8,10},{9,7},{10,... | collective-permute-start | bytes 2457608 | tf_op jit(solution)/shard_map/ppermute | solution.py:201
  53.8 6.3 %copy-start.5 = (bf16[320,1280]{1,0:T(8,128)(2,1)}, bf16[320,1280]{1,0:T(8,128)(2,1)S(1)}, u32[]{:S(2)}) copy-start(bf16[320,1280]{1,0:T(8,128)(2,1)S(1)} %collective-permute-done.8.refs_7_.refs_5_) | copy-start | bytes 2457604
  55.0 5.1 %copy-start.7 = (bf16[320,1280]{1,0:T(8,128)(2,1)}, bf16[320,1280]{1,0:T(8,128)(2,1)S(1)}, u32[]{:S(2)}) copy-start(bf16[320,1280]{1,0:T(8,128)(2,1)S(1)} %collective-permute-done.9.refs_10_.refs_8_) | copy-start | bytes 2457604
  60.1 1.2 copy-start
  61.3 0.9 copy-start.13
  64.7 35.0 %all-to-all-start.1 = ((bf16[16,80,640]{2,1,0:T(8,128)(2,1)}), bf16[16,80,640]{2,1,0:T(8,128)(2,1)}, u32[]{:S(2)}, u32[]{:S(2)}) async-start(bf16[16,80,640]{2,1,0:T(8,128)(2,1)} %bitcast.37), calls=%async_computation.1 | async-start | bytes 3276800 | tf_op jit(solution)/shard_map/all_to_all | solution.py:234
  71.1 1.1 copy-start.12
  72.3 1.1 copy-start.14
  73.4 0.9 copy-start.16
  74.4 0.9 copy-start.18
  75.3 5.8 %copy-start.24 = (s32[128]{0:T(128)S(1)}, s32[128]{0:T(128)}, u32[]{:S(2)}) copy-start(s32[128]{0:T(128)} %constant.91.clone) | copy-start | bytes 1540
  75.3 5.8 %copy-start.25 = (s32[128]{0:T(128)S(1)}, s32[128]{0:T(128)}, u32[]{:S(2)}) copy-start(s32[128]{0:T(128)} %constant.92.clone) | copy-start | bytes 1540
  75.3 5.8 %copy-start.26 = (s32[128]{0:T(128)S(1)}, s32[128]{0:T(128)}, u32[]{:S(2)}) copy-start(s32[128]{0:T(128)} %constant.93.clone) | copy-start | bytes 1540
  75.3 15.3 %copy-start.2 = (bf16[160,1280]{1,0:T(8,128)(2,1)S(1)}, bf16[160,1280]{1,0:T(8,128)(2,1)}, u32[]{:S(2)}) copy-start(bf16[160,1280]{1,0:T(8,128)(2,1)} %copy-done.1) | copy-start | bytes 1228804
  75.3 15.3 %copy-start.4 = (bf16[160,1280]{1,0:T(8,128)(2,1)S(1)}, bf16[160,1280]{1,0:T(8,128)(2,1)}, u32[]{:S(2)}) copy-start(bf16[160,1280]{1,0:T(8,128)(2,1)} %copy-done.3) | copy-start | bytes 1228804
  75.3 15.3 %copy-start.6 = (bf16[320,1280]{1,0:T(8,128)(2,1)S(1)}, bf16[320,1280]{1,0:T(8,128)(2,1)}, u32[]{:S(2)}) copy-start(bf16[320,1280]{1,0:T(8,128)(2,1)} %copy-done.5) | copy-start | bytes 2457604
  75.3 15.3 %copy-start.8 = (bf16[320,1280]{1,0:T(8,128)(2,1)S(1)}, bf16[320,1280]{1,0:T(8,128)(2,1)}, u32[]{:S(2)}) copy-start(bf16[320,1280]{1,0:T(8,128)(2,1)} %copy-done.7) | copy-start | bytes 2457604
  78.1 3.9 %collective-permute-start.13 = (bf16[160,128]{1,0:T(8,128)(2,1)S(1)}, bf16[160,128]{1,0:T(8,128)(2,1)S(1)}, u32[]{:S(2)}, u32[]{:S(2)}) collective-permute-start(bf16[160,128]{1,0:T(8,128)(2,1)S(1)} %bitcast.45), channel_id=1, source_target_pairs={{0,1},{1,0},{2,3},{3,2},{4,5},{5,4},{6,7},{7,6},{8,9},{9,8},{10,11... | collective-permute-start | bytes 122888 | tf_op jit(solution)/shard_map/ppermute | solution.py:19
  81.1 9.5 %collective-permute-start.12 = (bf16[128,1280]{1,0:T(8,128)(2,1)S(1)}, bf16[128,1280]{1,0:T(8,128)(2,1)S(1)}, u32[]{:S(2)}, u32[]{:S(2)}) collective-permute-start(bf16[128,1280]{1,0:T(8,128)(2,1)S(1)} %slice.29), channel_id=1, source_target_pairs={{0,2},{1,15},{2,4},{3,1},{4,6},{5,3},{6,8},{7,5},{8,10},{9,7},{10,... | collective-permute-start | bytes 983048 | tf_op jit(solution)/shard_map/ppermute | solution.py:201
  82.1 13.0 %collective-permute-start.14 = (bf16[160,128]{1,0:T(8,128)(2,1)S(1)}, bf16[160,128]{1,0:T(8,128)(2,1)S(1)}, u32[]{:S(2)}, u32[]{:S(2)}) collective-permute-start(bf16[160,128]{1,0:T(8,128)(2,1)S(1)} %convolution_convert_fusion.1), channel_id=1, source_target_pairs={{0,8},{2,10},{4,12},{6,14},{8,0},{10,2},{12,4},{14,6},{1,9},{3,11}... | collective-permute-start | bytes 122888 | tf_op jit(solution)/shard_map/ppermute | solution.py:19
  87.5 7.6 %collective-permute-start.15 = (bf16[160,128]{1,0:T(8,128)(2,1)S(1)}, bf16[160,128]{1,0:T(8,128)(2,1)S(1)}, u32[]{:S(2)}, u32[]{:S(2)}) collective-permute-start(bf16[160,128]{1,0:T(8,128)(2,1)S(1)} %convolution_convert_fusion.1), channel_id=1, source_target_pairs={{0,16},{16,0},{1,17},{17,1},{2,18},{18,2},{3,19},{19,3},{4,20},{20... | collective-permute-start | bytes 122888 | tf_op jit(solution)/shard_map/ppermute | solution.py:19
  90.6 9.2 %collective-permute-start.16 = (bf16[160,128]{1,0:T(8,128)(2,1)S(1)}, bf16[160,128]{1,0:T(8,128)(2,1)S(1)}, u32[]{:S(2)}, u32[]{:S(2)}) collective-permute-start(bf16[160,128]{1,0:T(8,128)(2,1)S(1)} %convolution_convert_fusion.1), channel_id=1, source_target_pairs={{0,24},{2,26},{4,28},{6,30},{8,16},{10,18},{12,20},{14,22},{16,8},... | collective-permute-start | bytes 122888 | tf_op jit(solution)/shard_map/ppermute | solution.py:260
  99.7 23.1 %all-to-all-start.2 = ((bf16[16,48,640]{2,1,0:T(8,128)(2,1)}), bf16[16,48,640]{2,1,0:T(8,128)(2,1)S(1)}, u32[]{:S(2)}, u32[]{:S(2)}) async-start(bf16[16,48,640]{2,1,0:T(8,128)(2,1)} %bitcast.16), calls=%async_computation.2 | async-start | bytes 1966080 | tf_op jit(solution)/shard_map/all_to_all | solution.py:234
  104.5 5.5 %collective-permute-start.18 = (bf16[2,2,160,128]{3,2,1,0:T(8,128)(2,1)S(1)}, bf16[2,2,160,128]{3,2,1,0:T(8,128)(2,1)S(1)}, u32[]{:S(2)}, u32[]{:S(2)}) collective-permute-start(bf16[2,2,160,128]{3,2,1,0:T(8,128)(2,1)S(1)} %pad_maximum_fusion.4.near), channel_id=1, source_target_pairs={{0,2},{2,4},{4,6},{6,8},{8,10},{10,12},{12,14},{14,0},{1,3},{3,5},... | collective-permute-start | bytes 491528 | tf_op jit(solution)/shard_map/ppermute | solution.py:19
  105.6 4.5 %collective-permute-start.19 = (bf16[2,2,160,128]{3,2,1,0:T(8,128)(2,1)S(1)}, bf16[2,2,160,128]{3,2,1,0:T(8,128)(2,1)S(1)}, u32[]{:S(2)}, u32[]{:S(2)}) collective-permute-start(bf16[2,2,160,128]{3,2,1,0:T(8,128)(2,1)S(1)} %pad_maximum_fusion.4.near), channel_id=1, source_target_pairs={{0,14},{2,0},{4,2},{6,4},{8,6},{10,8},{12,10},{14,12},{1,15},{3,1}... | collective-permute-start | bytes 491528 | tf_op jit(solution)/shard_map/ppermute | solution.py:19
  107.2 11.3 %collective-permute-start.20 = (bf16[2,2,160,128]{3,2,1,0:T(8,128)(2,1)S(1)}, bf16[2,2,160,128]{3,2,1,0:T(8,128)(2,1)S(1)}, u32[]{:S(2)}, u32[]{:S(2)}) collective-permute-start(bf16[2,2,160,128]{3,2,1,0:T(8,128)(2,1)S(1)} %pad_maximum_fusion.4.near), channel_id=1, source_target_pairs={{0,4},{2,6},{4,8},{6,10},{8,12},{10,14},{12,0},{14,2},{1,5},{3,7},... | collective-permute-start | bytes 491528 | tf_op jit(solution)/shard_map/ppermute | solution.py:19
  119.1 4.0 %copy-start.19 = (s32[256]{0:T(256)S(1)}, s32[256]{0:T(256)}, u32[]{:S(2)}) copy-start(s32[256]{0:T(256)} %constant.94.clone) | copy-start | bytes 3076
  119.1 4.0 %copy-start.20 = (s32[256]{0:T(256)S(1)}, s32[256]{0:T(256)}, u32[]{:S(2)}) copy-start(s32[256]{0:T(256)} %constant.95.clone) | copy-start | bytes 3076
  119.1 4.0 %copy-start.21 = (s32[256]{0:T(256)S(1)}, s32[256]{0:T(256)}, u32[]{:S(2)}) copy-start(s32[256]{0:T(256)} %constant.96.clone) | copy-start | bytes 3076
  119.2 4.0 %copy-start.22 = (s32[256]{0:T(256)S(1)}, s32[256]{0:T(256)}, u32[]{:S(2)}) copy-start(s32[256]{0:T(256)} %constant.97.clone) | copy-start | bytes 3076
  119.2 4.0 %copy-start.23 = (s32[256]{0:T(256)S(1)}, s32[256]{0:T(256)}, u32[]{:S(2)}) copy-start(s32[256]{0:T(256)} %constant.98.clone) | copy-start | bytes 3076
  119.2 4.1 %collective-permute-start.21 = (bf16[2560,128]{1,0:T(8,128)(2,1)S(1)}, bf16[2560,128]{1,0:T(8,128)(2,1)S(1)}, u32[]{:S(2)}, u32[]{:S(2)}) collective-permute-start(bf16[2560,128]{1,0:T(8,128)(2,1)S(1)} %bitcast.43), channel_id=1, source_target_pairs={{0,1},{1,0},{2,3},{3,2},{4,5},{5,4},{6,7},{7,6},{8,9},{9,8},{10,11... | collective-permute-start | bytes 1966088 | tf_op jit(solution)/shard_map/ppermute | solution.py:19
  123.1 1.4 collective-permute-start.17
  126.8 5.4 %copy-start.27 = (s32[8]{0:T(128)S(1)}, s32[8]{0:T(128)}, u32[]{:S(2)}) copy-start(s32[8]{0:T(128)} %param.17) | copy-start | bytes 100
  126.8 26.7 %all-to-all-start.3 = ((bf16[8,40,2560]{2,1,0:T(8,128)(2,1)}), bf16[8,40,2560]{2,1,0:T(8,128)(2,1)S(1)}, u32[]{:S(2)}, u32[]{:S(2)}) async-start(bf16[8,40,2560]{2,1,0:T(8,128)(2,1)} %bitcast.25), calls=%async_computation.3 | async-start | bytes 3276800 | tf_op jit(solution)/shard_map/all_to_all | solution.py:293

commit v4 on v3

--- a/solution.py
+++ b/solution.py
@@ -35,8 +35,8 @@
 
 
 def product_kernel(spans, xh_ref, *refs):
-    out_ref, left, right, sems = refs[-4:]
-    sources, pieces = refs[: len(spans)], refs[len(spans) : -4]
+    out_ref, left, right, ready_out, sems = refs[-5:]
+    sources, pieces = refs[: len(spans)], refs[len(spans) : -5]
     copies, row = [], 0
     for k, (ref, (first, rows)) in enumerate(zip(sources, spans)):
         copies.append(
@@ -54,7 +54,7 @@
         copy.start()
     groups, cols = out_ref.shape[1], out_ref.shape[3]
     step = 16
-    waited = 0
+    waited, sent = 0, []
     for half, ready in enumerate((len(spans) + 2, len(copies))):
         for copy in copies[waited:ready]:
             copy.wait()
@@ -69,9 +69,16 @@
         for slot in range(left.shape[0] // (groups * step)):
             for group in range(groups):
                 row = (slot * groups + group) * step
-                out_ref[side, group, slot * step : (slot + 1) * step] = out[
+                ready_out[half, group, slot * step : (slot + 1) * step] = out[
                     row : row + step
                 ]
+        send = pltpu.make_async_copy(
+            ready_out.at[half], out_ref.at[side], sems.at[len(copies) + half]
+        )
+        send.start()
+        sent.append(send)
+    for send in sent:
+        send.wait()
 
 
 def product(parts, pieces, xh):
@@ -85,11 +92,12 @@
         out_shape=jax.ShapeDtypeStruct((2, 8, total // 8, cols // 2), BF16),
         in_specs=[pl.BlockSpec(memory_space=pltpu.SMEM)]
         + [pl.BlockSpec(memory_space=pl.ANY)] * (len(parts) + len(pieces)),
-        out_specs=pl.BlockSpec(memory_space=pltpu.VMEM),
+        out_specs=pl.BlockSpec(memory_space=pltpu.HBM),
         scratch_shapes=[
             pltpu.VMEM((total, depth), BF16),
             pltpu.VMEM((cols, depth), BF16),
-            pltpu.SemaphoreType.DMA((len(parts) + len(pieces),)),
+            pltpu.VMEM((2, 8, total // 8, cols // 2), BF16),
+            pltpu.SemaphoreType.DMA((len(parts) + len(pieces) + 2,)),
         ],
         compiler_params=pltpu.CompilerParams(vmem_limit_bytes=40 << 20),
         cost_estimate=pl.CostEstimate(
@@ -101,8 +109,11 @@
 
 
 def inputs_kernel(spans, core_ref, *refs):
-    own, other, out_ref, chunks, sems = refs[-5:]
-    copies = []
+    out_ref, chunks, wide_cols, sems = refs[-4:]
+    copies = [
+        pltpu.make_async_copy(ref, wide_cols.at[k], sems.at[len(spans) + k])
+        for k, ref in enumerate(refs[len(spans) : len(spans) + 2])
+    ]
     for k, (ref, (first, rows)) in enumerate(zip(refs[: len(spans)], spans)):
         source = ref.at[pl.ds(first, rows)]
         copies.append(pltpu.make_async_copy(source, chunks.at[k], sems.at[k]))
@@ -112,7 +123,7 @@
         copy.wait()
     wide = [chunks[k].astype(F32) for k in range(len(spans))]
     depth = chunks.shape[2]
-    quarters = own.shape[1] // depth
+    quarters = wide_cols.shape[2] // depth
     totals = [0.0, 0.0]
     for q in range(quarters):
         rows = [
@@ -121,9 +132,9 @@
             for first in (q * 8, (quarters + q) * 8)
         ]
         heard = jnp.concatenate(rows).astype(BF16)
-        for side, cols in enumerate((own, other)):
+        for side in range(2):
             totals[side] += lax.dot_general(
-                cols[:, q * depth : (q + 1) * depth],
+                wide_cols[side, :, q * depth : (q + 1) * depth],
                 heard,
                 (((1,), (1,)), ((), ())),
                 preferred_element_type=F32,
@@ -141,14 +152,14 @@
         lambda *refs: inputs_kernel(spans, *refs),
         out_shape=jax.ShapeDtypeStruct((2, own.shape[0], tokens), BF16),
         in_specs=[pl.BlockSpec(memory_space=pltpu.SMEM)]
-        + [pl.BlockSpec(memory_space=pl.ANY)] * len(parts)
-        + [pl.BlockSpec(memory_space=pltpu.VMEM)] * 2,
+        + [pl.BlockSpec(memory_space=pltpu.HBM)] * (len(parts) + 2),
         out_specs=pl.BlockSpec(memory_space=pltpu.VMEM),
         scratch_shapes=[
             pltpu.VMEM((len(parts), rows, depth), BF16),
-            pltpu.SemaphoreType.DMA((len(parts),)),
+            pltpu.VMEM((2,) + own.shape, BF16),
+            pltpu.SemaphoreType.DMA((len(parts) + 2,)),
         ],
-        compiler_params=pltpu.CompilerParams(vmem_limit_bytes=24 << 20),
+        compiler_params=pltpu.CompilerParams(vmem_limit_bytes=60 << 20),
         cost_estimate=pl.CostEstimate(
             flops=4 * own.size * tokens,
             bytes_accessed=4 * own.size + 2 * len(parts) * rows * depth,
@@ -219,10 +230,11 @@
     give, got[0], turned, crossed = stage(give, got[0], turned, crossed)
     block_2 = ring(jnp.concatenate([turned[:size], crossed, turned[size:]]))
     got.append(shift(give[own_out // 2 :], "xh"))
+    got_c = [shift(got[0], "core")]
     got[1], block_2 = stage(got[1], block_2)
-    got_c = shift(jnp.concatenate(got), "core")
+    got_c.append(shift(got[1], "core"))
     block_3 = ring(block_2[: 2 * size + extra])
-    pieces = (keep, keep_c, *got, got_c)
+    pieces = (keep, keep_c, *got, *got_c)
     parts = [(panel, 0), (turned, 0), (crossed, 0), (block_2, 0), (block_2, size)]
     out = product([(*p, size) for p in parts], pieces, xh)
     out, block_3, in_cols, in_other, *pieces = stage(

time: 156 us -> 153 us (0.981)
  waiting for transfers between devices: 65.5 us -> 58.9 us
  local copies, waits for them, and re-layouts: 8.64 us -> 5.38 us
  starting transfers between devices: 60.4 us -> 63.6 us
  Pallas kernels: 12.9 us -> 15.1 us
    ppermute x1, waiting for transfers between devices: 4.62 us -> 1.32 us  [shards(): lax.ppermute(r, ('xh', 'z'), [(a * 8 + b, c * 8 + d) for (a, b), (c, d) i...]
    unnamed x56 -> x60, local copies, waits for them, and re-layouts: 6.96 us -> 3.71 us
    ppermute x7, waiting for transfers between devices: 14.3 us -> 12.2 us  [shards(): ring = lambda x, way=turn: lax.ppermute(x, ('z', 'core'), way)]
    ppermute x14 -> x15, starting transfers between devices: 27.9 us -> 29.8 us  [shift(): lax.ppermute(x, axis, [(i, (i + step) % count) for i in range(count)])]
    ppermute x14 -> x15, waiting for transfers between devices: 25.3 us -> 24 us  [shift(): lax.ppermute(x, axis, [(i, (i + step) % count) for i in range(count)])]
  transfers between devices with their start and end apart: 26 -> 27, of which waited for: 14 -> 14; matrix products, arithmetic and copies ran while one was open for 3% -> 4% of each run, Pallas kernels for 8% -> 10%
where the time goes in v4:
time: 153 us; the launch traced here: 152 us
  starting transfers between devices  63.6 us (42%)
  waiting for transfers between devices  58.9 us (38%)
  Pallas kernels  15.1 us (10%)
  other arithmetic  5.52 us (4%)
  local copies, waits for them, and re-layouts  5.38 us (4%)
  matrix products  3.24 us (2%)
    ppermute x15, starting transfers between devices, shift(): lax.ppermute(x, axis, [(i, (i + step) % count) for i in range(count)])  29.8 us
    ppermute x15, waiting for transfers between devices, shift(): lax.ppermute(x, axis, [(i, (i + step) % count) for i in range(count)])  24 us
    all_to_all x1, waiting for transfers between devices, shards(): lax.all_to_all(square.reshape(groups, own_out // groups, square.shape[1])...  21.3 us
    ppermute x7, waiting for transfers between devices, shards(): ring = lambda x, way=turn: lax.ppermute(x, ('z', 'core'), way)  12.2 us
    ppermute x7, starting transfers between devices, shards(): ring = lambda x, way=turn: lax.ppermute(x, ('z', 'core'), way)  12.1 us
    all_to_all x2, starting transfers between devices, home(): return lax.all_to_all(out, ('xh', 'xl', 'y'), 0, 0)  11.7 us
    pallas_call x2, Pallas kernels, product(): pl.pallas_call(lambda *refs: product_kernel(spans, *refs), out_shape=jax....  11 us
    all_to_all x1, starting transfers between devices, shards(): lax.all_to_all(square.reshape(groups, own_out // groups, square.shape[1])...  5.18 us
  transfers between devices with their start and end apart: 27, of which 14 were waited for; matrix products, arithmetic and copies ran while one was open for 4% of the time, Pallas kernels for 10%

profile of v4, /device:TPU:1, one launch (start us, length us, event | category | flops | bytes accessed | tf_op | source)
XLA Modules:
  0.0 152.3 jit_solution(4119828541472442936)
XLA Ops:
  0.0 3.6 %collective-permute-start = (bf16[8,5120]{1,0:T(8,128)(2,1)}, bf16[8,5120]{1,0:T(8,128)(2,1)S(1)}, u32[]{:S(2)}, u32[]{:S(2)}) collective-permute-start(bf16[8,5120]{1,0:T(8,128)(2,1)} %param.13), channel_id=1, source_target_pairs={{0,16},{16,0},{1,17},{17,1},{2,18},{18,2},{3,19},{19,3},{4,20},{20... | collective-permute-start | bytes 245768 | tf_op jit(solution)/shard_map/ppermute | solution.py:19
  3.6 4.9 %all-to-all-start = ((bf16[16,8,1280]{2,1,0:T(8,128)(2,1)}), bf16[16,8,1280]{2,1,0:T(8,128)(2,1)S(1)}, u32[]{:S(2)}, u32[]{:S(2)}) async-start(bf16[16,8,1280]{2,1,0:T(8,128)(2,1)} %bitcast.46), calls=%async_computation | async-start | bytes 655360 | tf_op jit(solution)/shard_map/all_to_all | solution.py:219
  8.5 0.9 pad_maximum_fusion.2.refs_1_
  9.4 5.7 %collective-permute-start.1 = (bf16[64,1280]{1,0:T(8,128)(2,1)S(1)}, bf16[64,1280]{1,0:T(8,128)(2,1)S(1)}, u32[]{:S(2)}, u32[]{:S(2)}) collective-permute-start(bf16[64,1280]{1,0:T(8,128)(2,1)S(1)} %pad_maximum_fusion.2.refs_1_), channel_id=1, source_target_pairs={{0,2},{1,15},{2,4},{3,1},{4,6},{5,3},{6,8},{7,5},{8,10},{9,7},{10,... | collective-permute-start | bytes 491528 | tf_op jit(solution)/shard_map/ppermute | solution.py:212
  15.0 1.5 dynamic-slice_bitcast_fusion
  16.6 1.2 collective-permute-done.1.refs_2_
  17.7 2.4 %collective-permute-done.2.refs_3_ = bf16[64,1280]{1,0:T(8,128)(2,1)S(1)} collective-permute-done((bf16[64,1280]{1,0:T(8,128)(2,1)S(1)}, bf16[64,1280]{1,0:T(8,128)(2,1)S(1)}, u32[]{:S(2)}, u32[]{:S(2)}) %collective-permute-start.2) | collective-permute-done | bytes 163872 | tf_op jit(solution)/shard_map/ppermute | solution.py:212
  20.1 2.5 %collective-permute-start.4 = (bf16[256,1280]{1,0:T(8,128)(2,1)S(1)}, bf16[256,1280]{1,0:T(8,128)(2,1)S(1)}, u32[]{:S(2)}, u32[]{:S(2)}) collective-permute-start(bf16[256,1280]{1,0:T(8,128)(2,1)S(1)} %pad_maximum_fusion.1), channel_id=1, source_target_pairs={{0,2},{1,15},{2,4},{3,1},{4,6},{5,3},{6,8},{7,5},{8,10},{9,7},{10,... | collective-permute-start | bytes 1966088 | tf_op jit(solution)/shard_map/ppermute | solution.py:212
  22.6 2.6 %collective-permute-start.3 = (bf16[160,1280]{1,0:T(8,128)(2,1)S(1)}, bf16[160,1280]{1,0:T(8,128)(2,1)S(1)}, u32[]{:S(2)}, u32[]{:S(2)}) collective-permute-start(bf16[160,1280]{1,0:T(8,128)(2,1)S(1)} %slice.24), channel_id=1, source_target_pairs={{0,16},{16,0},{1,17},{17,1},{2,18},{18,2},{3,19},{19,3},{4,20},{20... | collective-permute-start | bytes 1228808 | tf_op jit(solution)/shard_map/ppermute | solution.py:19
  25.3 8.2 %collective-permute-done.5.refs_3_ = bf16[128,1280]{1,0:T(8,128)(2,1)S(1)} collective-permute-done((bf16[128,1280]{1,0:T(8,128)(2,1)S(1)}, bf16[128,1280]{1,0:T(8,128)(2,1)S(1)}, u32[]{:S(2)}, u32[]{:S(2)}) %collective-permute-start.5) | collective-permute-done | bytes 327712 | tf_op jit(solution)/shard_map/ppermute | solution.py:212
  33.5 0.9 collective-permute-done.3.refs_8_.refs_6_
  34.4 0.1 pad_maximum_fusion
  34.5 2.5 %collective-permute-start.7 = (bf16[384,1280]{1,0:T(8,128)(2,1)S(1)}, bf16[384,1280]{1,0:T(8,128)(2,1)S(1)}, u32[]{:S(2)}, u32[]{:S(2)}) collective-permute-start(bf16[384,1280]{1,0:T(8,128)(2,1)S(1)} %pad_maximum_fusion), channel_id=1, source_target_pairs={{0,2},{1,15},{2,4},{3,1},{4,6},{5,3},{6,8},{7,5},{8,10},{9,7},{10,... | collective-permute-start | bytes 2949128 | tf_op jit(solution)/shard_map/ppermute | solution.py:212
  37.0 2.6 %collective-permute-start.6 = (bf16[160,1280]{1,0:T(8,128)(2,1)S(1)}, bf16[160,1280]{1,0:T(8,128)(2,1)S(1)}, u32[]{:S(2)}, u32[]{:S(2)}) collective-permute-start(bf16[160,1280]{1,0:T(8,128)(2,1)S(1)} %slice.25), channel_id=1, source_target_pairs={{0,16},{16,0},{1,17},{17,1},{2,18},{18,2},{3,19},{19,3},{4,20},{20... | collective-permute-start | bytes 1228808 | tf_op jit(solution)/shard_map/ppermute | solution.py:19
  39.7 0.2 collective-permute-start.8
  39.8 0.3 collective-permute-start.12
  40.2 9.6 %collective-permute-done.6.refs_9_.refs_7_ = bf16[160,1280]{1,0:T(8,128)(2,1)S(1)} collective-permute-done((bf16[160,1280]{1,0:T(8,128)(2,1)S(1)}, bf16[160,1280]{1,0:T(8,128)(2,1)S(1)}, u32[]{:S(2)}, u32[]{:S(2)}) %collective-permute-start.6) | collective-permute-done | bytes 409632 | tf_op jit(solution)/shard_map/ppermute | solution.py:19
  49.8 0.1 slice.28
  49.8 1.5 collective-permute-start.11
  51.3 1.2 collective-permute-start.9
  52.5 0.1 collective-permute-start.10
  52.6 1.3 collective-permute-done.9.refs_10_.refs_8_
  53.9 0.6 collective-permute-done.10.refs_11_.refs_9_
  54.4 6.3 %shard_map.127 = bf16[2,8,80,640]{3,2,1,0:T(8,128)(2,1)} custom-call(s32[1]{0:T(128)} %bitcast.refs_0_, bf16[128,1280]{1,0:T(8,128)(2,1)S(1)} %bitcast.39, bf16[256,1280]{1,0:T(8,128)(2,1)S(1)} %collective-permute-done.4.refs_2_.refs_4_.refs_5_, bf16[128,1280]{1,0:T(8,128)(2,1)S(1)} %collective-permute-done.5.refs_3_, ...), custom_call_target="tpu_custom_call" | custom-call | flops 2097152000 | bytes 6553600 | tf_op jit(solution)/shard_map/pallas_call | solution.py:90
  60.8 0.5 collective-permute-done.11.refs_1_.refs_2_.refs_8_
  61.4 0.4 copy-done.11
  61.8 6.3 %all-to-all-start.1 = ((bf16[16,80,640]{2,1,0:T(8,128)(2,1)}), bf16[16,80,640]{2,1,0:T(8,128)(2,1)}, u32[]{:S(2)}, u32[]{:S(2)}) async-start(bf16[16,80,640]{2,1,0:T(8,128)(2,1)} %bitcast.13), calls=%async_computation.1 | async-start | bytes 3276800 | tf_op jit(solution)/shard_map/all_to_all | solution.py:246
  68.2 0.0 copy-start.26
  68.2 0.0 copy-start.28
  68.2 3.5 %shard_map.129 = bf16[2,80,128]{2,1,0:T(8,128)(2,1)} custom-call(s32[1]{0:T(128)} %bitcast.14.refs_0_, bf16[64,1280]{1,0:T(8,128)(2,1)} %copy-done.14, bf16[64,1280]{1,0:T(8,128)(2,1)} %copy-done.12, bf16[64,1280]{1,0:T(8,128)(2,1)} %copy-done.13, bf16[256,1280]{1,0:T(8,128)(2,1)} %copy-done.1, bf16[256,1280]{1,0:T(8,128)(2,1)} %copy-done.1, ...), custom_call_target="tpu_custom_call" | custom-call | flops 209715200 | bytes 2949120 | tf_op jit(solution)/shard_map/pallas_call | solution.py:151
  71.8 4.7 %collective-permute-start.14 = (bf16[160,128]{1,0:T(8,128)(2,1)}, bf16[160,128]{1,0:T(8,128)(2,1)S(1)}, u32[]{:S(2)}, u32[]{:S(2)}) collective-permute-start(bf16[160,128]{1,0:T(8,128)(2,1)} %bitcast.49), channel_id=1, source_target_pairs={{0,1},{1,0},{2,3},{3,2},{4,5},{5,4},{6,7},{7,6},{8,9},{9,8},{10,11... | collective-permute-start | bytes 122888 | tf_op jit(solution)/shard_map/ppermute | solution.py:19
  76.6 1.0 collective-permute-done.14
  77.6 0.9 convolution_convert_fusion.1
  78.5 5.3 %collective-permute-start.15 = (bf16[160,128]{1,0:T(8,128)(2,1)S(1)}, bf16[160,128]{1,0:T(8,128)(2,1)S(1)}, u32[]{:S(2)}, u32[]{:S(2)}) collective-permute-start(bf16[160,128]{1,0:T(8,128)(2,1)S(1)} %convolution_convert_fusion.1), channel_id=1, source_target_pairs={{0,8},{2,10},{4,12},{6,14},{8,0},{10,2},{12,4},{14,6},{1,9},{3,11}... | collective-permute-start | bytes 122888 | tf_op jit(solution)/shard_map/ppermute | solution.py:19
  83.9 3.1 %collective-permute-start.16 = (bf16[160,128]{1,0:T(8,128)(2,1)S(1)}, bf16[160,128]{1,0:T(8,128)(2,1)S(1)}, u32[]{:S(2)}, u32[]{:S(2)}) collective-permute-start(bf16[160,128]{1,0:T(8,128)(2,1)S(1)} %convolution_convert_fusion.1), channel_id=1, source_target_pairs={{0,16},{16,0},{1,17},{17,1},{2,18},{18,2},{3,19},{19,3},{4,20},{20... | collective-permute-start | bytes 122888 | tf_op jit(solution)/shard_map/ppermute | solution.py:19
  87.0 1.0 copy-done.7
  88.0 1.0 copy-done.9
  89.0 4.6 %shard_map.128 = bf16[2,8,48,640]{3,2,1,0:T(8,128)(2,1)} custom-call(s32[1]{0:T(128)} %bitcast.refs_0_, bf16[320,1280]{1,0:T(8,128)(2,1)S(1)} %copy-done.3, bf16[320,1280]{1,0:T(8,128)(2,1)S(1)} %copy-done.3, bf16[128,1280]{1,0:T(8,128)(2,1)S(1)} %collective-permute-done.13.refs_3_, bf16[320,1280]{1,0:T(8,128)(2,1)S(1)} %get-tuple-element.44.refs_6_.refs_4_, ...), custom_call_target="tpu_custom_call" | custom-call | flops 1258291200 | bytes 5242880 | tf_op jit(solution)/shard_map/pallas_call | solution.py:90
  93.7 0.6 copy-done.17
  94.3 0.6 copy-done.19
  94.9 1.3 collective-permute-done.17
  96.2 5.4 %all-to-all-start.2 = ((bf16[16,48,640]{2,1,0:T(8,128)(2,1)}), bf16[16,48,640]{2,1,0:T(8,128)(2,1)S(1)}, u32[]{:S(2)}, u32[]{:S(2)}) async-start(bf16[16,48,640]{2,1,0:T(8,128)(2,1)} %bitcast.16), calls=%async_computation.2 | async-start | bytes 1966080 | tf_op jit(solution)/shard_map/all_to_all | solution.py:246
  101.7 0.8 maximum_bitcast_fusion
  102.5 0.5 collective-permute-start.19
  103.0 2.2 %collective-permute-start.20 = (bf16[2,2,160,128]{3,2,1,0:T(8,128)(2,1)S(1)}, bf16[2,2,160,128]{3,2,1,0:T(8,128)(2,1)S(1)}, u32[]{:S(2)}, u32[]{:S(2)}) collective-permute-start(bf16[2,2,160,128]{3,2,1,0:T(8,128)(2,1)S(1)} %pad_maximum_fusion.3.near), channel_id=1, source_target_pairs={{0,14},{2,0},{4,2},{6,4},{8,6},{10,8},{12,10},{14,12},{1,15},{3,1}... | collective-permute-start | bytes 491528 | tf_op jit(solution)/shard_map/ppermute | solution.py:19
  105.3 0.1 pad_add_fusion.place_ref
  105.3 2.9 %collective-permute-done.19.below = bf16[2,2,160,128]{3,2,1,0:T(8,128)(2,1)S(1)} collective-permute-done((bf16[2,2,160,128]{3,2,1,0:T(8,128)(2,1)S(1)}, bf16[2,2,160,128]{3,2,1,0:T(8,128)(2,1)S(1)}, u32[]{:S(2)}, u32[]{:S(2)}) %collective-permute-start.19) | collective-permute-done | bytes 163872 | tf_op jit(solution)/shard_map/ppermute | solution.py:19
  108.3 6.5 %collective-permute-done.21.two = bf16[2,2,160,128]{3,2,1,0:T(8,128)(2,1)S(1)} collective-permute-done((bf16[2,2,160,128]{3,2,1,0:T(8,128)(2,1)S(1)}, bf16[2,2,160,128]{3,2,1,0:T(8,128)(2,1)S(1)}, u32[]{:S(2)}, u32[]{:S(2)}) %collective-permute-start.21) | collective-permute-done | bytes 163872 | tf_op jit(solution)/shard_map/ppermute | solution.py:19
  114.8 0.6 shard_map.130
  115.4 0.0 copy-start.22
  115.4 0.0 copy-start.23
  115.4 0.0 copy-start.24
  115.4 0.0 copy-start.25
  115.4 3.1 %collective-permute-start.22 = (bf16[2560,128]{1,0:T(8,128)(2,1)S(1)}, bf16[2560,128]{1,0:T(8,128)(2,1)S(1)}, u32[]{:S(2)}, u32[]{:S(2)}) collective-permute-start(bf16[2560,128]{1,0:T(8,128)(2,1)S(1)} %bitcast.40), channel_id=1, source_target_pairs={{0,1},{1,0},{2,3},{3,2},{4,5},{5,4},{6,7},{7,6},{8,9},{9,8},{10,11... | collective-permute-start | bytes 1966088 | tf_op jit(solution)/shard_map/ppermute | solution.py:19
  118.5 1.7 %reduce_sum.52 = bf16[80,640]{1,0:T(8,128)(2,1)S(1)} reduce(bf16[16,80,640]{2,1,0:T(8,128)(2,1)} %all-to-all-done.1, bf16[]{:T(256)} %constant.88.clone.1), dimensions={0}, to_apply=%region_0.1 | reduce | flops 768000 | bytes 1740802 | tf_op jit(solution)/shard_map/reduce_sum | solution.py:297
  120.2 0.1 reduce_sum.53
  120.3 0.1 fusion.15
  120.4 0.1 collective-permute-start.18
  120.6 1.2 collective-permute-done.18
  121.8 2.3 %fusion = bf16[320,2560]{1,0:T(8,128)(2,1)} fusion(bf16[2560,128]{1,0:T(8,128)(2,1)S(1)} %collective-permute-done.22, bf16[2560,128]{1,0:T(8,128)(2,1)S(1)} %bitcast.41, bf16[128,320]{1,0:T(8,128)(2,1)S(1)} %collective-permute-done.18, bf16[128,320]{1,0:T(8,128)(2,1)S(1)} %get-tuple-element.65, s32[256]{0:T(256)S(1)} %fusion.26), kind=kOutput, calls=%fused_computation.3 | convolution fusion | flops 760283136 | bytes 3113984 | tf_op jit(solution)/shard_map/dot_general | solution.py:301
  124.1 5.2 %all-to-all-start.3 = ((bf16[8,40,2560]{2,1,0:T(8,128)(2,1)}), bf16[8,40,2560]{2,1,0:T(8,128)(2,1)S(1)}, u32[]{:S(2)}, u32[]{:S(2)}) async-start(bf16[8,40,2560]{2,1,0:T(8,128)(2,1)} %bitcast.25), calls=%async_computation.3 | async-start | bytes 3276800 | tf_op jit(solution)/shard_map/all_to_all | solution.py:305
  129.3 21.3 %all-to-all-done.3 = bf16[8,40,2560]{2,1,0:T(8,128)(2,1)S(1)} async-done(((bf16[8,40,2560]{2,1,0:T(8,128)(2,1)}), bf16[8,40,2560]{2,1,0:T(8,128)(2,1)S(1)}, u32[]{:S(2)}, u32[]{:S(2)}) %all-to-all-start.3) | async-done | bytes 1638432 | tf_op jit(solution)/shard_map/all_to_all | solution.py:305
  150.6 0.6 fusion.1
  151.3 1.0 fusion.9
  (77 shorter events, 0.4 us)
Async XLA Ops:
  0.0 8.5 %collective-permute-start = (bf16[8,5120]{1,0:T(8,128)(2,1)}, bf16[8,5120]{1,0:T(8,128)(2,1)S(1)}, u32[]{:S(2)}, u32[]{:S(2)}) collective-permute-start(bf16[8,5120]{1,0:T(8,128)(2,1)} %param.13), channel_id=1, source_target_pairs={{0,16},{16,0},{1,17},{17,1},{2,18},{18,2},{3,19},{19,3},{4,20},{20... | collective-permute-start | bytes 245768 | tf_op jit(solution)/shard_map/ppermute | solution.py:19
  3.6 16.5 %all-to-all-start = ((bf16[16,8,1280]{2,1,0:T(8,128)(2,1)}), bf16[16,8,1280]{2,1,0:T(8,128)(2,1)S(1)}, u32[]{:S(2)}, u32[]{:S(2)}) async-start(bf16[16,8,1280]{2,1,0:T(8,128)(2,1)} %bitcast.46), calls=%async_computation | async-start | bytes 655360 | tf_op jit(solution)/shard_map/all_to_all | solution.py:219
  9.4 7.2 %copy-start.14 = (bf16[64,1280]{1,0:T(8,128)(2,1)}, bf16[64,1280]{1,0:T(8,128)(2,1)S(1)}, u32[]{:S(2)}) copy-start(bf16[64,1280]{1,0:T(8,128)(2,1)S(1)} %pad_maximum_fusion.2.refs_1_) | copy-start | bytes 491524
  9.4 8.3 %collective-permute-start.1 = (bf16[64,1280]{1,0:T(8,128)(2,1)S(1)}, bf16[64,1280]{1,0:T(8,128)(2,1)S(1)}, u32[]{:S(2)}, u32[]{:S(2)}) collective-permute-start(bf16[64,1280]{1,0:T(8,128)(2,1)S(1)} %pad_maximum_fusion.2.refs_1_), channel_id=1, source_target_pairs={{0,2},{1,15},{2,4},{3,1},{4,6},{5,3},{6,8},{7,5},{8,10},{9,7},{10,... | collective-permute-start | bytes 491528 | tf_op jit(solution)/shard_map/ppermute | solution.py:212
  15.0 5.0 %collective-permute-start.2 = (bf16[64,1280]{1,0:T(8,128)(2,1)S(1)}, bf16[64,1280]{1,0:T(8,128)(2,1)S(1)}, u32[]{:S(2)}, u32[]{:S(2)}) collective-permute-start(bf16[64,1280]{1,0:T(8,128)(2,1)S(1)} %pad_maximum_fusion.2.refs_1_), channel_id=1, source_target_pairs={{0,15},{1,2},{2,1},{3,4},{4,3},{5,6},{6,5},{7,8},{8,7},{9,10},{10,... | collective-permute-start | bytes 491528 | tf_op jit(solution)/shard_map/ppermute | solution.py:212
  17.7 16.7 %copy-start.12 = (bf16[64,1280]{1,0:T(8,128)(2,1)}, bf16[64,1280]{1,0:T(8,128)(2,1)S(1)}, u32[]{:S(2)}) copy-start(bf16[64,1280]{1,0:T(8,128)(2,1)S(1)} %collective-permute-done.1.refs_2_) | copy-start | bytes 491524
  20.1 14.3 %copy-start.13 = (bf16[64,1280]{1,0:T(8,128)(2,1)}, bf16[64,1280]{1,0:T(8,128)(2,1)S(1)}, u32[]{:S(2)}) copy-start(bf16[64,1280]{1,0:T(8,128)(2,1)S(1)} %collective-permute-done.2.refs_3_) | copy-start | bytes 491524
  20.1 14.2 %collective-permute-start.4 = (bf16[256,1280]{1,0:T(8,128)(2,1)S(1)}, bf16[256,1280]{1,0:T(8,128)(2,1)S(1)}, u32[]{:S(2)}, u32[]{:S(2)}) collective-permute-start(bf16[256,1280]{1,0:T(8,128)(2,1)S(1)} %pad_maximum_fusion.1), channel_id=1, source_target_pairs={{0,2},{1,15},{2,4},{3,1},{4,6},{5,3},{6,8},{7,5},{8,10},{9,7},{10,... | collective-permute-start | bytes 1966088 | tf_op jit(solution)/shard_map/ppermute | solution.py:212
  22.6 11.7 %collective-permute-start.3 = (bf16[160,1280]{1,0:T(8,128)(2,1)S(1)}, bf16[160,1280]{1,0:T(8,128)(2,1)S(1)}, u32[]{:S(2)}, u32[]{:S(2)}) collective-permute-start(bf16[160,1280]{1,0:T(8,128)(2,1)S(1)} %slice.24), channel_id=1, source_target_pairs={{0,16},{16,0},{1,17},{17,1},{2,18},{18,2},{3,19},{19,3},{4,20},{20... | collective-permute-start | bytes 1228808 | tf_op jit(solution)/shard_map/ppermute | solution.py:19
  25.3 8.2 %collective-permute-start.5 = (bf16[128,1280]{1,0:T(8,128)(2,1)S(1)}, bf16[128,1280]{1,0:T(8,128)(2,1)S(1)}, u32[]{:S(2)}, u32[]{:S(2)}) collective-permute-start(bf16[128,1280]{1,0:T(8,128)(2,1)S(1)} %bitcast.38), channel_id=1, source_target_pairs={{0,15},{1,2},{2,1},{3,4},{4,3},{5,6},{6,5},{7,8},{8,7},{9,10},{10,... | collective-permute-start | bytes 983048 | tf_op jit(solution)/shard_map/ppermute | solution.py:212
  34.4 20.1 %copy-start.1 = (bf16[256,1280]{1,0:T(8,128)(2,1)}, bf16[256,1280]{1,0:T(8,128)(2,1)S(1)}, u32[]{:S(2)}) copy-start(bf16[256,1280]{1,0:T(8,128)(2,1)S(1)} %collective-permute-done.4.refs_2_.refs_4_.refs_5_) | copy-start | bytes 1966084
  34.4 5.4 %copy-start.10 = (bf16[5120,80]{0,1:T(8,128)(2,1)S(1)}, bf16[5120,80]{0,1:T(8,128)(2,1)}, u32[]{:S(2)}) copy-start(bf16[5120,80]{0,1:T(8,128)(2,1)} %param.15) | copy-start | bytes 2457604
  34.5 15.2 %collective-permute-start.7 = (bf16[384,1280]{1,0:T(8,128)(2,1)S(1)}, bf16[384,1280]{1,0:T(8,128)(2,1)S(1)}, u32[]{:S(2)}, u32[]{:S(2)}) collective-permute-start(bf16[384,1280]{1,0:T(8,128)(2,1)S(1)} %pad_maximum_fusion), channel_id=1, source_target_pairs={{0,2},{1,15},{2,4},{3,1},{4,6},{5,3},{6,8},{7,5},{8,10},{9,7},{10,... | collective-permute-start | bytes 2949128 | tf_op jit(solution)/shard_map/ppermute | solution.py:212
  37.0 12.7 %collective-permute-start.6 = (bf16[160,1280]{1,0:T(8,128)(2,1)S(1)}, bf16[160,1280]{1,0:T(8,128)(2,1)S(1)}, u32[]{:S(2)}, u32[]{:S(2)}) collective-permute-start(bf16[160,1280]{1,0:T(8,128)(2,1)S(1)} %slice.25), channel_id=1, source_target_pairs={{0,16},{16,0},{1,17},{17,1},{2,18},{18,2},{3,19},{19,3},{4,20},{20... | collective-permute-start | bytes 1228808 | tf_op jit(solution)/shard_map/ppermute | solution.py:19
  39.7 12.9 %collective-permute-start.8 = (bf16[320,1280]{1,0:T(8,128)(2,1)S(1)}, bf16[320,1280]{1,0:T(8,128)(2,1)S(1)}, u32[]{:S(2)}, u32[]{:S(2)}) collective-permute-start(bf16[320,1280]{1,0:T(8,128)(2,1)S(1)} %get-tuple-element.44.refs_6_.refs_4_), channel_id=1, source_target_pairs={{0,1},{1,0},{2,3},{3,2},{4,5},{5,4},{6,7},{7,6},{8,9},{9,8},{10,11... | collective-permute-start | bytes 2457608 | tf_op jit(solution)/shard_map/ppermute | solution.py:19
  39.8 21.0 %collective-permute-start.12 = (bf16[80,5120]{1,0:T(8,128)(2,1)S(1)}, bf16[80,5120]{1,0:T(8,128)(2,1)S(1)}, u32[]{:S(2)}, u32[]{:S(2)}) collective-permute-start(bf16[80,5120]{1,0:T(8,128)(2,1)S(1)} %bitcast.45), channel_id=1, source_target_pairs={{0,1},{1,0},{2,3},{3,2},{4,5},{5,4},{6,7},{7,6},{8,9},{9,8},{10,11... | collective-permute-start | bytes 2457608 | tf_op jit(solution)/shard_map/ppermute | solution.py:19
  49.8 11.0 %copy-start.4 = (bf16[160,1280]{1,0:T(8,128)(2,1)}, bf16[160,1280]{1,0:T(8,128)(2,1)S(1)}, u32[]{:S(2)}) copy-start(bf16[160,1280]{1,0:T(8,128)(2,1)S(1)} %collective-permute-done.6.refs_9_.refs_7_) | copy-start | bytes 1228804
  49.8 11.0 %copy-start = (bf16[384,1280]{1,0:T(8,128)(2,1)}, bf16[384,1280]{1,0:T(8,128)(2,1)S(1)}, u32[]{:S(2)}) copy-start(bf16[384,1280]{1,0:T(8,128)(2,1)S(1)} %collective-permute-done.7.refs_4_.refs_5_.refs_6_.refs_7_) | copy-start | bytes 2949124
  49.8 11.6 %collective-permute-start.11 = (bf16[320,1280]{1,0:T(8,128)(2,1)S(1)}, bf16[320,1280]{1,0:T(8,128)(2,1)S(1)}, u32[]{:S(2)}, u32[]{:S(2)}) collective-permute-start(bf16[320,1280]{1,0:T(8,128)(2,1)S(1)} %slice.28), channel_id=1, source_target_pairs={{0,2},{1,15},{2,4},{3,1},{4,6},{5,3},{6,8},{7,5},{8,10},{9,7},{10,... | collective-permute-start | bytes 2457608 | tf_op jit(solution)/shard_map/ppermute | solution.py:212
  51.3 2.6 %collective-permute-start.9 = (bf16[160,1280]{1,0:T(8,128)(2,1)S(1)}, bf16[160,1280]{1,0:T(8,128)(2,1)S(1)}, u32[]{:S(2)}, u32[]{:S(2)}) collective-permute-start(bf16[160,1280]{1,0:T(8,128)(2,1)S(1)} %collective-permute-done.3.refs_8_.refs_6_), channel_id=1, source_target_pairs={{0,1},{1,0},{2,3},{3,2},{4,5},{5,4},{6,7},{7,6},{8,9},{9,8},{10,11... | collective-permute-start | bytes 1228808 | tf_op jit(solution)/shard_map/ppermute | solution.py:19
  52.5 2.0 %collective-permute-start.10 = (bf16[160,1280]{1,0:T(8,128)(2,1)S(1)}, bf16[160,1280]{1,0:T(8,128)(2,1)S(1)}, u32[]{:S(2)}, u32[]{:S(2)}) collective-permute-start(bf16[160,1280]{1,0:T(8,128)(2,1)S(1)} %collective-permute-done.6.refs_9_.refs_7_), channel_id=1, source_target_pairs={{0,1},{1,0},{2,3},{3,2},{4,5},{5,4},{6,7},{7,6},{8,9},{9,8},{10,11... | collective-permute-start | bytes 1228808 | tf_op jit(solution)/shard_map/ppermute | solution.py:19
  53.9 7.0 %copy-start.6 = (bf16[160,1280]{1,0:T(8,128)(2,1)}, bf16[160,1280]{1,0:T(8,128)(2,1)S(1)}, u32[]{:S(2)}) copy-start(bf16[160,1280]{1,0:T(8,128)(2,1)S(1)} %collective-permute-done.9.refs_10_.refs_8_) | copy-start | bytes 1228804
  54.4 6.4 %copy-start.8 = (bf16[160,1280]{1,0:T(8,128)(2,1)}, bf16[160,1280]{1,0:T(8,128)(2,1)S(1)}, u32[]{:S(2)}) copy-start(bf16[160,1280]{1,0:T(8,128)(2,1)S(1)} %collective-permute-done.10.refs_11_.refs_9_) | copy-start | bytes 1228804
  60.8 0.9 copy-start.11
  61.8 6.4 %copy-start.2 = (bf16[320,1280]{1,0:T(8,128)(2,1)}, bf16[320,1280]{1,0:T(8,128)(2,1)S(1)}, u32[]{:S(2)}) copy-start(bf16[320,1280]{1,0:T(8,128)(2,1)S(1)} %collective-permute-done.11.refs_1_.refs_2_.refs_8_) | copy-start | bytes 2457604
  61.8 34.5 %all-to-all-start.1 = ((bf16[16,80,640]{2,1,0:T(8,128)(2,1)}), bf16[16,80,640]{2,1,0:T(8,128)(2,1)}, u32[]{:S(2)}, u32[]{:S(2)}) async-start(bf16[16,80,640]{2,1,0:T(8,128)(2,1)} %bitcast.13), calls=%async_computation.1 | async-start | bytes 3276800 | tf_op jit(solution)/shard_map/all_to_all | solution.py:246
  68.2 8.4 %copy-start.26 = (s32[128]{0:T(128)S(1)}, s32[128]{0:T(128)}, u32[]{:S(2)}) copy-start(s32[128]{0:T(128)} %constant.91.clone) | copy-start | bytes 1540
  68.2 8.3 %copy-start.27 = (s32[128]{0:T(128)S(1)}, s32[128]{0:T(128)}, u32[]{:S(2)}) copy-start(s32[128]{0:T(128)} %constant.92.clone) | copy-start | bytes 1540
  68.2 8.3 %copy-start.28 = (s32[128]{0:T(128)S(1)}, s32[128]{0:T(128)}, u32[]{:S(2)}) copy-start(s32[128]{0:T(128)} %constant.93.clone) | copy-start | bytes 1540
  68.2 18.8 %copy-start.3 = (bf16[320,1280]{1,0:T(8,128)(2,1)S(1)}, bf16[320,1280]{1,0:T(8,128)(2,1)}, u32[]{:S(2)}) copy-start(bf16[320,1280]{1,0:T(8,128)(2,1)} %copy-done.2) | copy-start | bytes 2457604
  68.2 18.8 %copy-start.5 = (bf16[160,1280]{1,0:T(8,128)(2,1)S(1)}, bf16[160,1280]{1,0:T(8,128)(2,1)}, u32[]{:S(2)}) copy-start(bf16[160,1280]{1,0:T(8,128)(2,1)} %copy-done.4) | copy-start | bytes 1228804
  71.8 5.8 %collective-permute-start.14 = (bf16[160,128]{1,0:T(8,128)(2,1)}, bf16[160,128]{1,0:T(8,128)(2,1)S(1)}, u32[]{:S(2)}, u32[]{:S(2)}) collective-permute-start(bf16[160,128]{1,0:T(8,128)(2,1)} %bitcast.49), channel_id=1, source_target_pairs={{0,1},{1,0},{2,3},{3,2},{4,5},{5,4},{6,7},{7,6},{8,9},{9,8},{10,11... | collective-permute-start | bytes 122888 | tf_op jit(solution)/shard_map/ppermute | solution.py:19
  76.5 10.5 %collective-permute-start.13 = (bf16[128,1280]{1,0:T(8,128)(2,1)S(1)}, bf16[128,1280]{1,0:T(8,128)(2,1)S(1)}, u32[]{:S(2)}, u32[]{:S(2)}) collective-permute-start(bf16[128,1280]{1,0:T(8,128)(2,1)S(1)} %slice.29), channel_id=1, source_target_pairs={{0,2},{1,15},{2,4},{3,1},{4,6},{5,3},{6,8},{7,5},{8,10},{9,7},{10,... | collective-permute-start | bytes 983048 | tf_op jit(solution)/shard_map/ppermute | solution.py:212
  78.5 15.1 %copy-start.15 = (bf16[160,128]{1,0:T(8,128)(2,1)}, bf16[160,128]{1,0:T(8,128)(2,1)S(1)}, u32[]{:S(2)}) copy-start(bf16[160,128]{1,0:T(8,128)(2,1)S(1)} %convolution_convert_fusion.1) | copy-start | bytes 122884
  78.5 15.1 %collective-permute-start.15 = (bf16[160,128]{1,0:T(8,128)(2,1)S(1)}, bf16[160,128]{1,0:T(8,128)(2,1)S(1)}, u32[]{:S(2)}, u32[]{:S(2)}) collective-permute-start(bf16[160,128]{1,0:T(8,128)(2,1)S(1)} %convolution_convert_fusion.1), channel_id=1, source_target_pairs={{0,8},{2,10},{4,12},{6,14},{8,0},{10,2},{12,4},{14,6},{1,9},{3,11}... | collective-permute-start | bytes 122888 | tf_op jit(solution)/shard_map/ppermute | solution.py:19
  83.9 9.8 %collective-permute-start.16 = (bf16[160,128]{1,0:T(8,128)(2,1)S(1)}, bf16[160,128]{1,0:T(8,128)(2,1)S(1)}, u32[]{:S(2)}, u32[]{:S(2)}) collective-permute-start(bf16[160,128]{1,0:T(8,128)(2,1)S(1)} %convolution_convert_fusion.1), channel_id=1, source_target_pairs={{0,16},{16,0},{1,17},{17,1},{2,18},{18,2},{3,19},{19,3},{4,20},{20... | collective-permute-start | bytes 122888 | tf_op jit(solution)/shard_map/ppermute | solution.py:19
  87.0 9.3 %collective-permute-start.17 = (bf16[160,128]{1,0:T(8,128)(2,1)S(1)}, bf16[160,128]{1,0:T(8,128)(2,1)}, u32[]{:S(2)}, u32[]{:S(2)}) collective-permute-start(bf16[160,128]{1,0:T(8,128)(2,1)S(1)} %convolution_convert_fusion.1), channel_id=1, source_target_pairs={{0,24},{2,26},{4,28},{6,30},{8,16},{10,18},{12,20},{14,22},{16,8},... | collective-permute-start | bytes 122888 | tf_op jit(solution)/shard_map/ppermute | solution.py:272
  87.0 1.0 copy-start.7
  88.0 1.0 copy-start.9
  93.7 0.6 copy-start.17
  93.7 8.0 %copy-start.16 = (bf16[160,128]{1,0:T(8,128)(2,1)S(1)}, bf16[160,128]{1,0:T(8,128)(2,1)}, u32[]{:S(2)}) copy-start(bf16[160,128]{1,0:T(8,128)(2,1)} %copy-done.15) | copy-start | bytes 122884
  94.3 0.6 copy-start.19
  96.2 5.4 %copy-start.18 = (bf16[160,128]{1,0:T(8,128)(2,1)S(1)}, bf16[160,128]{1,0:T(8,128)(2,1)}, u32[]{:S(2)}) copy-start(bf16[160,128]{1,0:T(8,128)(2,1)} %copy-done.17) | copy-start | bytes 122884
  96.2 5.4 %copy-start.20 = (bf16[160,128]{1,0:T(8,128)(2,1)S(1)}, bf16[160,128]{1,0:T(8,128)(2,1)}, u32[]{:S(2)}) copy-start(bf16[160,128]{1,0:T(8,128)(2,1)} %copy-done.19) | copy-start | bytes 122884
  96.2 23.9 %all-to-all-start.2 = ((bf16[16,48,640]{2,1,0:T(8,128)(2,1)}), bf16[16,48,640]{2,1,0:T(8,128)(2,1)S(1)}, u32[]{:S(2)}, u32[]{:S(2)}) async-start(bf16[16,48,640]{2,1,0:T(8,128)(2,1)} %bitcast.16), calls=%async_computation.2 | async-start | bytes 1966080 | tf_op jit(solution)/shard_map/all_to_all | solution.py:246
  102.5 5.8 %collective-permute-start.19 = (bf16[2,2,160,128]{3,2,1,0:T(8,128)(2,1)S(1)}, bf16[2,2,160,128]{3,2,1,0:T(8,128)(2,1)S(1)}, u32[]{:S(2)}, u32[]{:S(2)}) collective-permute-start(bf16[2,2,160,128]{3,2,1,0:T(8,128)(2,1)S(1)} %pad_maximum_fusion.3.near), channel_id=1, source_target_pairs={{0,2},{2,4},{4,6},{6,8},{8,10},{10,12},{12,14},{14,0},{1,3},{3,5},... | collective-permute-start | bytes 491528 | tf_op jit(solution)/shard_map/ppermute | solution.py:19
  103.0 5.2 %collective-permute-start.20 = (bf16[2,2,160,128]{3,2,1,0:T(8,128)(2,1)S(1)}, bf16[2,2,160,128]{3,2,1,0:T(8,128)(2,1)S(1)}, u32[]{:S(2)}, u32[]{:S(2)}) collective-permute-start(bf16[2,2,160,128]{3,2,1,0:T(8,128)(2,1)S(1)} %pad_maximum_fusion.3.near), channel_id=1, source_target_pairs={{0,14},{2,0},{4,2},{6,4},{8,6},{10,8},{12,10},{14,12},{1,15},{3,1}... | collective-permute-start | bytes 491528 | tf_op jit(solution)/shard_map/ppermute | solution.py:19
  105.3 9.5 %collective-permute-start.21 = (bf16[2,2,160,128]{3,2,1,0:T(8,128)(2,1)S(1)}, bf16[2,2,160,128]{3,2,1,0:T(8,128)(2,1)S(1)}, u32[]{:S(2)}, u32[]{:S(2)}) collective-permute-start(bf16[2,2,160,128]{3,2,1,0:T(8,128)(2,1)S(1)} %pad_maximum_fusion.3.near), channel_id=1, source_target_pairs={{0,4},{2,6},{4,8},{6,10},{8,12},{10,14},{12,0},{14,2},{1,5},{3,7},... | collective-permute-start | bytes 491528 | tf_op jit(solution)/shard_map/ppermute | solution.py:19
  115.4 5.2 %copy-start.21 = (s32[256]{0:T(256)S(1)}, s32[256]{0:T(256)}, u32[]{:S(2)}) copy-start(s32[256]{0:T(256)} %constant.94.clone) | copy-start | bytes 3076
  115.4 5.2 %copy-start.22 = (s32[256]{0:T(256)S(1)}, s32[256]{0:T(256)}, u32[]{:S(2)}) copy-start(s32[256]{0:T(256)} %constant.95.clone) | copy-start | bytes 3076
  115.4 5.2 %copy-start.23 = (s32[256]{0:T(256)S(1)}, s32[256]{0:T(256)}, u32[]{:S(2)}) copy-start(s32[256]{0:T(256)} %constant.96.clone) | copy-start | bytes 3076
  115.4 5.2 %copy-start.24 = (s32[256]{0:T(256)S(1)}, s32[256]{0:T(256)}, u32[]{:S(2)}) copy-start(s32[256]{0:T(256)} %constant.97.clone) | copy-start | bytes 3076
  115.4 5.2 %copy-start.25 = (s32[256]{0:T(256)S(1)}, s32[256]{0:T(256)}, u32[]{:S(2)}) copy-start(s32[256]{0:T(256)} %constant.98.clone) | copy-start | bytes 3076
  115.4 5.2 %collective-permute-start.22 = (bf16[2560,128]{1,0:T(8,128)(2,1)S(1)}, bf16[2560,128]{1,0:T(8,128)(2,1)S(1)}, u32[]{:S(2)}, u32[]{:S(2)}) collective-permute-start(bf16[2560,128]{1,0:T(8,128)(2,1)S(1)} %bitcast.40), channel_id=1, source_target_pairs={{0,1},{1,0},{2,3},{3,2},{4,5},{5,4},{6,7},{7,6},{8,9},{9,8},{10,11... | collective-permute-start | bytes 1966088 | tf_op jit(solution)/shard_map/ppermute | solution.py:19
  120.4 1.4 collective-permute-start.18
  124.1 5.2 %copy-start.29 = (s32[8]{0:T(128)S(1)}, s32[8]{0:T(128)}, u32[]{:S(2)}) copy-start(s32[8]{0:T(128)} %param.17) | copy-start | bytes 100
  124.1 26.5 %all-to-all-start.3 = ((bf16[8,40,2560]{2,1,0:T(8,128)(2,1)}), bf16[8,40,2560]{2,1,0:T(8,128)(2,1)S(1)}, u32[]{:S(2)}, u32[]{:S(2)}) async-start(bf16[8,40,2560]{2,1,0:T(8,128)(2,1)} %bitcast.25), calls=%async_computation.3 | async-start | bytes 3276800 | tf_op jit(solution)/shard_map/all_to_all | solution.py:305

commit v5 on v4

--- a/solution.py
+++ b/solution.py
@@ -81,7 +81,7 @@
         send.wait()
 
 
-def product(parts, pieces, xh):
+def product(parts, pieces, xh, grant):
     arrays = [p[0] for p in parts]
     depth = arrays[0].shape[1]
     total = sum(p[2] for p in parts)
@@ -99,7 +99,7 @@
             pltpu.VMEM((2, 8, total // 8, cols // 2), BF16),
             pltpu.SemaphoreType.DMA((len(parts) + len(pieces) + 2,)),
         ],
-        compiler_params=pltpu.CompilerParams(vmem_limit_bytes=40 << 20),
+        compiler_params=pltpu.CompilerParams(vmem_limit_bytes=grant << 20),
         cost_estimate=pl.CostEstimate(
             flops=2 * total * depth * cols,
             bytes_accessed=2 * (total * depth + cols * depth + total * cols),
@@ -236,7 +236,7 @@
     block_3 = ring(block_2[: 2 * size + extra])
     pieces = (keep, keep_c, *got, *got_c)
     parts = [(panel, 0), (turned, 0), (crossed, 0), (block_2, 0), (block_2, size)]
-    out = product([(*p, size) for p in parts], pieces, xh)
+    out = product([(*p, size) for p in parts], pieces, xh, 40)
     out, block_3, in_cols, in_other, *pieces = stage(
         out, block_3, in_cols, in_other, *pieces
     )
@@ -273,12 +273,14 @@
         r, ("xh", "z"), [(a * 8 + b, c * 8 + d) for (a, b), (c, d) in both]
     )
     parts = [(block_3, 0, size), (block_3, size, size), (last, 0, size)]
-    out = product(parts, pieces, xh)
+    out = product(parts, pieces, xh, 60)
     out, first, r, far, cross, far_cross = stage(out, first, r, far, cross, far_cross)
     second = home(out)
 
     quad = jnp.stack([jnp.stack([r, cross]), jnp.stack([far, far_cross])])
     below, above, two = shift(quad, "z", 1), shift(quad, "z", -1), shift(quad, "z", 2)
+    added = lambda p: jnp.sum(p.astype(F32), axis=0).astype(BF16)
+    below, above, two, first = stage(below, above, two, added(first))
     place = jnp.stack([xh, z]).astype(jnp.int32)
     r = arrange(place, quad, below, above, two).reshape(32 * own_in, 16 * tokens)
     r = jnp.concatenate([r, shift(r, "core")], axis=1)
@@ -293,9 +295,7 @@
     pick = (jnp.arange(32 * tokens)[:, None] == source[None, :]).astype(BF16)
     rotated_in = jnp.dot(r, pick, preferred_element_type=F32).astype(BF16)
 
-    mixed = jnp.concatenate(
-        [jnp.sum(p.astype(F32), axis=0).astype(BF16) for p in (first, second)]
-    )
+    mixed = jnp.concatenate([first, added(second)])
     left = jnp.concatenate([mixed[:, :own_out], shift(mixed[:, own_out:], "core")])
 
     corr = lax.dot_general(

time: 153 us -> 152 us (level)
  waiting for transfers between devices: 58.9 us -> 62.7 us
  other arithmetic: 5.52 us -> 3.3 us
  local copies, waits for them, and re-layouts: 5.38 us -> 3.73 us
    unnamed x60 -> x46, local copies, waits for them, and re-layouts: 3.71 us -> 1.09 us
    ppermute x1, waiting for transfers between devices: 1.32 us -> 3.39 us  [shards(): lax.ppermute(r, ('xh', 'z'), [(a * 8 + b, c * 8 + d) for (a, b), (c, d) i...]
    ppermute x15, waiting for transfers between devices: 24 us -> 25.8 us  [shift(): lax.ppermute(x, axis, [(i, (i + step) % count) for i in range(count)])]
  transfers between devices with their start and end apart: 27 -> 27, of which waited for: 14 -> 15; matrix products, arithmetic and copies ran while one was open for 4% -> 3% of each run, Pallas kernels for 10% -> 10%
where the time goes in v5:
time: 152 us; the launch traced here: 151 us
  waiting for transfers between devices  62.7 us (41%)
  starting transfers between devices  62.4 us (41%)
  Pallas kernels  15.4 us (10%)
  local copies, waits for them, and re-layouts  3.73 us (2%)
  other arithmetic  3.3 us (2%)
  matrix products  3.25 us (2%)
    ppermute x15, starting transfers between devices, shift(): lax.ppermute(x, axis, [(i, (i + step) % count) for i in range(count)])  29 us
    ppermute x15, waiting for transfers between devices, shift(): lax.ppermute(x, axis, [(i, (i + step) % count) for i in range(count)])  25.8 us
    all_to_all x1, waiting for transfers between devices, shards(): lax.all_to_all(square.reshape(groups, own_out // groups, square.shape[1])...  21.2 us
    ppermute x7, waiting for transfers between devices, shards(): ring = lambda x, way=turn: lax.ppermute(x, ('z', 'core'), way)  12.3 us
    ppermute x7, starting transfers between devices, shards(): ring = lambda x, way=turn: lax.ppermute(x, ('z', 'core'), way)  12.1 us
    pallas_call x2, Pallas kernels, product(): pl.pallas_call(lambda *refs: product_kernel(spans, *refs), out_shape=jax....  11.4 us
    all_to_all x2, starting transfers between devices, home(): return lax.all_to_all(out, ('xh', 'xl', 'y'), 0, 0)  11 us
    all_to_all x1, starting transfers between devices, shards(): lax.all_to_all(square.reshape(groups, own_out // groups, square.shape[1])...  5.45 us
  transfers between devices with their start and end apart: 27, of which 15 were waited for; matrix products, arithmetic and copies ran while one was open for 3% of the time, Pallas kernels for 10%

profile of v5, /device:TPU:1, one launch (start us, length us, event | category | flops | bytes accessed | tf_op | source)
XLA Modules:
  0.0 151.2 jit_solution(9242080914337661507)
XLA Ops:
  0.0 3.6 %collective-permute-start = (bf16[8,5120]{1,0:T(8,128)(2,1)}, bf16[8,5120]{1,0:T(8,128)(2,1)S(1)}, u32[]{:S(2)}, u32[]{:S(2)}) collective-permute-start(bf16[8,5120]{1,0:T(8,128)(2,1)} %param.13), channel_id=1, source_target_pairs={{0,16},{16,0},{1,17},{17,1},{2,18},{18,2},{3,19},{19,3},{4,20},{20... | collective-permute-start | bytes 245768 | tf_op jit(solution)/shard_map/ppermute | solution.py:19
  3.6 4.9 %all-to-all-start = ((bf16[16,8,1280]{2,1,0:T(8,128)(2,1)}), bf16[16,8,1280]{2,1,0:T(8,128)(2,1)S(1)}, u32[]{:S(2)}, u32[]{:S(2)}) async-start(bf16[16,8,1280]{2,1,0:T(8,128)(2,1)} %bitcast.47), calls=%async_computation | async-start | bytes 655360 | tf_op jit(solution)/shard_map/all_to_all | solution.py:219
  8.5 0.9 pad_maximum_fusion.2.refs_1_
  9.4 5.7 %collective-permute-start.1 = (bf16[64,1280]{1,0:T(8,128)(2,1)S(1)}, bf16[64,1280]{1,0:T(8,128)(2,1)S(1)}, u32[]{:S(2)}, u32[]{:S(2)}) collective-permute-start(bf16[64,1280]{1,0:T(8,128)(2,1)S(1)} %pad_maximum_fusion.2.refs_1_), channel_id=1, source_target_pairs={{0,2},{1,15},{2,4},{3,1},{4,6},{5,3},{6,8},{7,5},{8,10},{9,7},{10,... | collective-permute-start | bytes 491528 | tf_op jit(solution)/shard_map/ppermute | solution.py:212
  15.0 1.5 dynamic-slice_bitcast_fusion
  16.6 1.2 collective-permute-done.1.refs_2_
  17.7 2.4 %collective-permute-done.2.refs_3_ = bf16[64,1280]{1,0:T(8,128)(2,1)S(1)} collective-permute-done((bf16[64,1280]{1,0:T(8,128)(2,1)S(1)}, bf16[64,1280]{1,0:T(8,128)(2,1)S(1)}, u32[]{:S(2)}, u32[]{:S(2)}) %collective-permute-start.2) | collective-permute-done | bytes 163872 | tf_op jit(solution)/shard_map/ppermute | solution.py:212
  20.1 2.5 %collective-permute-start.4 = (bf16[256,1280]{1,0:T(8,128)(2,1)S(1)}, bf16[256,1280]{1,0:T(8,128)(2,1)S(1)}, u32[]{:S(2)}, u32[]{:S(2)}) collective-permute-start(bf16[256,1280]{1,0:T(8,128)(2,1)S(1)} %pad_maximum_fusion.1), channel_id=1, source_target_pairs={{0,2},{1,15},{2,4},{3,1},{4,6},{5,3},{6,8},{7,5},{8,10},{9,7},{10,... | collective-permute-start | bytes 1966088 | tf_op jit(solution)/shard_map/ppermute | solution.py:212
  22.6 2.6 %collective-permute-start.3 = (bf16[160,1280]{1,0:T(8,128)(2,1)S(1)}, bf16[160,1280]{1,0:T(8,128)(2,1)S(1)}, u32[]{:S(2)}, u32[]{:S(2)}) collective-permute-start(bf16[160,1280]{1,0:T(8,128)(2,1)S(1)} %slice.24), channel_id=1, source_target_pairs={{0,16},{16,0},{1,17},{17,1},{2,18},{18,2},{3,19},{19,3},{4,20},{20... | collective-permute-start | bytes 1228808 | tf_op jit(solution)/shard_map/ppermute | solution.py:19
  25.3 8.2 %collective-permute-done.5.refs_3_ = bf16[128,1280]{1,0:T(8,128)(2,1)S(1)} collective-permute-done((bf16[128,1280]{1,0:T(8,128)(2,1)S(1)}, bf16[128,1280]{1,0:T(8,128)(2,1)S(1)}, u32[]{:S(2)}, u32[]{:S(2)}) %collective-permute-start.5) | collective-permute-done | bytes 327712 | tf_op jit(solution)/shard_map/ppermute | solution.py:212
  33.5 0.9 collective-permute-done.3.refs_8_.refs_6_
  34.4 0.1 pad_maximum_fusion
  34.5 2.5 %collective-permute-start.7 = (bf16[384,1280]{1,0:T(8,128)(2,1)S(1)}, bf16[384,1280]{1,0:T(8,128)(2,1)S(1)}, u32[]{:S(2)}, u32[]{:S(2)}) collective-permute-start(bf16[384,1280]{1,0:T(8,128)(2,1)S(1)} %pad_maximum_fusion), channel_id=1, source_target_pairs={{0,2},{1,15},{2,4},{3,1},{4,6},{5,3},{6,8},{7,5},{8,10},{9,7},{10,... | collective-permute-start | bytes 2949128 | tf_op jit(solution)/shard_map/ppermute | solution.py:212
  37.0 2.6 %collective-permute-start.6 = (bf16[160,1280]{1,0:T(8,128)(2,1)S(1)}, bf16[160,1280]{1,0:T(8,128)(2,1)S(1)}, u32[]{:S(2)}, u32[]{:S(2)}) collective-permute-start(bf16[160,1280]{1,0:T(8,128)(2,1)S(1)} %slice.25), channel_id=1, source_target_pairs={{0,16},{16,0},{1,17},{17,1},{2,18},{18,2},{3,19},{19,3},{4,20},{20... | collective-permute-start | bytes 1228808 | tf_op jit(solution)/shard_map/ppermute | solution.py:19
  39.7 0.2 collective-permute-start.8
  39.8 0.3 collective-permute-start.12
  40.2 9.6 %collective-permute-done.6.refs_9_.refs_7_ = bf16[160,1280]{1,0:T(8,128)(2,1)S(1)} collective-permute-done((bf16[160,1280]{1,0:T(8,128)(2,1)S(1)}, bf16[160,1280]{1,0:T(8,128)(2,1)S(1)}, u32[]{:S(2)}, u32[]{:S(2)}) %collective-permute-start.6) | collective-permute-done | bytes 409632 | tf_op jit(solution)/shard_map/ppermute | solution.py:19
  49.8 0.1 slice.28
  49.8 1.5 collective-permute-start.11
  51.3 1.2 collective-permute-start.9
  52.5 0.1 collective-permute-start.10
  52.6 1.3 collective-permute-done.9.refs_10_.refs_8_
  53.9 0.6 collective-permute-done.10.refs_11_.refs_9_
  54.5 6.3 %shard_map.127 = bf16[2,8,80,640]{3,2,1,0:T(8,128)(2,1)} custom-call(s32[1]{0:T(128)} %bitcast.refs_0_, bf16[128,1280]{1,0:T(8,128)(2,1)S(1)} %bitcast.39, bf16[256,1280]{1,0:T(8,128)(2,1)S(1)} %collective-permute-done.4.refs_2_.refs_4_.refs_5_, bf16[128,1280]{1,0:T(8,128)(2,1)S(1)} %collective-permute-done.5.refs_3_, ...), custom_call_target="tpu_custom_call" | custom-call | flops 2097152000 | bytes 6553600 | tf_op jit(solution)/shard_map/pallas_call | solution.py:90
  60.9 0.6 collective-permute-done.11.refs_1_.refs_2_.refs_8_
  61.5 0.3 copy-done.9
  61.8 6.3 %all-to-all-start.1 = ((bf16[16,80,640]{2,1,0:T(8,128)(2,1)}), bf16[16,80,640]{2,1,0:T(8,128)(2,1)S(1)}, u32[]{:S(2)}, u32[]{:S(2)}) async-start(bf16[16,80,640]{2,1,0:T(8,128)(2,1)} %bitcast.13), calls=%async_computation.1 | async-start | bytes 3276800 | tf_op jit(solution)/shard_map/all_to_all | solution.py:246
  68.1 1.0 slice.29
  69.1 0.0 copy-start.19
  69.1 0.0 copy-start.20
  69.1 0.0 copy-start.21
  69.1 3.5 %shard_map.129 = bf16[2,80,128]{2,1,0:T(8,128)(2,1)} custom-call(s32[1]{0:T(128)} %bitcast.14.refs_0_, bf16[64,1280]{1,0:T(8,128)(2,1)} %copy-done.12, bf16[64,1280]{1,0:T(8,128)(2,1)} %copy-done.10, bf16[64,1280]{1,0:T(8,128)(2,1)} %copy-done.11, bf16[256,1280]{1,0:T(8,128)(2,1)} %copy-done.1, bf16[256,1280]{1,0:T(8,128)(2,1)} %copy-done.1, ...), custom_call_target="tpu_custom_call" | custom-call | flops 209715200 | bytes 2949120 | tf_op jit(solution)/shard_map/pallas_call | solution.py:151
  72.6 4.8 %collective-permute-start.14 = (bf16[160,128]{1,0:T(8,128)(2,1)}, bf16[160,128]{1,0:T(8,128)(2,1)S(1)}, u32[]{:S(2)}, u32[]{:S(2)}) collective-permute-start(bf16[160,128]{1,0:T(8,128)(2,1)} %bitcast.50), channel_id=1, source_target_pairs={{0,1},{1,0},{2,3},{3,2},{4,5},{5,4},{6,7},{7,6},{8,9},{9,8},{10,11... | collective-permute-start | bytes 122888 | tf_op jit(solution)/shard_map/ppermute | solution.py:19
  77.5 1.0 collective-permute-done.14
  78.5 0.9 convolution_convert_fusion.1
  79.4 5.3 %collective-permute-start.15 = (bf16[160,128]{1,0:T(8,128)(2,1)S(1)}, bf16[160,128]{1,0:T(8,128)(2,1)S(1)}, u32[]{:S(2)}, u32[]{:S(2)}) collective-permute-start(bf16[160,128]{1,0:T(8,128)(2,1)S(1)} %convolution_convert_fusion.1), channel_id=1, source_target_pairs={{0,8},{2,10},{4,12},{6,14},{8,0},{10,2},{12,4},{14,6},{1,9},{3,11}... | collective-permute-start | bytes 122888 | tf_op jit(solution)/shard_map/ppermute | solution.py:19
  84.8 3.1 %collective-permute-start.16 = (bf16[160,128]{1,0:T(8,128)(2,1)S(1)}, bf16[160,128]{1,0:T(8,128)(2,1)S(1)}, u32[]{:S(2)}, u32[]{:S(2)}) collective-permute-start(bf16[160,128]{1,0:T(8,128)(2,1)S(1)} %convolution_convert_fusion.1), channel_id=1, source_target_pairs={{0,16},{16,0},{1,17},{17,1},{2,18},{18,2},{3,19},{19,3},{4,20},{20... | collective-permute-start | bytes 122888 | tf_op jit(solution)/shard_map/ppermute | solution.py:19
  87.9 0.7 copy-done.13
  88.7 5.0 %shard_map.128 = bf16[2,8,48,640]{3,2,1,0:T(8,128)(2,1)} custom-call(s32[1]{0:T(128)} %bitcast.refs_0_, bf16[320,1280]{1,0:T(8,128)(2,1)} %collective-permute-done.11.refs_1_.refs_2_.refs_8_, bf16[320,1280]{1,0:T(8,128)(2,1)} %collective-permute-done.11.refs_1_.refs_2_.refs_8_, bf16[128,1280]{1,0:T(8,128)(2,1)} %copy-done.13, bf16[320,1280]{1,0:T(8,128)(2,1)} %copy-done.2, ...), custom_call_target="tpu_custom_call" | custom-call | flops 1258291200 | bytes 5242880 | tf_op jit(solution)/shard_map/pallas_call | solution.py:90
  93.7 3.4 %collective-permute-done.17 = bf16[160,128]{1,0:T(8,128)(2,1)S(1)} collective-permute-done((bf16[160,128]{1,0:T(8,128)(2,1)S(1)}, bf16[160,128]{1,0:T(8,128)(2,1)S(1)}, u32[]{:S(2)}, u32[]{:S(2)}) %collective-permute-start.17) | collective-permute-done | bytes 40992 | tf_op jit(solution)/shard_map/ppermute | solution.py:272
  97.1 4.7 %all-to-all-start.2 = ((bf16[16,48,640]{2,1,0:T(8,128)(2,1)}), bf16[16,48,640]{2,1,0:T(8,128)(2,1)S(1)}, u32[]{:S(2)}, u32[]{:S(2)}) async-start(bf16[16,48,640]{2,1,0:T(8,128)(2,1)} %bitcast.42), calls=%async_computation.2 | async-start | bytes 1966080 | tf_op jit(solution)/shard_map/all_to_all | solution.py:246
  101.8 0.5 collective-permute-start.18
  102.3 2.2 %collective-permute-start.19 = (bf16[2,2,160,128]{3,2,1,0:T(8,128)(2,1)S(1)}, bf16[2,2,160,128]{3,2,1,0:T(8,128)(2,1)S(1)}, u32[]{:S(2)}, u32[]{:S(2)}) collective-permute-start(bf16[2,2,160,128]{3,2,1,0:T(8,128)(2,1)S(1)} %pad_maximum_fusion.3.near), channel_id=1, source_target_pairs={{0,14},{2,0},{4,2},{6,4},{8,6},{10,8},{12,10},{14,12},{1,15},{3,1}... | collective-permute-start | bytes 491528 | tf_op jit(solution)/shard_map/ppermute | solution.py:19
  104.6 0.1 pad_add_fusion.place_ref
  104.7 0.2 reduce_sum.52
  104.9 0.0 copy-start.14
  104.9 0.0 copy-start.15
  104.9 0.0 copy-start.16
  104.9 0.0 copy-start.17
  105.0 0.0 copy-start.18
  105.0 2.3 %collective-permute-done.18.below = bf16[2,2,160,128]{3,2,1,0:T(8,128)(2,1)S(1)} collective-permute-done((bf16[2,2,160,128]{3,2,1,0:T(8,128)(2,1)S(1)}, bf16[2,2,160,128]{3,2,1,0:T(8,128)(2,1)S(1)}, u32[]{:S(2)}, u32[]{:S(2)}) %collective-permute-start.18) | collective-permute-done | bytes 163872 | tf_op jit(solution)/shard_map/ppermute | solution.py:19
  107.3 9.1 %collective-permute-done.20.two = bf16[2,2,160,128]{3,2,1,0:T(8,128)(2,1)S(1)} collective-permute-done((bf16[2,2,160,128]{3,2,1,0:T(8,128)(2,1)S(1)}, bf16[2,2,160,128]{3,2,1,0:T(8,128)(2,1)S(1)}, u32[]{:S(2)}, u32[]{:S(2)}) %collective-permute-start.20) | collective-permute-done | bytes 163872 | tf_op jit(solution)/shard_map/ppermute | solution.py:19
  116.4 0.6 shard_map.130
  117.0 1.7 %collective-permute-start.22 = (bf16[2560,128]{1,0:T(8,128)(2,1)S(1)}, bf16[2560,128]{1,0:T(8,128)(2,1)S(1)}, u32[]{:S(2)}, u32[]{:S(2)}) collective-permute-start(bf16[2560,128]{1,0:T(8,128)(2,1)S(1)} %bitcast.40), channel_id=1, source_target_pairs={{0,1},{1,0},{2,3},{3,2},{4,5},{5,4},{6,7},{7,6},{8,9},{9,8},{10,11... | collective-permute-start | bytes 1966088 | tf_op jit(solution)/shard_map/ppermute | solution.py:19
  118.7 0.1 reduce_sum.53
  118.8 0.1 fusion.15
  118.9 0.6 collective-permute-start.21
  119.5 0.9 collective-permute-done.22
  120.4 0.1 collective-permute-done.21
  120.5 2.3 %fusion = bf16[320,2560]{1,0:T(8,128)(2,1)} fusion(bf16[2560,128]{1,0:T(8,128)(2,1)S(1)} %collective-permute-done.22, bf16[2560,128]{1,0:T(8,128)(2,1)S(1)} %bitcast.41, bf16[128,320]{1,0:T(8,128)(2,1)S(1)} %collective-permute-done.21, bf16[128,320]{1,0:T(8,128)(2,1)S(1)} %get-tuple-element.73, s32[256]{0:T(256)S(1)} %fusion.26), kind=kOutput, calls=%fused_computation.3 | convolution fusion | flops 760283136 | bytes 3113984 | tf_op jit(solution)/shard_map/dot_general | solution.py:301
  122.8 5.5 %all-to-all-start.3 = ((bf16[8,40,2560]{2,1,0:T(8,128)(2,1)}), bf16[8,40,2560]{2,1,0:T(8,128)(2,1)S(1)}, u32[]{:S(2)}, u32[]{:S(2)}) async-start(bf16[8,40,2560]{2,1,0:T(8,128)(2,1)} %bitcast.25), calls=%async_computation.3 | async-start | bytes 3276800 | tf_op jit(solution)/shard_map/all_to_all | solution.py:305
  128.3 21.2 %all-to-all-done.3 = bf16[8,40,2560]{2,1,0:T(8,128)(2,1)S(1)} async-done(((bf16[8,40,2560]{2,1,0:T(8,128)(2,1)}), bf16[8,40,2560]{2,1,0:T(8,128)(2,1)S(1)}, u32[]{:S(2)}, u32[]{:S(2)}) %all-to-all-start.3) | async-done | bytes 1638432 | tf_op jit(solution)/shard_map/all_to_all | solution.py:305
  149.6 0.6 fusion.1
  150.3 1.0 fusion.9
  (63 shorter events, 0.4 us)
Async XLA Ops:
  0.0 8.5 %collective-permute-start = (bf16[8,5120]{1,0:T(8,128)(2,1)}, bf16[8,5120]{1,0:T(8,128)(2,1)S(1)}, u32[]{:S(2)}, u32[]{:S(2)}) collective-permute-start(bf16[8,5120]{1,0:T(8,128)(2,1)} %param.13), channel_id=1, source_target_pairs={{0,16},{16,0},{1,17},{17,1},{2,18},{18,2},{3,19},{19,3},{4,20},{20... | collective-permute-start | bytes 245768 | tf_op jit(solution)/shard_map/ppermute | solution.py:19
  3.6 16.5 %all-to-all-start = ((bf16[16,8,1280]{2,1,0:T(8,128)(2,1)}), bf16[16,8,1280]{2,1,0:T(8,128)(2,1)S(1)}, u32[]{:S(2)}, u32[]{:S(2)}) async-start(bf16[16,8,1280]{2,1,0:T(8,128)(2,1)} %bitcast.47), calls=%async_computation | async-start | bytes 655360 | tf_op jit(solution)/shard_map/all_to_all | solution.py:219
  9.4 7.2 %copy-start.12 = (bf16[64,1280]{1,0:T(8,128)(2,1)}, bf16[64,1280]{1,0:T(8,128)(2,1)S(1)}, u32[]{:S(2)}) copy-start(bf16[64,1280]{1,0:T(8,128)(2,1)S(1)} %pad_maximum_fusion.2.refs_1_) | copy-start | bytes 491524
  9.4 8.3 %collective-permute-start.1 = (bf16[64,1280]{1,0:T(8,128)(2,1)S(1)}, bf16[64,1280]{1,0:T(8,128)(2,1)S(1)}, u32[]{:S(2)}, u32[]{:S(2)}) collective-permute-start(bf16[64,1280]{1,0:T(8,128)(2,1)S(1)} %pad_maximum_fusion.2.refs_1_), channel_id=1, source_target_pairs={{0,2},{1,15},{2,4},{3,1},{4,6},{5,3},{6,8},{7,5},{8,10},{9,7},{10,... | collective-permute-start | bytes 491528 | tf_op jit(solution)/shard_map/ppermute | solution.py:212
  15.0 5.0 %collective-permute-start.2 = (bf16[64,1280]{1,0:T(8,128)(2,1)S(1)}, bf16[64,1280]{1,0:T(8,128)(2,1)S(1)}, u32[]{:S(2)}, u32[]{:S(2)}) collective-permute-start(bf16[64,1280]{1,0:T(8,128)(2,1)S(1)} %pad_maximum_fusion.2.refs_1_), channel_id=1, source_target_pairs={{0,15},{1,2},{2,1},{3,4},{4,3},{5,6},{6,5},{7,8},{8,7},{9,10},{10,... | collective-permute-start | bytes 491528 | tf_op jit(solution)/shard_map/ppermute | solution.py:212
  16.6 37.9 %copy-start.2 = (bf16[320,1280]{1,0:T(8,128)(2,1)}, bf16[320,1280]{1,0:T(8,128)(2,1)S(1)}, u32[]{:S(2)}) copy-start(bf16[320,1280]{1,0:T(8,128)(2,1)S(1)} %get-tuple-element.48.refs_6_.refs_4_) | copy-start | bytes 2457604
  17.7 16.7 %copy-start.10 = (bf16[64,1280]{1,0:T(8,128)(2,1)}, bf16[64,1280]{1,0:T(8,128)(2,1)S(1)}, u32[]{:S(2)}) copy-start(bf16[64,1280]{1,0:T(8,128)(2,1)S(1)} %collective-permute-done.1.refs_2_) | copy-start | bytes 491524
  20.1 14.3 %copy-start.11 = (bf16[64,1280]{1,0:T(8,128)(2,1)}, bf16[64,1280]{1,0:T(8,128)(2,1)S(1)}, u32[]{:S(2)}) copy-start(bf16[64,1280]{1,0:T(8,128)(2,1)S(1)} %collective-permute-done.2.refs_3_) | copy-start | bytes 491524
  20.1 14.2 %collective-permute-start.4 = (bf16[256,1280]{1,0:T(8,128)(2,1)S(1)}, bf16[256,1280]{1,0:T(8,128)(2,1)S(1)}, u32[]{:S(2)}, u32[]{:S(2)}) collective-permute-start(bf16[256,1280]{1,0:T(8,128)(2,1)S(1)} %pad_maximum_fusion.1), channel_id=1, source_target_pairs={{0,2},{1,15},{2,4},{3,1},{4,6},{5,3},{6,8},{7,5},{8,10},{9,7},{10,... | collective-permute-start | bytes 1966088 | tf_op jit(solution)/shard_map/ppermute | solution.py:212
  22.6 11.7 %collective-permute-start.3 = (bf16[160,1280]{1,0:T(8,128)(2,1)S(1)}, bf16[160,1280]{1,0:T(8,128)(2,1)S(1)}, u32[]{:S(2)}, u32[]{:S(2)}) collective-permute-start(bf16[160,1280]{1,0:T(8,128)(2,1)S(1)} %slice.24), channel_id=1, source_target_pairs={{0,16},{16,0},{1,17},{17,1},{2,18},{18,2},{3,19},{19,3},{4,20},{20... | collective-permute-start | bytes 1228808 | tf_op jit(solution)/shard_map/ppermute | solution.py:19
  25.3 8.2 %collective-permute-start.5 = (bf16[128,1280]{1,0:T(8,128)(2,1)S(1)}, bf16[128,1280]{1,0:T(8,128)(2,1)S(1)}, u32[]{:S(2)}, u32[]{:S(2)}) collective-permute-start(bf16[128,1280]{1,0:T(8,128)(2,1)S(1)} %bitcast.38), channel_id=1, source_target_pairs={{0,15},{1,2},{2,1},{3,4},{4,3},{5,6},{6,5},{7,8},{8,7},{9,10},{10,... | collective-permute-start | bytes 983048 | tf_op jit(solution)/shard_map/ppermute | solution.py:212
  34.4 20.1 %copy-start.4 = (bf16[160,1280]{1,0:T(8,128)(2,1)}, bf16[160,1280]{1,0:T(8,128)(2,1)S(1)}, u32[]{:S(2)}) copy-start(bf16[160,1280]{1,0:T(8,128)(2,1)S(1)} %collective-permute-done.3.refs_8_.refs_6_) | copy-start | bytes 1228804
  34.4 20.1 %copy-start.1 = (bf16[256,1280]{1,0:T(8,128)(2,1)}, bf16[256,1280]{1,0:T(8,128)(2,1)S(1)}, u32[]{:S(2)}) copy-start(bf16[256,1280]{1,0:T(8,128)(2,1)S(1)} %collective-permute-done.4.refs_2_.refs_4_.refs_5_) | copy-start | bytes 1966084
  34.4 5.4 %copy-start.8 = (bf16[5120,80]{0,1:T(8,128)(2,1)S(1)}, bf16[5120,80]{0,1:T(8,128)(2,1)}, u32[]{:S(2)}) copy-start(bf16[5120,80]{0,1:T(8,128)(2,1)} %param.15) | copy-start | bytes 2457604
  34.5 15.2 %collective-permute-start.7 = (bf16[384,1280]{1,0:T(8,128)(2,1)S(1)}, bf16[384,1280]{1,0:T(8,128)(2,1)S(1)}, u32[]{:S(2)}, u32[]{:S(2)}) collective-permute-start(bf16[384,1280]{1,0:T(8,128)(2,1)S(1)} %pad_maximum_fusion), channel_id=1, source_target_pairs={{0,2},{1,15},{2,4},{3,1},{4,6},{5,3},{6,8},{7,5},{8,10},{9,7},{10,... | collective-permute-start | bytes 2949128 | tf_op jit(solution)/shard_map/ppermute | solution.py:212
  37.0 12.7 %collective-permute-start.6 = (bf16[160,1280]{1,0:T(8,128)(2,1)S(1)}, bf16[160,1280]{1,0:T(8,128)(2,1)S(1)}, u32[]{:S(2)}, u32[]{:S(2)}) collective-permute-start(bf16[160,1280]{1,0:T(8,128)(2,1)S(1)} %slice.25), channel_id=1, source_target_pairs={{0,16},{16,0},{1,17},{17,1},{2,18},{18,2},{3,19},{19,3},{4,20},{20... | collective-permute-start | bytes 1228808 | tf_op jit(solution)/shard_map/ppermute | solution.py:19
  39.7 12.9 %collective-permute-start.8 = (bf16[320,1280]{1,0:T(8,128)(2,1)S(1)}, bf16[320,1280]{1,0:T(8,128)(2,1)S(1)}, u32[]{:S(2)}, u32[]{:S(2)}) collective-permute-start(bf16[320,1280]{1,0:T(8,128)(2,1)S(1)} %get-tuple-element.48.refs_6_.refs_4_), channel_id=1, source_target_pairs={{0,1},{1,0},{2,3},{3,2},{4,5},{5,4},{6,7},{7,6},{8,9},{9,8},{10,11... | collective-permute-start | bytes 2457608 | tf_op jit(solution)/shard_map/ppermute | solution.py:19
  39.8 21.0 %collective-permute-start.12 = (bf16[80,5120]{1,0:T(8,128)(2,1)S(1)}, bf16[80,5120]{1,0:T(8,128)(2,1)S(1)}, u32[]{:S(2)}, u32[]{:S(2)}) collective-permute-start(bf16[80,5120]{1,0:T(8,128)(2,1)S(1)} %bitcast.46), channel_id=1, source_target_pairs={{0,1},{1,0},{2,3},{3,2},{4,5},{5,4},{6,7},{7,6},{8,9},{9,8},{10,11... | collective-permute-start | bytes 2457608 | tf_op jit(solution)/shard_map/ppermute | solution.py:19
  49.8 11.0 %copy-start.5 = (bf16[160,1280]{1,0:T(8,128)(2,1)}, bf16[160,1280]{1,0:T(8,128)(2,1)S(1)}, u32[]{:S(2)}) copy-start(bf16[160,1280]{1,0:T(8,128)(2,1)S(1)} %collective-permute-done.6.refs_9_.refs_7_) | copy-start | bytes 1228804
  49.8 11.0 %copy-start = (bf16[384,1280]{1,0:T(8,128)(2,1)}, bf16[384,1280]{1,0:T(8,128)(2,1)S(1)}, u32[]{:S(2)}) copy-start(bf16[384,1280]{1,0:T(8,128)(2,1)S(1)} %collective-permute-done.7.refs_4_.refs_5_.refs_6_.refs_7_) | copy-start | bytes 2949124
  49.8 11.7 %collective-permute-start.11 = (bf16[320,1280]{1,0:T(8,128)(2,1)S(1)}, bf16[320,1280]{1,0:T(8,128)(2,1)}, u32[]{:S(2)}, u32[]{:S(2)}) collective-permute-start(bf16[320,1280]{1,0:T(8,128)(2,1)S(1)} %slice.28), channel_id=1, source_target_pairs={{0,2},{1,15},{2,4},{3,1},{4,6},{5,3},{6,8},{7,5},{8,10},{9,7},{10,... | collective-permute-start | bytes 2457608 | tf_op jit(solution)/shard_map/ppermute | solution.py:212
  51.3 2.6 %collective-permute-start.9 = (bf16[160,1280]{1,0:T(8,128)(2,1)S(1)}, bf16[160,1280]{1,0:T(8,128)(2,1)S(1)}, u32[]{:S(2)}, u32[]{:S(2)}) collective-permute-start(bf16[160,1280]{1,0:T(8,128)(2,1)S(1)} %collective-permute-done.3.refs_8_.refs_6_), channel_id=1, source_target_pairs={{0,1},{1,0},{2,3},{3,2},{4,5},{5,4},{6,7},{7,6},{8,9},{9,8},{10,11... | collective-permute-start | bytes 1228808 | tf_op jit(solution)/shard_map/ppermute | solution.py:19
  52.5 2.0 %collective-permute-start.10 = (bf16[160,1280]{1,0:T(8,128)(2,1)S(1)}, bf16[160,1280]{1,0:T(8,128)(2,1)S(1)}, u32[]{:S(2)}, u32[]{:S(2)}) collective-permute-start(bf16[160,1280]{1,0:T(8,128)(2,1)S(1)} %collective-permute-done.6.refs_9_.refs_7_), channel_id=1, source_target_pairs={{0,1},{1,0},{2,3},{3,2},{4,5},{5,4},{6,7},{7,6},{8,9},{9,8},{10,11... | collective-permute-start | bytes 1228808 | tf_op jit(solution)/shard_map/ppermute | solution.py:19
  52.6 8.2 %copy-start.3 = (bf16[320,1280]{1,0:T(8,128)(2,1)}, bf16[320,1280]{1,0:T(8,128)(2,1)S(1)}, u32[]{:S(2)}) copy-start(bf16[320,1280]{1,0:T(8,128)(2,1)S(1)} %collective-permute-done.8.refs_7_.refs_5_) | copy-start | bytes 2457604
  53.9 7.0 %copy-start.6 = (bf16[160,1280]{1,0:T(8,128)(2,1)}, bf16[160,1280]{1,0:T(8,128)(2,1)S(1)}, u32[]{:S(2)}) copy-start(bf16[160,1280]{1,0:T(8,128)(2,1)S(1)} %collective-permute-done.9.refs_10_.refs_8_) | copy-start | bytes 1228804
  54.4 6.4 %copy-start.7 = (bf16[160,1280]{1,0:T(8,128)(2,1)}, bf16[160,1280]{1,0:T(8,128)(2,1)S(1)}, u32[]{:S(2)}) copy-start(bf16[160,1280]{1,0:T(8,128)(2,1)S(1)} %collective-permute-done.10.refs_11_.refs_9_) | copy-start | bytes 1228804
  60.9 0.9 copy-start.9
  61.8 35.4 %all-to-all-start.1 = ((bf16[16,80,640]{2,1,0:T(8,128)(2,1)}), bf16[16,80,640]{2,1,0:T(8,128)(2,1)S(1)}, u32[]{:S(2)}, u32[]{:S(2)}) async-start(bf16[16,80,640]{2,1,0:T(8,128)(2,1)} %bitcast.13), calls=%async_computation.1 | async-start | bytes 3276800 | tf_op jit(solution)/shard_map/all_to_all | solution.py:246
  69.1 8.4 %copy-start.19 = (s32[128]{0:T(128)S(1)}, s32[128]{0:T(128)}, u32[]{:S(2)}) copy-start(s32[128]{0:T(128)} %constant.91.clone) | copy-start | bytes 1540
  69.1 8.3 %copy-start.20 = (s32[128]{0:T(128)S(1)}, s32[128]{0:T(128)}, u32[]{:S(2)}) copy-start(s32[128]{0:T(128)} %constant.92.clone) | copy-start | bytes 1540
  69.1 8.3 %copy-start.21 = (s32[128]{0:T(128)S(1)}, s32[128]{0:T(128)}, u32[]{:S(2)}) copy-start(s32[128]{0:T(128)} %constant.93.clone) | copy-start | bytes 1540
  72.6 5.9 %collective-permute-start.14 = (bf16[160,128]{1,0:T(8,128)(2,1)}, bf16[160,128]{1,0:T(8,128)(2,1)S(1)}, u32[]{:S(2)}, u32[]{:S(2)}) collective-permute-start(bf16[160,128]{1,0:T(8,128)(2,1)} %bitcast.50), channel_id=1, source_target_pairs={{0,1},{1,0},{2,3},{3,2},{4,5},{5,4},{6,7},{7,6},{8,9},{9,8},{10,11... | collective-permute-start | bytes 122888 | tf_op jit(solution)/shard_map/ppermute | solution.py:19
  77.4 10.5 %collective-permute-start.13 = (bf16[128,1280]{1,0:T(8,128)(2,1)S(1)}, bf16[128,1280]{1,0:T(8,128)(2,1)S(1)}, u32[]{:S(2)}, u32[]{:S(2)}) collective-permute-start(bf16[128,1280]{1,0:T(8,128)(2,1)S(1)} %slice.29), channel_id=1, source_target_pairs={{0,2},{1,15},{2,4},{3,1},{4,6},{5,3},{6,8},{7,5},{8,10},{9,7},{10,... | collective-permute-start | bytes 983048 | tf_op jit(solution)/shard_map/ppermute | solution.py:212
  79.4 14.2 %collective-permute-start.15 = (bf16[160,128]{1,0:T(8,128)(2,1)S(1)}, bf16[160,128]{1,0:T(8,128)(2,1)S(1)}, u32[]{:S(2)}, u32[]{:S(2)}) collective-permute-start(bf16[160,128]{1,0:T(8,128)(2,1)S(1)} %convolution_convert_fusion.1), channel_id=1, source_target_pairs={{0,8},{2,10},{4,12},{6,14},{8,0},{10,2},{12,4},{14,6},{1,9},{3,11}... | collective-permute-start | bytes 122888 | tf_op jit(solution)/shard_map/ppermute | solution.py:19
  84.8 8.9 %collective-permute-start.16 = (bf16[160,128]{1,0:T(8,128)(2,1)S(1)}, bf16[160,128]{1,0:T(8,128)(2,1)S(1)}, u32[]{:S(2)}, u32[]{:S(2)}) collective-permute-start(bf16[160,128]{1,0:T(8,128)(2,1)S(1)} %convolution_convert_fusion.1), channel_id=1, source_target_pairs={{0,16},{16,0},{1,17},{17,1},{2,18},{18,2},{3,19},{19,3},{4,20},{20... | collective-permute-start | bytes 122888 | tf_op jit(solution)/shard_map/ppermute | solution.py:19
  87.9 9.2 %collective-permute-start.17 = (bf16[160,128]{1,0:T(8,128)(2,1)S(1)}, bf16[160,128]{1,0:T(8,128)(2,1)S(1)}, u32[]{:S(2)}, u32[]{:S(2)}) collective-permute-start(bf16[160,128]{1,0:T(8,128)(2,1)S(1)} %convolution_convert_fusion.1), channel_id=1, source_target_pairs={{0,24},{2,26},{4,28},{6,30},{8,16},{10,18},{12,20},{14,22},{16,8},... | collective-permute-start | bytes 122888 | tf_op jit(solution)/shard_map/ppermute | solution.py:272
  87.9 0.7 copy-start.13
  97.1 21.6 %all-to-all-start.2 = ((bf16[16,48,640]{2,1,0:T(8,128)(2,1)}), bf16[16,48,640]{2,1,0:T(8,128)(2,1)S(1)}, u32[]{:S(2)}, u32[]{:S(2)}) async-start(bf16[16,48,640]{2,1,0:T(8,128)(2,1)} %bitcast.42), calls=%async_computation.2 | async-start | bytes 1966080 | tf_op jit(solution)/shard_map/all_to_all | solution.py:246
  101.8 5.5 %collective-permute-start.18 = (bf16[2,2,160,128]{3,2,1,0:T(8,128)(2,1)S(1)}, bf16[2,2,160,128]{3,2,1,0:T(8,128)(2,1)S(1)}, u32[]{:S(2)}, u32[]{:S(2)}) collective-permute-start(bf16[2,2,160,128]{3,2,1,0:T(8,128)(2,1)S(1)} %pad_maximum_fusion.3.near), channel_id=1, source_target_pairs={{0,2},{2,4},{4,6},{6,8},{8,10},{10,12},{12,14},{14,0},{1,3},{3,5},... | collective-permute-start | bytes 491528 | tf_op jit(solution)/shard_map/ppermute | solution.py:19
  102.3 5.0 %collective-permute-start.19 = (bf16[2,2,160,128]{3,2,1,0:T(8,128)(2,1)S(1)}, bf16[2,2,160,128]{3,2,1,0:T(8,128)(2,1)S(1)}, u32[]{:S(2)}, u32[]{:S(2)}) collective-permute-start(bf16[2,2,160,128]{3,2,1,0:T(8,128)(2,1)S(1)} %pad_maximum_fusion.3.near), channel_id=1, source_target_pairs={{0,14},{2,0},{4,2},{6,4},{8,6},{10,8},{12,10},{14,12},{1,15},{3,1}... | collective-permute-start | bytes 491528 | tf_op jit(solution)/shard_map/ppermute | solution.py:19
  104.6 11.8 %collective-permute-start.20 = (bf16[2,2,160,128]{3,2,1,0:T(8,128)(2,1)S(1)}, bf16[2,2,160,128]{3,2,1,0:T(8,128)(2,1)S(1)}, u32[]{:S(2)}, u32[]{:S(2)}) collective-permute-start(bf16[2,2,160,128]{3,2,1,0:T(8,128)(2,1)S(1)} %pad_maximum_fusion.3.near), channel_id=1, source_target_pairs={{0,4},{2,6},{4,8},{6,10},{8,12},{10,14},{12,0},{14,2},{1,5},{3,7},... | collective-permute-start | bytes 491528 | tf_op jit(solution)/shard_map/ppermute | solution.py:19
  104.9 14.6 %copy-start.14 = (s32[256]{0:T(256)S(1)}, s32[256]{0:T(256)}, u32[]{:S(2)}) copy-start(s32[256]{0:T(256)} %constant.94.clone) | copy-start | bytes 3076
  104.9 14.6 %copy-start.15 = (s32[256]{0:T(256)S(1)}, s32[256]{0:T(256)}, u32[]{:S(2)}) copy-start(s32[256]{0:T(256)} %constant.95.clone) | copy-start | bytes 3076
  104.9 14.6 %copy-start.16 = (s32[256]{0:T(256)S(1)}, s32[256]{0:T(256)}, u32[]{:S(2)}) copy-start(s32[256]{0:T(256)} %constant.96.clone) | copy-start | bytes 3076
  104.9 14.5 %copy-start.17 = (s32[256]{0:T(256)S(1)}, s32[256]{0:T(256)}, u32[]{:S(2)}) copy-start(s32[256]{0:T(256)} %constant.97.clone) | copy-start | bytes 3076
  105.0 14.5 %copy-start.18 = (s32[256]{0:T(256)S(1)}, s32[256]{0:T(256)}, u32[]{:S(2)}) copy-start(s32[256]{0:T(256)} %constant.98.clone) | copy-start | bytes 3076
  117.0 3.4 %collective-permute-start.22 = (bf16[2560,128]{1,0:T(8,128)(2,1)S(1)}, bf16[2560,128]{1,0:T(8,128)(2,1)S(1)}, u32[]{:S(2)}, u32[]{:S(2)}) collective-permute-start(bf16[2560,128]{1,0:T(8,128)(2,1)S(1)} %bitcast.40), channel_id=1, source_target_pairs={{0,1},{1,0},{2,3},{3,2},{4,5},{5,4},{6,7},{7,6},{8,9},{9,8},{10,11... | collective-permute-start | bytes 1966088 | tf_op jit(solution)/shard_map/ppermute | solution.py:19
  118.9 1.6 %collective-permute-start.21 = (bf16[128,320]{1,0:T(8,128)(2,1)S(1)}, bf16[128,320]{1,0:T(8,128)(2,1)S(1)}, u32[]{:S(2)}, u32[]{:S(2)}) collective-permute-start(bf16[128,320]{1,0:T(8,128)(2,1)S(1)} %get-tuple-element.74), channel_id=1, source_target_pairs={{0,1},{1,0},{2,3},{3,2},{4,5},{5,4},{6,7},{7,6},{8,9},{9,8},{10,11... | collective-permute-start | bytes 245768 | tf_op jit(solution)/shard_map/ppermute | solution.py:19
  122.8 5.5 %copy-start.22 = (s32[8]{0:T(128)S(1)}, s32[8]{0:T(128)}, u32[]{:S(2)}) copy-start(s32[8]{0:T(128)} %param.17) | copy-start | bytes 100
  122.8 26.7 %all-to-all-start.3 = ((bf16[8,40,2560]{2,1,0:T(8,128)(2,1)}), bf16[8,40,2560]{2,1,0:T(8,128)(2,1)S(1)}, u32[]{:S(2)}, u32[]{:S(2)}) async-start(bf16[8,40,2560]{2,1,0:T(8,128)(2,1)} %bitcast.25), calls=%async_computation.3 | async-start | bytes 3276800 | tf_op jit(solution)/shard_map/all_to_all | solution.py:305

commit v6 on v5

--- a/solution.py
+++ b/solution.py
@@ -266,21 +266,22 @@
     pick = (jnp.arange(32 * tokens)[:, None] == source[None, :]).astype(BF16)
     r = jnp.dot(r, pick, preferred_element_type=F32).astype(BF16)
 
-    far = shift(r, "z", 4)
-    cross = shift(r, "xh")
     both = [((a, b), (1 - a, (b + 4) % 8)) for a in range(2) for b in range(8)]
     far_cross = lax.ppermute(
         r, ("xh", "z"), [(a * 8 + b, c * 8 + d) for (a, b), (c, d) in both]
     )
+    cross = shift(r, "xh")
+    far = shift(r, "z", 4)
     parts = [(block_3, 0, size), (block_3, size, size), (last, 0, size)]
     out = product(parts, pieces, xh, 60)
-    out, first, r, far, cross, far_cross = stage(out, first, r, far, cross, far_cross)
+    out, first, r, far_cross, cross, far = stage(out, first, r, far_cross, cross, far)
     second = home(out)
 
     quad = jnp.stack([jnp.stack([r, cross]), jnp.stack([far, far_cross])])
-    below, above, two = shift(quad, "z", 1), shift(quad, "z", -1), shift(quad, "z", 2)
+    two = shift(quad, "z", 2)
+    below, above = shift(quad, "z", 1), shift(quad, "z", -1)
     added = lambda p: jnp.sum(p.astype(F32), axis=0).astype(BF16)
-    below, above, two, first = stage(below, above, two, added(first))
+    two, below, above, first = stage(two, below, above, added(first))
     place = jnp.stack([xh, z]).astype(jnp.int32)
     r = arrange(place, quad, below, above, two).reshape(32 * own_in, 16 * tokens)
     r = jnp.concatenate([r, shift(r, "core")], axis=1)

time: 152 us -> 150 us (0.987)
  waiting for transfers between devices: 62.7 us -> 59 us
  starting transfers between devices: 62.4 us -> 64.3 us
    ppermute x1, starting transfers between devices: 0.01 us -> 8.19 us  [shards(): lax.ppermute(r, ('xh', 'z'), [(a * 8 + b, c * 8 + d) for (a, b), (c, d) i...]
    ppermute x15, starting transfers between devices: 29 us -> 22.2 us  [shift(): lax.ppermute(x, axis, [(i, (i + step) % count) for i in range(count)])]
    ppermute x1, waiting for transfers between devices: 3.39 us -> 0.01 us  [shards(): lax.ppermute(r, ('xh', 'z'), [(a * 8 + b, c * 8 + d) for (a, b), (c, d) i...]
    all_to_all x2, starting transfers between devices: 11 us -> 12.7 us  [home(): return lax.all_to_all(out, ('xh', 'xl', 'y'), 0, 0)]
  transfers between devices with their start and end apart: 27 -> 27, of which waited for: 15 -> 14; matrix products, arithmetic and copies ran while one was open for 3% -> 3% of each run, Pallas kernels for 10% -> 10%
where the time goes in v6:
time: 150 us; the launch traced here: 149 us
  starting transfers between devices  64.3 us (43%)
  waiting for transfers between devices  59 us (39%)
  Pallas kernels  15.4 us (10%)
  local copies, waits for them, and re-layouts  3.74 us (2%)
  other arithmetic  3.3 us (2%)
  matrix products  3.25 us (2%)
    ppermute x15, waiting for transfers between devices, shift(): lax.ppermute(x, axis, [(i, (i + step) % count) for i in range(count)])  25.4 us
    ppermute x15, starting transfers between devices, shift(): lax.ppermute(x, axis, [(i, (i + step) % count) for i in range(count)])  22.2 us
    all_to_all x1, waiting for transfers between devices, shards(): lax.all_to_all(square.reshape(groups, own_out // groups, square.shape[1])...  21.3 us
    all_to_all x2, starting transfers between devices, home(): return lax.all_to_all(out, ('xh', 'xl', 'y'), 0, 0)  12.7 us
    ppermute x7, waiting for transfers between devices, shards(): ring = lambda x, way=turn: lax.ppermute(x, ('z', 'core'), way)  12.3 us
    ppermute x7, starting transfers between devices, shards(): ring = lambda x, way=turn: lax.ppermute(x, ('z', 'core'), way)  12.1 us
    pallas_call x2, Pallas kernels, product(): pl.pallas_call(lambda *refs: product_kernel(spans, *refs), out_shape=jax....  11.4 us
    ppermute x1, starting transfers between devices, shards(): lax.ppermute(r, ('xh', 'z'), [(a * 8 + b, c * 8 + d) for (a, b), (c, d) i...  8.19 us
  transfers between devices with their start and end apart: 27, of which 14 were waited for; matrix products, arithmetic and copies ran while one was open for 3% of the time, Pallas kernels for 10%

profile of v6, /device:TPU:1, one launch (start us, length us, event | category | flops | bytes accessed | tf_op | source)
XLA Modules:
  0.0 149.4 jit_solution(16474322045525760985)
XLA Ops:
  0.0 3.6 %collective-permute-start = (bf16[8,5120]{1,0:T(8,128)(2,1)}, bf16[8,5120]{1,0:T(8,128)(2,1)S(1)}, u32[]{:S(2)}, u32[]{:S(2)}) collective-permute-start(bf16[8,5120]{1,0:T(8,128)(2,1)} %param.13), channel_id=1, source_target_pairs={{0,16},{16,0},{1,17},{17,1},{2,18},{18,2},{3,19},{19,3},{4,20},{20... | collective-permute-start | bytes 245768 | tf_op jit(solution)/shard_map/ppermute | solution.py:19
  3.6 4.9 %all-to-all-start = ((bf16[16,8,1280]{2,1,0:T(8,128)(2,1)}), bf16[16,8,1280]{2,1,0:T(8,128)(2,1)S(1)}, u32[]{:S(2)}, u32[]{:S(2)}) async-start(bf16[16,8,1280]{2,1,0:T(8,128)(2,1)} %bitcast.47), calls=%async_computation | async-start | bytes 655360 | tf_op jit(solution)/shard_map/all_to_all | solution.py:219
  8.5 0.9 pad_maximum_fusion.2.refs_1_
  9.4 5.7 %collective-permute-start.1 = (bf16[64,1280]{1,0:T(8,128)(2,1)S(1)}, bf16[64,1280]{1,0:T(8,128)(2,1)S(1)}, u32[]{:S(2)}, u32[]{:S(2)}) collective-permute-start(bf16[64,1280]{1,0:T(8,128)(2,1)S(1)} %pad_maximum_fusion.2.refs_1_), channel_id=1, source_target_pairs={{0,2},{1,15},{2,4},{3,1},{4,6},{5,3},{6,8},{7,5},{8,10},{9,7},{10,... | collective-permute-start | bytes 491528 | tf_op jit(solution)/shard_map/ppermute | solution.py:212
  15.0 1.5 %dynamic-slice_bitcast_fusion = (bf16[320,1280]{1,0:T(8,128)(2,1)S(1)}, bf16[320,1280]{1,0:T(8,128)(2,1)S(1)}) fusion(bf16[2560,320]{0,1:T(8,128)(2,1)} %param.16, s32[]{:T(128)S(6)} %select_n.42, s32[]{:T(128)S(6)} %select_n.41), kind=kLoop, calls=%fused_computation.14 | loop fusion | bytes 3276808 | tf_op jit(solution)/shard_map/dynamic_slice | solution.py:223
  16.6 1.2 collective-permute-done.1.refs_2_
  17.7 2.4 %collective-permute-done.2.refs_3_ = bf16[64,1280]{1,0:T(8,128)(2,1)S(1)} collective-permute-done((bf16[64,1280]{1,0:T(8,128)(2,1)S(1)}, bf16[64,1280]{1,0:T(8,128)(2,1)S(1)}, u32[]{:S(2)}, u32[]{:S(2)}) %collective-permute-start.2) | collective-permute-done | bytes 163872 | tf_op jit(solution)/shard_map/ppermute | solution.py:212
  20.1 2.5 %collective-permute-start.4 = (bf16[256,1280]{1,0:T(8,128)(2,1)S(1)}, bf16[256,1280]{1,0:T(8,128)(2,1)S(1)}, u32[]{:S(2)}, u32[]{:S(2)}) collective-permute-start(bf16[256,1280]{1,0:T(8,128)(2,1)S(1)} %pad_maximum_fusion.1), channel_id=1, source_target_pairs={{0,2},{1,15},{2,4},{3,1},{4,6},{5,3},{6,8},{7,5},{8,10},{9,7},{10,... | collective-permute-start | bytes 1966088 | tf_op jit(solution)/shard_map/ppermute | solution.py:212
  22.6 2.6 %collective-permute-start.3 = (bf16[160,1280]{1,0:T(8,128)(2,1)S(1)}, bf16[160,1280]{1,0:T(8,128)(2,1)S(1)}, u32[]{:S(2)}, u32[]{:S(2)}) collective-permute-start(bf16[160,1280]{1,0:T(8,128)(2,1)S(1)} %slice.24), channel_id=1, source_target_pairs={{0,16},{16,0},{1,17},{17,1},{2,18},{18,2},{3,19},{19,3},{4,20},{20... | collective-permute-start | bytes 1228808 | tf_op jit(solution)/shard_map/ppermute | solution.py:19
  25.3 8.2 %collective-permute-done.5.refs_3_ = bf16[128,1280]{1,0:T(8,128)(2,1)S(1)} collective-permute-done((bf16[128,1280]{1,0:T(8,128)(2,1)S(1)}, bf16[128,1280]{1,0:T(8,128)(2,1)S(1)}, u32[]{:S(2)}, u32[]{:S(2)}) %collective-permute-start.5) | collective-permute-done | bytes 327712 | tf_op jit(solution)/shard_map/ppermute | solution.py:212
  33.5 0.9 collective-permute-done.3.refs_8_.refs_6_
  34.4 0.1 pad_maximum_fusion
  34.5 2.5 %collective-permute-start.7 = (bf16[384,1280]{1,0:T(8,128)(2,1)S(1)}, bf16[384,1280]{1,0:T(8,128)(2,1)S(1)}, u32[]{:S(2)}, u32[]{:S(2)}) collective-permute-start(bf16[384,1280]{1,0:T(8,128)(2,1)S(1)} %pad_maximum_fusion), channel_id=1, source_target_pairs={{0,2},{1,15},{2,4},{3,1},{4,6},{5,3},{6,8},{7,5},{8,10},{9,7},{10,... | collective-permute-start | bytes 2949128 | tf_op jit(solution)/shard_map/ppermute | solution.py:212
  37.0 2.6 %collective-permute-start.6 = (bf16[160,1280]{1,0:T(8,128)(2,1)S(1)}, bf16[160,1280]{1,0:T(8,128)(2,1)S(1)}, u32[]{:S(2)}, u32[]{:S(2)}) collective-permute-start(bf16[160,1280]{1,0:T(8,128)(2,1)S(1)} %slice.25), channel_id=1, source_target_pairs={{0,16},{16,0},{1,17},{17,1},{2,18},{18,2},{3,19},{19,3},{4,20},{20... | collective-permute-start | bytes 1228808 | tf_op jit(solution)/shard_map/ppermute | solution.py:19
  39.7 0.2 collective-permute-start.8
  39.8 0.3 collective-permute-start.12
  40.2 9.6 %collective-permute-done.6.refs_9_.refs_7_ = bf16[160,1280]{1,0:T(8,128)(2,1)S(1)} collective-permute-done((bf16[160,1280]{1,0:T(8,128)(2,1)S(1)}, bf16[160,1280]{1,0:T(8,128)(2,1)S(1)}, u32[]{:S(2)}, u32[]{:S(2)}) %collective-permute-start.6) | collective-permute-done | bytes 409632 | tf_op jit(solution)/shard_map/ppermute | solution.py:19
  49.8 0.1 slice.28
  49.8 1.5 collective-permute-start.11
  51.3 1.2 collective-permute-start.9
  52.5 0.1 collective-permute-start.10
  52.6 1.3 collective-permute-done.9.refs_10_.refs_8_
  53.9 0.6 collective-permute-done.10.refs_11_.refs_9_
  54.5 6.3 %shard_map.127 = bf16[2,8,80,640]{3,2,1,0:T(8,128)(2,1)} custom-call(s32[1]{0:T(128)} %bitcast.refs_0_, bf16[128,1280]{1,0:T(8,128)(2,1)S(1)} %bitcast.39, bf16[256,1280]{1,0:T(8,128)(2,1)S(1)} %collective-permute-done.4.refs_2_.refs_4_.refs_5_, bf16[128,1280]{1,0:T(8,128)(2,1)S(1)} %collective-permute-done.5.refs_3_, ...), custom_call_target="tpu_custom_call" | custom-call | flops 2097152000 | bytes 6553600 | tf_op jit(solution)/shard_map/pallas_call | solution.py:90
  60.9 0.6 collective-permute-done.11.refs_1_.refs_2_.refs_8_
  61.5 0.3 copy-done.9
  61.8 6.3 %all-to-all-start.1 = ((bf16[16,80,640]{2,1,0:T(8,128)(2,1)}), bf16[16,80,640]{2,1,0:T(8,128)(2,1)S(1)}, u32[]{:S(2)}, u32[]{:S(2)}) async-start(bf16[16,80,640]{2,1,0:T(8,128)(2,1)} %bitcast.13), calls=%async_computation.1 | async-start | bytes 3276800 | tf_op jit(solution)/shard_map/all_to_all | solution.py:246
  68.1 1.0 slice.29
  69.1 0.0 copy-start.19
  69.1 0.0 copy-start.20
  69.1 0.0 copy-start.21
  69.1 3.5 %shard_map.129 = bf16[2,80,128]{2,1,0:T(8,128)(2,1)} custom-call(s32[1]{0:T(128)} %bitcast.14.refs_0_, bf16[64,1280]{1,0:T(8,128)(2,1)} %copy-done.12, bf16[64,1280]{1,0:T(8,128)(2,1)} %copy-done.10, bf16[64,1280]{1,0:T(8,128)(2,1)} %copy-done.11, bf16[256,1280]{1,0:T(8,128)(2,1)} %copy-done.1, bf16[256,1280]{1,0:T(8,128)(2,1)} %copy-done.1, ...), custom_call_target="tpu_custom_call" | custom-call | flops 209715200 | bytes 2949120 | tf_op jit(solution)/shard_map/pallas_call | solution.py:151
  72.6 4.8 %collective-permute-start.14 = (bf16[160,128]{1,0:T(8,128)(2,1)}, bf16[160,128]{1,0:T(8,128)(2,1)S(1)}, u32[]{:S(2)}, u32[]{:S(2)}) collective-permute-start(bf16[160,128]{1,0:T(8,128)(2,1)} %bitcast.50), channel_id=1, source_target_pairs={{0,1},{1,0},{2,3},{3,2},{4,5},{5,4},{6,7},{7,6},{8,9},{9,8},{10,11... | collective-permute-start | bytes 122888 | tf_op jit(solution)/shard_map/ppermute | solution.py:19
  77.5 1.0 collective-permute-done.14
  78.5 0.9 convolution_convert_fusion.1
  79.4 8.2 %collective-permute-start.15 = (bf16[160,128]{1,0:T(8,128)(2,1)S(1)}, bf16[160,128]{1,0:T(8,128)(2,1)S(1)}, u32[]{:S(2)}, u32[]{:S(2)}) collective-permute-start(bf16[160,128]{1,0:T(8,128)(2,1)S(1)} %convolution_convert_fusion.1), channel_id=1, source_target_pairs={{0,24},{2,26},{4,28},{6,30},{8,16},{10,18},{12,20},{14,22},{16,8},... | collective-permute-start | bytes 122888 | tf_op jit(solution)/shard_map/ppermute | solution.py:270
  87.6 0.4 collective-permute-start.17
  88.0 0.7 copy-done.13
  88.8 5.0 %shard_map.128 = bf16[2,8,48,640]{3,2,1,0:T(8,128)(2,1)} custom-call(s32[1]{0:T(128)} %bitcast.refs_0_, bf16[320,1280]{1,0:T(8,128)(2,1)} %collective-permute-done.11.refs_1_.refs_2_.refs_8_, bf16[320,1280]{1,0:T(8,128)(2,1)} %collective-permute-done.11.refs_1_.refs_2_.refs_8_, bf16[128,1280]{1,0:T(8,128)(2,1)} %copy-done.13, bf16[320,1280]{1,0:T(8,128)(2,1)} %copy-done.2, ...), custom_call_target="tpu_custom_call" | custom-call | flops 1258291200 | bytes 5242880 | tf_op jit(solution)/shard_map/pallas_call | solution.py:90
  93.8 1.0 collective-permute-done.17
  94.8 6.4 %all-to-all-start.2 = ((bf16[16,48,640]{2,1,0:T(8,128)(2,1)}), bf16[16,48,640]{2,1,0:T(8,128)(2,1)S(1)}, u32[]{:S(2)}, u32[]{:S(2)}) async-start(bf16[16,48,640]{2,1,0:T(8,128)(2,1)} %bitcast.42), calls=%async_computation.2 | async-start | bytes 1966080 | tf_op jit(solution)/shard_map/all_to_all | solution.py:246
  101.2 0.1 collective-permute-start.18
  101.3 1.4 collective-permute-start.19
  102.8 1.5 %collective-permute-start.20 = (bf16[2,2,160,128]{3,2,1,0:T(8,128)(2,1)S(1)}, bf16[2,2,160,128]{3,2,1,0:T(8,128)(2,1)S(1)}, u32[]{:S(2)}, u32[]{:S(2)}) collective-permute-start(bf16[2,2,160,128]{3,2,1,0:T(8,128)(2,1)S(1)} %pad_maximum_fusion.3.near), channel_id=1, source_target_pairs={{0,14},{2,0},{4,2},{6,4},{8,6},{10,8},{12,10},{14,12},{1,15},{3,1}... | collective-permute-start | bytes 491528 | tf_op jit(solution)/shard_map/ppermute | solution.py:19
  104.3 0.1 pad_add_fusion.place_ref
  104.4 0.2 reduce_sum.52
  104.6 0.0 copy-start.14
  104.6 0.0 copy-start.15
  104.6 0.0 copy-start.16
  104.6 0.0 copy-start.17
  104.6 0.0 copy-start.18
  104.7 4.1 %collective-permute-done.18.two = bf16[2,2,160,128]{3,2,1,0:T(8,128)(2,1)S(1)} collective-permute-done((bf16[2,2,160,128]{3,2,1,0:T(8,128)(2,1)S(1)}, bf16[2,2,160,128]{3,2,1,0:T(8,128)(2,1)S(1)}, u32[]{:S(2)}, u32[]{:S(2)}) %collective-permute-start.18) | collective-permute-done | bytes 163872 | tf_op jit(solution)/shard_map/ppermute | solution.py:19
  108.7 6.0 %collective-permute-done.19.below = bf16[2,2,160,128]{3,2,1,0:T(8,128)(2,1)S(1)} collective-permute-done((bf16[2,2,160,128]{3,2,1,0:T(8,128)(2,1)S(1)}, bf16[2,2,160,128]{3,2,1,0:T(8,128)(2,1)S(1)}, u32[]{:S(2)}, u32[]{:S(2)}) %collective-permute-start.19) | collective-permute-done | bytes 163872 | tf_op jit(solution)/shard_map/ppermute | solution.py:19
  114.8 0.6 shard_map.130
  115.4 1.8 %collective-permute-start.22 = (bf16[2560,128]{1,0:T(8,128)(2,1)S(1)}, bf16[2560,128]{1,0:T(8,128)(2,1)S(1)}, u32[]{:S(2)}, u32[]{:S(2)}) collective-permute-start(bf16[2560,128]{1,0:T(8,128)(2,1)S(1)} %bitcast.40), channel_id=1, source_target_pairs={{0,1},{1,0},{2,3},{3,2},{4,5},{5,4},{6,7},{7,6},{8,9},{9,8},{10,11... | collective-permute-start | bytes 1966088 | tf_op jit(solution)/shard_map/ppermute | solution.py:19
  117.2 0.1 reduce_sum.53
  117.3 0.1 fusion.15
  117.4 1.5 collective-permute-start.21
  118.9 0.9 collective-permute-done.21
  119.8 2.3 %fusion = bf16[320,2560]{1,0:T(8,128)(2,1)} fusion(bf16[2560,128]{1,0:T(8,128)(2,1)S(1)} %collective-permute-done.22, bf16[2560,128]{1,0:T(8,128)(2,1)S(1)} %bitcast.41, bf16[128,320]{1,0:T(8,128)(2,1)S(1)} %collective-permute-done.21, bf16[128,320]{1,0:T(8,128)(2,1)S(1)} %get-tuple-element.73, s32[256]{0:T(256)S(1)} %fusion.26), kind=kOutput, calls=%fused_computation.3 | convolution fusion | flops 760283136 | bytes 3113984 | tf_op jit(solution)/shard_map/dot_general | solution.py:302
  122.1 4.4 %all-to-all-start.3 = ((bf16[8,40,2560]{2,1,0:T(8,128)(2,1)}), bf16[8,40,2560]{2,1,0:T(8,128)(2,1)S(1)}, u32[]{:S(2)}, u32[]{:S(2)}) async-start(bf16[8,40,2560]{2,1,0:T(8,128)(2,1)} %bitcast.25), calls=%async_computation.3 | async-start | bytes 3276800 | tf_op jit(solution)/shard_map/all_to_all | solution.py:306
  126.5 21.3 %all-to-all-done.3 = bf16[8,40,2560]{2,1,0:T(8,128)(2,1)S(1)} async-done(((bf16[8,40,2560]{2,1,0:T(8,128)(2,1)}), bf16[8,40,2560]{2,1,0:T(8,128)(2,1)S(1)}, u32[]{:S(2)}, u32[]{:S(2)}) %all-to-all-start.3) | async-done | bytes 1638432 | tf_op jit(solution)/shard_map/all_to_all | solution.py:306
  147.8 0.6 fusion.1
  148.5 1.0 fusion.9
  (63 shorter events, 0.4 us)
Async XLA Ops:
  0.0 8.5 %collective-permute-start = (bf16[8,5120]{1,0:T(8,128)(2,1)}, bf16[8,5120]{1,0:T(8,128)(2,1)S(1)}, u32[]{:S(2)}, u32[]{:S(2)}) collective-permute-start(bf16[8,5120]{1,0:T(8,128)(2,1)} %param.13), channel_id=1, source_target_pairs={{0,16},{16,0},{1,17},{17,1},{2,18},{18,2},{3,19},{19,3},{4,20},{20... | collective-permute-start | bytes 245768 | tf_op jit(solution)/shard_map/ppermute | solution.py:19
  3.6 16.5 %all-to-all-start = ((bf16[16,8,1280]{2,1,0:T(8,128)(2,1)}), bf16[16,8,1280]{2,1,0:T(8,128)(2,1)S(1)}, u32[]{:S(2)}, u32[]{:S(2)}) async-start(bf16[16,8,1280]{2,1,0:T(8,128)(2,1)} %bitcast.47), calls=%async_computation | async-start | bytes 655360 | tf_op jit(solution)/shard_map/all_to_all | solution.py:219
  9.4 7.2 %copy-start.12 = (bf16[64,1280]{1,0:T(8,128)(2,1)}, bf16[64,1280]{1,0:T(8,128)(2,1)S(1)}, u32[]{:S(2)}) copy-start(bf16[64,1280]{1,0:T(8,128)(2,1)S(1)} %pad_maximum_fusion.2.refs_1_) | copy-start | bytes 491524
  9.4 8.3 %collective-permute-start.1 = (bf16[64,1280]{1,0:T(8,128)(2,1)S(1)}, bf16[64,1280]{1,0:T(8,128)(2,1)S(1)}, u32[]{:S(2)}, u32[]{:S(2)}) collective-permute-start(bf16[64,1280]{1,0:T(8,128)(2,1)S(1)} %pad_maximum_fusion.2.refs_1_), channel_id=1, source_target_pairs={{0,2},{1,15},{2,4},{3,1},{4,6},{5,3},{6,8},{7,5},{8,10},{9,7},{10,... | collective-permute-start | bytes 491528 | tf_op jit(solution)/shard_map/ppermute | solution.py:212
  15.0 5.0 %collective-permute-start.2 = (bf16[64,1280]{1,0:T(8,128)(2,1)S(1)}, bf16[64,1280]{1,0:T(8,128)(2,1)S(1)}, u32[]{:S(2)}, u32[]{:S(2)}) collective-permute-start(bf16[64,1280]{1,0:T(8,128)(2,1)S(1)} %pad_maximum_fusion.2.refs_1_), channel_id=1, source_target_pairs={{0,15},{1,2},{2,1},{3,4},{4,3},{5,6},{6,5},{7,8},{8,7},{9,10},{10,... | collective-permute-start | bytes 491528 | tf_op jit(solution)/shard_map/ppermute | solution.py:212
  16.6 37.9 %copy-start.2 = (bf16[320,1280]{1,0:T(8,128)(2,1)}, bf16[320,1280]{1,0:T(8,128)(2,1)S(1)}, u32[]{:S(2)}) copy-start(bf16[320,1280]{1,0:T(8,128)(2,1)S(1)} %get-tuple-element.48.refs_6_.refs_4_) | copy-start | bytes 2457604
  17.7 16.7 %copy-start.10 = (bf16[64,1280]{1,0:T(8,128)(2,1)}, bf16[64,1280]{1,0:T(8,128)(2,1)S(1)}, u32[]{:S(2)}) copy-start(bf16[64,1280]{1,0:T(8,128)(2,1)S(1)} %collective-permute-done.1.refs_2_) | copy-start | bytes 491524
  20.1 14.3 %copy-start.11 = (bf16[64,1280]{1,0:T(8,128)(2,1)}, bf16[64,1280]{1,0:T(8,128)(2,1)S(1)}, u32[]{:S(2)}) copy-start(bf16[64,1280]{1,0:T(8,128)(2,1)S(1)} %collective-permute-done.2.refs_3_) | copy-start | bytes 491524
  20.1 14.2 %collective-permute-start.4 = (bf16[256,1280]{1,0:T(8,128)(2,1)S(1)}, bf16[256,1280]{1,0:T(8,128)(2,1)S(1)}, u32[]{:S(2)}, u32[]{:S(2)}) collective-permute-start(bf16[256,1280]{1,0:T(8,128)(2,1)S(1)} %pad_maximum_fusion.1), channel_id=1, source_target_pairs={{0,2},{1,15},{2,4},{3,1},{4,6},{5,3},{6,8},{7,5},{8,10},{9,7},{10,... | collective-permute-start | bytes 1966088 | tf_op jit(solution)/shard_map/ppermute | solution.py:212
  22.6 11.7 %collective-permute-start.3 = (bf16[160,1280]{1,0:T(8,128)(2,1)S(1)}, bf16[160,1280]{1,0:T(8,128)(2,1)S(1)}, u32[]{:S(2)}, u32[]{:S(2)}) collective-permute-start(bf16[160,1280]{1,0:T(8,128)(2,1)S(1)} %slice.24), channel_id=1, source_target_pairs={{0,16},{16,0},{1,17},{17,1},{2,18},{18,2},{3,19},{19,3},{4,20},{20... | collective-permute-start | bytes 1228808 | tf_op jit(solution)/shard_map/ppermute | solution.py:19
  25.3 8.2 %collective-permute-start.5 = (bf16[128,1280]{1,0:T(8,128)(2,1)S(1)}, bf16[128,1280]{1,0:T(8,128)(2,1)S(1)}, u32[]{:S(2)}, u32[]{:S(2)}) collective-permute-start(bf16[128,1280]{1,0:T(8,128)(2,1)S(1)} %bitcast.38), channel_id=1, source_target_pairs={{0,15},{1,2},{2,1},{3,4},{4,3},{5,6},{6,5},{7,8},{8,7},{9,10},{10,... | collective-permute-start | bytes 983048 | tf_op jit(solution)/shard_map/ppermute | solution.py:212
  34.4 20.1 %copy-start.4 = (bf16[160,1280]{1,0:T(8,128)(2,1)}, bf16[160,1280]{1,0:T(8,128)(2,1)S(1)}, u32[]{:S(2)}) copy-start(bf16[160,1280]{1,0:T(8,128)(2,1)S(1)} %collective-permute-done.3.refs_8_.refs_6_) | copy-start | bytes 1228804
  34.4 20.1 %copy-start.1 = (bf16[256,1280]{1,0:T(8,128)(2,1)}, bf16[256,1280]{1,0:T(8,128)(2,1)S(1)}, u32[]{:S(2)}) copy-start(bf16[256,1280]{1,0:T(8,128)(2,1)S(1)} %collective-permute-done.4.refs_2_.refs_4_.refs_5_) | copy-start | bytes 1966084
  34.4 5.4 %copy-start.8 = (bf16[5120,80]{0,1:T(8,128)(2,1)S(1)}, bf16[5120,80]{0,1:T(8,128)(2,1)}, u32[]{:S(2)}) copy-start(bf16[5120,80]{0,1:T(8,128)(2,1)} %param.15) | copy-start | bytes 2457604
  34.5 15.2 %collective-permute-start.7 = (bf16[384,1280]{1,0:T(8,128)(2,1)S(1)}, bf16[384,1280]{1,0:T(8,128)(2,1)S(1)}, u32[]{:S(2)}, u32[]{:S(2)}) collective-permute-start(bf16[384,1280]{1,0:T(8,128)(2,1)S(1)} %pad_maximum_fusion), channel_id=1, source_target_pairs={{0,2},{1,15},{2,4},{3,1},{4,6},{5,3},{6,8},{7,5},{8,10},{9,7},{10,... | collective-permute-start | bytes 2949128 | tf_op jit(solution)/shard_map/ppermute | solution.py:212
  37.0 12.7 %collective-permute-start.6 = (bf16[160,1280]{1,0:T(8,128)(2,1)S(1)}, bf16[160,1280]{1,0:T(8,128)(2,1)S(1)}, u32[]{:S(2)}, u32[]{:S(2)}) collective-permute-start(bf16[160,1280]{1,0:T(8,128)(2,1)S(1)} %slice.25), channel_id=1, source_target_pairs={{0,16},{16,0},{1,17},{17,1},{2,18},{18,2},{3,19},{19,3},{4,20},{20... | collective-permute-start | bytes 1228808 | tf_op jit(solution)/shard_map/ppermute | solution.py:19
  39.7 12.9 %collective-permute-start.8 = (bf16[320,1280]{1,0:T(8,128)(2,1)S(1)}, bf16[320,1280]{1,0:T(8,128)(2,1)S(1)}, u32[]{:S(2)}, u32[]{:S(2)}) collective-permute-start(bf16[320,1280]{1,0:T(8,128)(2,1)S(1)} %get-tuple-element.48.refs_6_.refs_4_), channel_id=1, source_target_pairs={{0,1},{1,0},{2,3},{3,2},{4,5},{5,4},{6,7},{7,6},{8,9},{9,8},{10,11... | collective-permute-start | bytes 2457608 | tf_op jit(solution)/shard_map/ppermute | solution.py:19
  39.8 21.0 %collective-permute-start.12 = (bf16[80,5120]{1,0:T(8,128)(2,1)S(1)}, bf16[80,5120]{1,0:T(8,128)(2,1)S(1)}, u32[]{:S(2)}, u32[]{:S(2)}) collective-permute-start(bf16[80,5120]{1,0:T(8,128)(2,1)S(1)} %bitcast.46), channel_id=1, source_target_pairs={{0,1},{1,0},{2,3},{3,2},{4,5},{5,4},{6,7},{7,6},{8,9},{9,8},{10,11... | collective-permute-start | bytes 2457608 | tf_op jit(solution)/shard_map/ppermute | solution.py:19
  49.8 11.0 %copy-start.5 = (bf16[160,1280]{1,0:T(8,128)(2,1)}, bf16[160,1280]{1,0:T(8,128)(2,1)S(1)}, u32[]{:S(2)}) copy-start(bf16[160,1280]{1,0:T(8,128)(2,1)S(1)} %collective-permute-done.6.refs_9_.refs_7_) | copy-start | bytes 1228804
  49.8 11.0 %copy-start = (bf16[384,1280]{1,0:T(8,128)(2,1)}, bf16[384,1280]{1,0:T(8,128)(2,1)S(1)}, u32[]{:S(2)}) copy-start(bf16[384,1280]{1,0:T(8,128)(2,1)S(1)} %collective-permute-done.7.refs_4_.refs_5_.refs_6_.refs_7_) | copy-start | bytes 2949124
  49.8 11.7 %collective-permute-start.11 = (bf16[320,1280]{1,0:T(8,128)(2,1)S(1)}, bf16[320,1280]{1,0:T(8,128)(2,1)}, u32[]{:S(2)}, u32[]{:S(2)}) collective-permute-start(bf16[320,1280]{1,0:T(8,128)(2,1)S(1)} %slice.28), channel_id=1, source_target_pairs={{0,2},{1,15},{2,4},{3,1},{4,6},{5,3},{6,8},{7,5},{8,10},{9,7},{10,... | collective-permute-start | bytes 2457608 | tf_op jit(solution)/shard_map/ppermute | solution.py:212
  51.3 2.6 %collective-permute-start.9 = (bf16[160,1280]{1,0:T(8,128)(2,1)S(1)}, bf16[160,1280]{1,0:T(8,128)(2,1)S(1)}, u32[]{:S(2)}, u32[]{:S(2)}) collective-permute-start(bf16[160,1280]{1,0:T(8,128)(2,1)S(1)} %collective-permute-done.3.refs_8_.refs_6_), channel_id=1, source_target_pairs={{0,1},{1,0},{2,3},{3,2},{4,5},{5,4},{6,7},{7,6},{8,9},{9,8},{10,11... | collective-permute-start | bytes 1228808 | tf_op jit(solution)/shard_map/ppermute | solution.py:19
  52.5 2.0 %collective-permute-start.10 = (bf16[160,1280]{1,0:T(8,128)(2,1)S(1)}, bf16[160,1280]{1,0:T(8,128)(2,1)S(1)}, u32[]{:S(2)}, u32[]{:S(2)}) collective-permute-start(bf16[160,1280]{1,0:T(8,128)(2,1)S(1)} %collective-permute-done.6.refs_9_.refs_7_), channel_id=1, source_target_pairs={{0,1},{1,0},{2,3},{3,2},{4,5},{5,4},{6,7},{7,6},{8,9},{9,8},{10,11... | collective-permute-start | bytes 1228808 | tf_op jit(solution)/shard_map/ppermute | solution.py:19
  52.6 8.2 %copy-start.3 = (bf16[320,1280]{1,0:T(8,128)(2,1)}, bf16[320,1280]{1,0:T(8,128)(2,1)S(1)}, u32[]{:S(2)}) copy-start(bf16[320,1280]{1,0:T(8,128)(2,1)S(1)} %collective-permute-done.8.refs_7_.refs_5_) | copy-start | bytes 2457604
  53.9 7.0 %copy-start.6 = (bf16[160,1280]{1,0:T(8,128)(2,1)}, bf16[160,1280]{1,0:T(8,128)(2,1)S(1)}, u32[]{:S(2)}) copy-start(bf16[160,1280]{1,0:T(8,128)(2,1)S(1)} %collective-permute-done.9.refs_10_.refs_8_) | copy-start | bytes 1228804
  54.4 6.4 %copy-start.7 = (bf16[160,1280]{1,0:T(8,128)(2,1)}, bf16[160,1280]{1,0:T(8,128)(2,1)S(1)}, u32[]{:S(2)}) copy-start(bf16[160,1280]{1,0:T(8,128)(2,1)S(1)} %collective-permute-done.10.refs_11_.refs_9_) | copy-start | bytes 1228804
  60.9 0.9 copy-start.9
  61.8 33.1 %all-to-all-start.1 = ((bf16[16,80,640]{2,1,0:T(8,128)(2,1)}), bf16[16,80,640]{2,1,0:T(8,128)(2,1)S(1)}, u32[]{:S(2)}, u32[]{:S(2)}) async-start(bf16[16,80,640]{2,1,0:T(8,128)(2,1)} %bitcast.13), calls=%async_computation.1 | async-start | bytes 3276800 | tf_op jit(solution)/shard_map/all_to_all | solution.py:246
  69.1 8.4 %copy-start.19 = (s32[128]{0:T(128)S(1)}, s32[128]{0:T(128)}, u32[]{:S(2)}) copy-start(s32[128]{0:T(128)} %constant.91.clone) | copy-start | bytes 1540
  69.1 8.3 %copy-start.20 = (s32[128]{0:T(128)S(1)}, s32[128]{0:T(128)}, u32[]{:S(2)}) copy-start(s32[128]{0:T(128)} %constant.92.clone) | copy-start | bytes 1540
  69.1 8.3 %copy-start.21 = (s32[128]{0:T(128)S(1)}, s32[128]{0:T(128)}, u32[]{:S(2)}) copy-start(s32[128]{0:T(128)} %constant.93.clone) | copy-start | bytes 1540
  72.6 5.9 %collective-permute-start.14 = (bf16[160,128]{1,0:T(8,128)(2,1)}, bf16[160,128]{1,0:T(8,128)(2,1)S(1)}, u32[]{:S(2)}, u32[]{:S(2)}) collective-permute-start(bf16[160,128]{1,0:T(8,128)(2,1)} %bitcast.50), channel_id=1, source_target_pairs={{0,1},{1,0},{2,3},{3,2},{4,5},{5,4},{6,7},{7,6},{8,9},{9,8},{10,11... | collective-permute-start | bytes 122888 | tf_op jit(solution)/shard_map/ppermute | solution.py:19
  77.4 10.6 %collective-permute-start.13 = (bf16[128,1280]{1,0:T(8,128)(2,1)S(1)}, bf16[128,1280]{1,0:T(8,128)(2,1)S(1)}, u32[]{:S(2)}, u32[]{:S(2)}) collective-permute-start(bf16[128,1280]{1,0:T(8,128)(2,1)S(1)} %slice.29), channel_id=1, source_target_pairs={{0,2},{1,15},{2,4},{3,1},{4,6},{5,3},{6,8},{7,5},{8,10},{9,7},{10,... | collective-permute-start | bytes 983048 | tf_op jit(solution)/shard_map/ppermute | solution.py:212
  79.4 14.3 %collective-permute-start.15 = (bf16[160,128]{1,0:T(8,128)(2,1)S(1)}, bf16[160,128]{1,0:T(8,128)(2,1)S(1)}, u32[]{:S(2)}, u32[]{:S(2)}) collective-permute-start(bf16[160,128]{1,0:T(8,128)(2,1)S(1)} %convolution_convert_fusion.1), channel_id=1, source_target_pairs={{0,24},{2,26},{4,28},{6,30},{8,16},{10,18},{12,20},{14,22},{16,8},... | collective-permute-start | bytes 122888 | tf_op jit(solution)/shard_map/ppermute | solution.py:270
  87.6 6.2 %collective-permute-start.16 = (bf16[160,128]{1,0:T(8,128)(2,1)S(1)}, bf16[160,128]{1,0:T(8,128)(2,1)S(1)}, u32[]{:S(2)}, u32[]{:S(2)}) collective-permute-start(bf16[160,128]{1,0:T(8,128)(2,1)S(1)} %convolution_convert_fusion.1), channel_id=1, source_target_pairs={{0,16},{16,0},{1,17},{17,1},{2,18},{18,2},{3,19},{19,3},{4,20},{20... | collective-permute-start | bytes 122888 | tf_op jit(solution)/shard_map/ppermute | solution.py:19
  87.6 7.2 %collective-permute-start.17 = (bf16[160,128]{1,0:T(8,128)(2,1)S(1)}, bf16[160,128]{1,0:T(8,128)(2,1)S(1)}, u32[]{:S(2)}, u32[]{:S(2)}) collective-permute-start(bf16[160,128]{1,0:T(8,128)(2,1)S(1)} %convolution_convert_fusion.1), channel_id=1, source_target_pairs={{0,8},{2,10},{4,12},{6,14},{8,0},{10,2},{12,4},{14,6},{1,9},{3,11}... | collective-permute-start | bytes 122888 | tf_op jit(solution)/shard_map/ppermute | solution.py:19
  88.0 0.7 copy-start.13
  94.8 22.3 %all-to-all-start.2 = ((bf16[16,48,640]{2,1,0:T(8,128)(2,1)}), bf16[16,48,640]{2,1,0:T(8,128)(2,1)S(1)}, u32[]{:S(2)}, u32[]{:S(2)}) async-start(bf16[16,48,640]{2,1,0:T(8,128)(2,1)} %bitcast.42), calls=%async_computation.2 | async-start | bytes 1966080 | tf_op jit(solution)/shard_map/all_to_all | solution.py:246
  101.2 7.5 %collective-permute-start.18 = (bf16[2,2,160,128]{3,2,1,0:T(8,128)(2,1)S(1)}, bf16[2,2,160,128]{3,2,1,0:T(8,128)(2,1)S(1)}, u32[]{:S(2)}, u32[]{:S(2)}) collective-permute-start(bf16[2,2,160,128]{3,2,1,0:T(8,128)(2,1)S(1)} %pad_maximum_fusion.3.near), channel_id=1, source_target_pairs={{0,4},{2,6},{4,8},{6,10},{8,12},{10,14},{12,0},{14,2},{1,5},{3,7},... | collective-permute-start | bytes 491528 | tf_op jit(solution)/shard_map/ppermute | solution.py:19
  101.3 13.4 %collective-permute-start.19 = (bf16[2,2,160,128]{3,2,1,0:T(8,128)(2,1)S(1)}, bf16[2,2,160,128]{3,2,1,0:T(8,128)(2,1)S(1)}, u32[]{:S(2)}, u32[]{:S(2)}) collective-permute-start(bf16[2,2,160,128]{3,2,1,0:T(8,128)(2,1)S(1)} %pad_maximum_fusion.3.near), channel_id=1, source_target_pairs={{0,2},{2,4},{4,6},{6,8},{8,10},{10,12},{12,14},{14,0},{1,3},{3,5},... | collective-permute-start | bytes 491528 | tf_op jit(solution)/shard_map/ppermute | solution.py:19
  102.8 12.0 %collective-permute-start.20 = (bf16[2,2,160,128]{3,2,1,0:T(8,128)(2,1)S(1)}, bf16[2,2,160,128]{3,2,1,0:T(8,128)(2,1)S(1)}, u32[]{:S(2)}, u32[]{:S(2)}) collective-permute-start(bf16[2,2,160,128]{3,2,1,0:T(8,128)(2,1)S(1)} %pad_maximum_fusion.3.near), channel_id=1, source_target_pairs={{0,14},{2,0},{4,2},{6,4},{8,6},{10,8},{12,10},{14,12},{1,15},{3,1}... | collective-permute-start | bytes 491528 | tf_op jit(solution)/shard_map/ppermute | solution.py:19
  104.6 14.3 %copy-start.14 = (s32[256]{0:T(256)S(1)}, s32[256]{0:T(256)}, u32[]{:S(2)}) copy-start(s32[256]{0:T(256)} %constant.94.clone) | copy-start | bytes 3076
  104.6 14.3 %copy-start.15 = (s32[256]{0:T(256)S(1)}, s32[256]{0:T(256)}, u32[]{:S(2)}) copy-start(s32[256]{0:T(256)} %constant.95.clone) | copy-start | bytes 3076
  104.6 14.3 %copy-start.16 = (s32[256]{0:T(256)S(1)}, s32[256]{0:T(256)}, u32[]{:S(2)}) copy-start(s32[256]{0:T(256)} %constant.96.clone) | copy-start | bytes 3076
  104.6 14.3 %copy-start.17 = (s32[256]{0:T(256)S(1)}, s32[256]{0:T(256)}, u32[]{:S(2)}) copy-start(s32[256]{0:T(256)} %constant.97.clone) | copy-start | bytes 3076
  104.6 14.2 %copy-start.18 = (s32[256]{0:T(256)S(1)}, s32[256]{0:T(256)}, u32[]{:S(2)}) copy-start(s32[256]{0:T(256)} %constant.98.clone) | copy-start | bytes 3076
  115.4 3.5 %collective-permute-start.22 = (bf16[2560,128]{1,0:T(8,128)(2,1)S(1)}, bf16[2560,128]{1,0:T(8,128)(2,1)S(1)}, u32[]{:S(2)}, u32[]{:S(2)}) collective-permute-start(bf16[2560,128]{1,0:T(8,128)(2,1)S(1)} %bitcast.40), channel_id=1, source_target_pairs={{0,1},{1,0},{2,3},{3,2},{4,5},{5,4},{6,7},{7,6},{8,9},{9,8},{10,11... | collective-permute-start | bytes 1966088 | tf_op jit(solution)/shard_map/ppermute | solution.py:19
  117.4 2.4 %collective-permute-start.21 = (bf16[128,320]{1,0:T(8,128)(2,1)S(1)}, bf16[128,320]{1,0:T(8,128)(2,1)S(1)}, u32[]{:S(2)}, u32[]{:S(2)}) collective-permute-start(bf16[128,320]{1,0:T(8,128)(2,1)S(1)} %get-tuple-element.74), channel_id=1, source_target_pairs={{0,1},{1,0},{2,3},{3,2},{4,5},{5,4},{6,7},{7,6},{8,9},{9,8},{10,11... | collective-permute-start | bytes 245768 | tf_op jit(solution)/shard_map/ppermute | solution.py:19
  122.1 4.4 %copy-start.22 = (s32[8]{0:T(128)S(1)}, s32[8]{0:T(128)}, u32[]{:S(2)}) copy-start(s32[8]{0:T(128)} %param.17) | copy-start | bytes 100
  122.1 25.6 %all-to-all-start.3 = ((bf16[8,40,2560]{2,1,0:T(8,128)(2,1)}), bf16[8,40,2560]{2,1,0:T(8,128)(2,1)S(1)}, u32[]{:S(2)}, u32[]{:S(2)}) async-start(bf16[8,40,2560]{2,1,0:T(8,128)(2,1)} %bitcast.25), calls=%async_computation.3 | async-start | bytes 3276800 | tf_op jit(solution)/shard_map/all_to_all | solution.py:306

commit v7 on v6

--- a/solution.py
+++ b/solution.py
@@ -246,7 +246,6 @@
         return lax.all_to_all(out, ("xh", "xl", "y"), 0, 0)
 
     first = home(out)
-    last = ring(block_3[:size])
 
     parts = [
         (own_acts, 0),
@@ -255,7 +254,10 @@
         *((block_2, 2 * size + k * extra) for k in range(2)),
         (block_3, 2 * size),
     ]
-    r = inputs([(*p, extra) for p in parts], in_cols, in_other, core).reshape(2 * own_in, 16 * tokens)
+    r = inputs([(*p, extra) for p in parts], in_cols, in_other, core)
+    r, end = stage(r, block_3)
+    last = ring(end[:size])
+    r = r.reshape(2 * own_in, 16 * tokens)
     r = jnp.concatenate([r, shift(r, "core")], axis=1)
     z_j, xh_j, row = np.unravel_index(np.arange(16 * tokens), (8, 2, tokens))
     apart = (z_j - z) % 8

time: 150 us -> 150 us (level)
  no operation moved by 1% of the time
where the time goes in v7:
time: 150 us; the launch traced here: 149 us
  starting transfers between devices  64.9 us (43%)
  waiting for transfers between devices  58 us (39%)
  Pallas kernels  15.4 us (10%)
  local copies, waits for them, and re-layouts  3.73 us (2%)
  other arithmetic  3.3 us (2%)
  matrix products  3.25 us (2%)
    ppermute x15, waiting for transfers between devices, shift(): lax.ppermute(x, axis, [(i, (i + step) % count) for i in range(count)])  24.5 us
    ppermute x15, starting transfers between devices, shift(): lax.ppermute(x, axis, [(i, (i + step) % count) for i in range(count)])  21.7 us
    all_to_all x1, waiting for transfers between devices, shards(): lax.all_to_all(square.reshape(groups, own_out // groups, square.shape[1])...  21.3 us
    all_to_all x2, starting transfers between devices, home(): return lax.all_to_all(out, ('xh', 'xl', 'y'), 0, 0)  13.1 us
    ppermute x7, waiting for transfers between devices, shards(): ring = lambda x, way=turn: lax.ppermute(x, ('z', 'core'), way)  12.3 us
    ppermute x7, starting transfers between devices, shards(): ring = lambda x, way=turn: lax.ppermute(x, ('z', 'core'), way)  12.1 us
    pallas_call x2, Pallas kernels, product(): pl.pallas_call(lambda *refs: product_kernel(spans, *refs), out_shape=jax....  11.4 us
    ppermute x1, starting transfers between devices, shards(): lax.ppermute(r, ('xh', 'z'), [(a * 8 + b, c * 8 + d) for (a, b), (c, d) i...  8.19 us
  transfers between devices with their start and end apart: 27, of which 14 were waited for; matrix products, arithmetic and copies ran while one was open for 3% of the time, Pallas kernels for 10%

profile of v7, /device:TPU:1, one launch (start us, length us, event | category | flops | bytes accessed | tf_op | source)
XLA Modules:
  0.0 149.1 jit_solution(15112446029893629265)
XLA Ops:
  0.0 3.6 %collective-permute-start = (bf16[8,5120]{1,0:T(8,128)(2,1)}, bf16[8,5120]{1,0:T(8,128)(2,1)S(1)}, u32[]{:S(2)}, u32[]{:S(2)}) collective-permute-start(bf16[8,5120]{1,0:T(8,128)(2,1)} %param.13), channel_id=1, source_target_pairs={{0,16},{16,0},{1,17},{17,1},{2,18},{18,2},{3,19},{19,3},{4,20},{20... | collective-permute-start | bytes 245768 | tf_op jit(solution)/shard_map/ppermute | solution.py:19
  3.6 4.9 %all-to-all-start = ((bf16[16,8,1280]{2,1,0:T(8,128)(2,1)}), bf16[16,8,1280]{2,1,0:T(8,128)(2,1)S(1)}, u32[]{:S(2)}, u32[]{:S(2)}) async-start(bf16[16,8,1280]{2,1,0:T(8,128)(2,1)} %bitcast.47), calls=%async_computation | async-start | bytes 655360 | tf_op jit(solution)/shard_map/all_to_all | solution.py:219
  8.5 0.9 pad_maximum_fusion.2.refs_1_
  9.4 5.7 %collective-permute-start.1 = (bf16[64,1280]{1,0:T(8,128)(2,1)S(1)}, bf16[64,1280]{1,0:T(8,128)(2,1)S(1)}, u32[]{:S(2)}, u32[]{:S(2)}) collective-permute-start(bf16[64,1280]{1,0:T(8,128)(2,1)S(1)} %pad_maximum_fusion.2.refs_1_), channel_id=1, source_target_pairs={{0,2},{1,15},{2,4},{3,1},{4,6},{5,3},{6,8},{7,5},{8,10},{9,7},{10,... | collective-permute-start | bytes 491528 | tf_op jit(solution)/shard_map/ppermute | solution.py:212
  15.0 1.5 %dynamic-slice_bitcast_fusion = (bf16[320,1280]{1,0:T(8,128)(2,1)S(1)}, bf16[320,1280]{1,0:T(8,128)(2,1)S(1)}) fusion(bf16[2560,320]{0,1:T(8,128)(2,1)} %param.16, s32[]{:T(128)S(6)} %select_n.42, s32[]{:T(128)S(6)} %select_n.41), kind=kLoop, calls=%fused_computation.14 | loop fusion | bytes 3276808 | tf_op jit(solution)/shard_map/dynamic_slice | solution.py:223
  16.6 1.2 collective-permute-done.1.refs_2_
  17.7 2.4 %collective-permute-done.2.refs_3_ = bf16[64,1280]{1,0:T(8,128)(2,1)S(1)} collective-permute-done((bf16[64,1280]{1,0:T(8,128)(2,1)S(1)}, bf16[64,1280]{1,0:T(8,128)(2,1)S(1)}, u32[]{:S(2)}, u32[]{:S(2)}) %collective-permute-start.2) | collective-permute-done | bytes 163872 | tf_op jit(solution)/shard_map/ppermute | solution.py:212
  20.1 2.5 %collective-permute-start.4 = (bf16[256,1280]{1,0:T(8,128)(2,1)S(1)}, bf16[256,1280]{1,0:T(8,128)(2,1)S(1)}, u32[]{:S(2)}, u32[]{:S(2)}) collective-permute-start(bf16[256,1280]{1,0:T(8,128)(2,1)S(1)} %pad_maximum_fusion.1), channel_id=1, source_target_pairs={{0,2},{1,15},{2,4},{3,1},{4,6},{5,3},{6,8},{7,5},{8,10},{9,7},{10,... | collective-permute-start | bytes 1966088 | tf_op jit(solution)/shard_map/ppermute | solution.py:212
  22.6 2.6 %collective-permute-start.3 = (bf16[160,1280]{1,0:T(8,128)(2,1)S(1)}, bf16[160,1280]{1,0:T(8,128)(2,1)S(1)}, u32[]{:S(2)}, u32[]{:S(2)}) collective-permute-start(bf16[160,1280]{1,0:T(8,128)(2,1)S(1)} %slice.24), channel_id=1, source_target_pairs={{0,16},{16,0},{1,17},{17,1},{2,18},{18,2},{3,19},{19,3},{4,20},{20... | collective-permute-start | bytes 1228808 | tf_op jit(solution)/shard_map/ppermute | solution.py:19
  25.3 8.2 %collective-permute-done.5.refs_3_ = bf16[128,1280]{1,0:T(8,128)(2,1)S(1)} collective-permute-done((bf16[128,1280]{1,0:T(8,128)(2,1)S(1)}, bf16[128,1280]{1,0:T(8,128)(2,1)S(1)}, u32[]{:S(2)}, u32[]{:S(2)}) %collective-permute-start.5) | collective-permute-done | bytes 327712 | tf_op jit(solution)/shard_map/ppermute | solution.py:212
  33.5 0.9 collective-permute-done.3.refs_8_.refs_6_
  34.4 0.1 pad_maximum_fusion
  34.5 2.5 %collective-permute-start.7 = (bf16[384,1280]{1,0:T(8,128)(2,1)S(1)}, bf16[384,1280]{1,0:T(8,128)(2,1)S(1)}, u32[]{:S(2)}, u32[]{:S(2)}) collective-permute-start(bf16[384,1280]{1,0:T(8,128)(2,1)S(1)} %pad_maximum_fusion), channel_id=1, source_target_pairs={{0,2},{1,15},{2,4},{3,1},{4,6},{5,3},{6,8},{7,5},{8,10},{9,7},{10,... | collective-permute-start | bytes 2949128 | tf_op jit(solution)/shard_map/ppermute | solution.py:212
  37.0 2.6 %collective-permute-start.6 = (bf16[160,1280]{1,0:T(8,128)(2,1)S(1)}, bf16[160,1280]{1,0:T(8,128)(2,1)S(1)}, u32[]{:S(2)}, u32[]{:S(2)}) collective-permute-start(bf16[160,1280]{1,0:T(8,128)(2,1)S(1)} %slice.25), channel_id=1, source_target_pairs={{0,16},{16,0},{1,17},{17,1},{2,18},{18,2},{3,19},{19,3},{4,20},{20... | collective-permute-start | bytes 1228808 | tf_op jit(solution)/shard_map/ppermute | solution.py:19
  39.7 0.2 collective-permute-start.8
  39.8 0.3 collective-permute-start.12
  40.2 9.6 %collective-permute-done.6.refs_9_.refs_7_ = bf16[160,1280]{1,0:T(8,128)(2,1)S(1)} collective-permute-done((bf16[160,1280]{1,0:T(8,128)(2,1)S(1)}, bf16[160,1280]{1,0:T(8,128)(2,1)S(1)}, u32[]{:S(2)}, u32[]{:S(2)}) %collective-permute-start.6) | collective-permute-done | bytes 409632 | tf_op jit(solution)/shard_map/ppermute | solution.py:19
  49.8 0.1 slice.28
  49.8 1.5 collective-permute-start.11
  51.3 1.2 collective-permute-start.9
  52.5 0.1 collective-permute-start.10
  52.6 1.3 collective-permute-done.9.refs_10_.refs_8_
  53.9 0.6 collective-permute-done.10.refs_11_.refs_9_
  54.5 6.3 %shard_map.127 = bf16[2,8,80,640]{3,2,1,0:T(8,128)(2,1)} custom-call(s32[1]{0:T(128)} %bitcast.refs_0_, bf16[128,1280]{1,0:T(8,128)(2,1)S(1)} %bitcast.39, bf16[256,1280]{1,0:T(8,128)(2,1)S(1)} %collective-permute-done.4.refs_2_.refs_4_.refs_5_, bf16[128,1280]{1,0:T(8,128)(2,1)S(1)} %collective-permute-done.5.refs_3_, ...), custom_call_target="tpu_custom_call" | custom-call | flops 2097152000 | bytes 6553600 | tf_op jit(solution)/shard_map/pallas_call | solution.py:90
  60.9 0.6 collective-permute-done.11.refs_8_.refs_1_.refs_2_
  61.5 0.3 copy-done.9
  61.8 6.3 %all-to-all-start.1 = ((bf16[16,80,640]{2,1,0:T(8,128)(2,1)}), bf16[16,80,640]{2,1,0:T(8,128)(2,1)S(1)}, u32[]{:S(2)}, u32[]{:S(2)}) async-start(bf16[16,80,640]{2,1,0:T(8,128)(2,1)} %bitcast.14), calls=%async_computation.1 | async-start | bytes 3276800 | tf_op jit(solution)/shard_map/all_to_all | solution.py:246
  68.1 0.0 copy-start.19
  68.1 0.0 copy-start.20
  68.1 0.0 copy-start.21
  68.1 3.5 %shard_map.128 = bf16[2,80,128]{2,1,0:T(8,128)(2,1)} custom-call(s32[1]{0:T(128)} %bitcast.13.refs_0_, bf16[64,1280]{1,0:T(8,128)(2,1)} %copy-done.12, bf16[64,1280]{1,0:T(8,128)(2,1)} %copy-done.10, bf16[64,1280]{1,0:T(8,128)(2,1)} %copy-done.11, bf16[256,1280]{1,0:T(8,128)(2,1)} %copy-done.1, bf16[256,1280]{1,0:T(8,128)(2,1)} %copy-done.1, ...), custom_call_target="tpu_custom_call" | custom-call | flops 209715200 | bytes 2949120 | tf_op jit(solution)/shard_map/pallas_call | solution.py:151
  71.6 4.8 %collective-permute-start.14 = (bf16[160,128]{1,0:T(8,128)(2,1)}, bf16[160,128]{1,0:T(8,128)(2,1)S(1)}, u32[]{:S(2)}, u32[]{:S(2)}) collective-permute-start(bf16[160,128]{1,0:T(8,128)(2,1)} %bitcast.50), channel_id=1, source_target_pairs={{0,1},{1,0},{2,3},{3,2},{4,5},{5,4},{6,7},{7,6},{8,9},{9,8},{10,11... | collective-permute-start | bytes 122888 | tf_op jit(solution)/shard_map/ppermute | solution.py:19
  76.4 1.0 slice.29
  77.4 0.1 collective-permute-start.13
  77.6 0.9 convolution_convert_fusion.1
  78.5 8.2 %collective-permute-start.15 = (bf16[160,128]{1,0:T(8,128)(2,1)S(1)}, bf16[160,128]{1,0:T(8,128)(2,1)S(1)}, u32[]{:S(2)}, u32[]{:S(2)}) collective-permute-start(bf16[160,128]{1,0:T(8,128)(2,1)S(1)} %convolution_convert_fusion.1), channel_id=1, source_target_pairs={{0,24},{2,26},{4,28},{6,30},{8,16},{10,18},{12,20},{14,22},{16,8},... | collective-permute-start | bytes 122888 | tf_op jit(solution)/shard_map/ppermute | solution.py:272
  86.7 0.4 collective-permute-start.17
  87.1 0.7 copy-done.13
  87.8 5.0 %shard_map.129 = bf16[2,8,48,640]{3,2,1,0:T(8,128)(2,1)} custom-call(s32[1]{0:T(128)} %bitcast.refs_0_, bf16[320,1280]{1,0:T(8,128)(2,1)} %collective-permute-done.11.refs_8_.refs_1_.refs_2_, bf16[320,1280]{1,0:T(8,128)(2,1)} %collective-permute-done.11.refs_8_.refs_1_.refs_2_, bf16[128,1280]{1,0:T(8,128)(2,1)} %copy-done.13, bf16[320,1280]{1,0:T(8,128)(2,1)} %copy-done.2, ...), custom_call_target="tpu_custom_call" | custom-call | flops 1258291200 | bytes 5242880 | tf_op jit(solution)/shard_map/pallas_call | solution.py:90
  92.9 0.6 collective-permute-done.17
  93.5 6.8 %all-to-all-start.2 = ((bf16[16,48,640]{2,1,0:T(8,128)(2,1)}), bf16[16,48,640]{2,1,0:T(8,128)(2,1)S(1)}, u32[]{:S(2)}, u32[]{:S(2)}) async-start(bf16[16,48,640]{2,1,0:T(8,128)(2,1)} %bitcast.42), calls=%async_computation.2 | async-start | bytes 1966080 | tf_op jit(solution)/shard_map/all_to_all | solution.py:246
  100.3 0.1 collective-permute-start.18
  100.4 2.0 %collective-permute-start.19 = (bf16[2,2,160,128]{3,2,1,0:T(8,128)(2,1)S(1)}, bf16[2,2,160,128]{3,2,1,0:T(8,128)(2,1)S(1)}, u32[]{:S(2)}, u32[]{:S(2)}) collective-permute-start(bf16[2,2,160,128]{3,2,1,0:T(8,128)(2,1)S(1)} %pad_maximum_fusion.3.near), channel_id=1, source_target_pairs={{0,2},{2,4},{4,6},{6,8},{8,10},{10,12},{12,14},{14,0},{1,3},{3,5},... | collective-permute-start | bytes 491528 | tf_op jit(solution)/shard_map/ppermute | solution.py:19
  102.4 2.3 %collective-permute-start.20 = (bf16[2,2,160,128]{3,2,1,0:T(8,128)(2,1)S(1)}, bf16[2,2,160,128]{3,2,1,0:T(8,128)(2,1)S(1)}, u32[]{:S(2)}, u32[]{:S(2)}) collective-permute-start(bf16[2,2,160,128]{3,2,1,0:T(8,128)(2,1)S(1)} %pad_maximum_fusion.3.near), channel_id=1, source_target_pairs={{0,14},{2,0},{4,2},{6,4},{8,6},{10,8},{12,10},{14,12},{1,15},{3,1}... | collective-permute-start | bytes 491528 | tf_op jit(solution)/shard_map/ppermute | solution.py:19
  104.7 0.1 pad_add_fusion.place_ref
  104.7 0.2 reduce_sum.52
  105.0 0.0 copy-start.15
  105.0 0.0 copy-start.16
  105.0 0.0 copy-start.17
  105.0 0.0 copy-start.18
  105.0 1.7 %collective-permute-done.18.two = bf16[2,2,160,128]{3,2,1,0:T(8,128)(2,1)S(1)} collective-permute-done((bf16[2,2,160,128]{3,2,1,0:T(8,128)(2,1)S(1)}, bf16[2,2,160,128]{3,2,1,0:T(8,128)(2,1)S(1)}, u32[]{:S(2)}, u32[]{:S(2)}) %collective-permute-start.18) | collective-permute-done | bytes 163872 | tf_op jit(solution)/shard_map/ppermute | solution.py:19
  106.8 8.9 %collective-permute-done.19.below = bf16[2,2,160,128]{3,2,1,0:T(8,128)(2,1)S(1)} collective-permute-done((bf16[2,2,160,128]{3,2,1,0:T(8,128)(2,1)S(1)}, bf16[2,2,160,128]{3,2,1,0:T(8,128)(2,1)S(1)}, u32[]{:S(2)}, u32[]{:S(2)}) %collective-permute-start.19) | collective-permute-done | bytes 163872 | tf_op jit(solution)/shard_map/ppermute | solution.py:19
  115.7 0.6 shard_map.130
  116.3 0.6 collective-permute-start.22
  116.8 0.1 reduce_sum.53
  117.0 0.1 fusion.15
  117.1 0.9 collective-permute-start.21
  118.0 0.6 collective-permute-done.22
  118.5 0.3 collective-permute-done.21
  118.9 2.3 %fusion = bf16[320,2560]{1,0:T(8,128)(2,1)} fusion(bf16[2560,128]{1,0:T(8,128)(2,1)S(1)} %collective-permute-done.22, bf16[2560,128]{1,0:T(8,128)(2,1)S(1)} %bitcast.41, bf16[128,320]{1,0:T(8,128)(2,1)S(1)} %collective-permute-done.21, bf16[128,320]{1,0:T(8,128)(2,1)S(1)} %get-tuple-element.77, s32[256]{0:T(256)S(1)} %fusion.26), kind=kOutput, calls=%fused_computation.3 | convolution fusion | flops 760283136 | bytes 3113984 | tf_op jit(solution)/shard_map/dot_general | solution.py:304
  121.2 5.0 %all-to-all-start.3 = ((bf16[8,40,2560]{2,1,0:T(8,128)(2,1)}), bf16[8,40,2560]{2,1,0:T(8,128)(2,1)S(1)}, u32[]{:S(2)}, u32[]{:S(2)}) async-start(bf16[8,40,2560]{2,1,0:T(8,128)(2,1)} %bitcast.25), calls=%async_computation.3 | async-start | bytes 3276800 | tf_op jit(solution)/shard_map/all_to_all | solution.py:308
  126.2 21.3 %all-to-all-done.3 = bf16[8,40,2560]{2,1,0:T(8,128)(2,1)S(1)} async-done(((bf16[8,40,2560]{2,1,0:T(8,128)(2,1)}), bf16[8,40,2560]{2,1,0:T(8,128)(2,1)S(1)}, u32[]{:S(2)}, u32[]{:S(2)}) %all-to-all-start.3) | async-done | bytes 1638432 | tf_op jit(solution)/shard_map/all_to_all | solution.py:308
  147.4 0.6 fusion.1
  148.1 1.0 fusion.9
  (63 shorter events, 0.4 us)
Async XLA Ops:
  0.0 8.5 %collective-permute-start = (bf16[8,5120]{1,0:T(8,128)(2,1)}, bf16[8,5120]{1,0:T(8,128)(2,1)S(1)}, u32[]{:S(2)}, u32[]{:S(2)}) collective-permute-start(bf16[8,5120]{1,0:T(8,128)(2,1)} %param.13), channel_id=1, source_target_pairs={{0,16},{16,0},{1,17},{17,1},{2,18},{18,2},{3,19},{19,3},{4,20},{20... | collective-permute-start | bytes 245768 | tf_op jit(solution)/shard_map/ppermute | solution.py:19
  3.6 16.5 %all-to-all-start = ((bf16[16,8,1280]{2,1,0:T(8,128)(2,1)}), bf16[16,8,1280]{2,1,0:T(8,128)(2,1)S(1)}, u32[]{:S(2)}, u32[]{:S(2)}) async-start(bf16[16,8,1280]{2,1,0:T(8,128)(2,1)} %bitcast.47), calls=%async_computation | async-start | bytes 655360 | tf_op jit(solution)/shard_map/all_to_all | solution.py:219
  9.4 7.2 %copy-start.12 = (bf16[64,1280]{1,0:T(8,128)(2,1)}, bf16[64,1280]{1,0:T(8,128)(2,1)S(1)}, u32[]{:S(2)}) copy-start(bf16[64,1280]{1,0:T(8,128)(2,1)S(1)} %pad_maximum_fusion.2.refs_1_) | copy-start | bytes 491524
  9.4 8.3 %collective-permute-start.1 = (bf16[64,1280]{1,0:T(8,128)(2,1)S(1)}, bf16[64,1280]{1,0:T(8,128)(2,1)S(1)}, u32[]{:S(2)}, u32[]{:S(2)}) collective-permute-start(bf16[64,1280]{1,0:T(8,128)(2,1)S(1)} %pad_maximum_fusion.2.refs_1_), channel_id=1, source_target_pairs={{0,2},{1,15},{2,4},{3,1},{4,6},{5,3},{6,8},{7,5},{8,10},{9,7},{10,... | collective-permute-start | bytes 491528 | tf_op jit(solution)/shard_map/ppermute | solution.py:212
  15.0 5.0 %collective-permute-start.2 = (bf16[64,1280]{1,0:T(8,128)(2,1)S(1)}, bf16[64,1280]{1,0:T(8,128)(2,1)S(1)}, u32[]{:S(2)}, u32[]{:S(2)}) collective-permute-start(bf16[64,1280]{1,0:T(8,128)(2,1)S(1)} %pad_maximum_fusion.2.refs_1_), channel_id=1, source_target_pairs={{0,15},{1,2},{2,1},{3,4},{4,3},{5,6},{6,5},{7,8},{8,7},{9,10},{10,... | collective-permute-start | bytes 491528 | tf_op jit(solution)/shard_map/ppermute | solution.py:212
  16.6 37.9 %copy-start.2 = (bf16[320,1280]{1,0:T(8,128)(2,1)}, bf16[320,1280]{1,0:T(8,128)(2,1)S(1)}, u32[]{:S(2)}) copy-start(bf16[320,1280]{1,0:T(8,128)(2,1)S(1)} %get-tuple-element.53.refs_6_.refs_4_) | copy-start | bytes 2457604
  17.7 16.7 %copy-start.10 = (bf16[64,1280]{1,0:T(8,128)(2,1)}, bf16[64,1280]{1,0:T(8,128)(2,1)S(1)}, u32[]{:S(2)}) copy-start(bf16[64,1280]{1,0:T(8,128)(2,1)S(1)} %collective-permute-done.1.refs_2_) | copy-start | bytes 491524
  20.1 14.3 %copy-start.11 = (bf16[64,1280]{1,0:T(8,128)(2,1)}, bf16[64,1280]{1,0:T(8,128)(2,1)S(1)}, u32[]{:S(2)}) copy-start(bf16[64,1280]{1,0:T(8,128)(2,1)S(1)} %collective-permute-done.2.refs_3_) | copy-start | bytes 491524
  20.1 14.2 %collective-permute-start.4 = (bf16[256,1280]{1,0:T(8,128)(2,1)S(1)}, bf16[256,1280]{1,0:T(8,128)(2,1)S(1)}, u32[]{:S(2)}, u32[]{:S(2)}) collective-permute-start(bf16[256,1280]{1,0:T(8,128)(2,1)S(1)} %pad_maximum_fusion.1), channel_id=1, source_target_pairs={{0,2},{1,15},{2,4},{3,1},{4,6},{5,3},{6,8},{7,5},{8,10},{9,7},{10,... | collective-permute-start | bytes 1966088 | tf_op jit(solution)/shard_map/ppermute | solution.py:212
  22.6 11.7 %collective-permute-start.3 = (bf16[160,1280]{1,0:T(8,128)(2,1)S(1)}, bf16[160,1280]{1,0:T(8,128)(2,1)S(1)}, u32[]{:S(2)}, u32[]{:S(2)}) collective-permute-start(bf16[160,1280]{1,0:T(8,128)(2,1)S(1)} %slice.24), channel_id=1, source_target_pairs={{0,16},{16,0},{1,17},{17,1},{2,18},{18,2},{3,19},{19,3},{4,20},{20... | collective-permute-start | bytes 1228808 | tf_op jit(solution)/shard_map/ppermute | solution.py:19
  25.3 8.2 %collective-permute-start.5 = (bf16[128,1280]{1,0:T(8,128)(2,1)S(1)}, bf16[128,1280]{1,0:T(8,128)(2,1)S(1)}, u32[]{:S(2)}, u32[]{:S(2)}) collective-permute-start(bf16[128,1280]{1,0:T(8,128)(2,1)S(1)} %bitcast.38), channel_id=1, source_target_pairs={{0,15},{1,2},{2,1},{3,4},{4,3},{5,6},{6,5},{7,8},{8,7},{9,10},{10,... | collective-permute-start | bytes 983048 | tf_op jit(solution)/shard_map/ppermute | solution.py:212
  34.4 20.1 %copy-start.4 = (bf16[160,1280]{1,0:T(8,128)(2,1)}, bf16[160,1280]{1,0:T(8,128)(2,1)S(1)}, u32[]{:S(2)}) copy-start(bf16[160,1280]{1,0:T(8,128)(2,1)S(1)} %collective-permute-done.3.refs_8_.refs_6_) | copy-start | bytes 1228804
  34.4 20.1 %copy-start.1 = (bf16[256,1280]{1,0:T(8,128)(2,1)}, bf16[256,1280]{1,0:T(8,128)(2,1)S(1)}, u32[]{:S(2)}) copy-start(bf16[256,1280]{1,0:T(8,128)(2,1)S(1)} %collective-permute-done.4.refs_2_.refs_4_.refs_5_) | copy-start | bytes 1966084
  34.4 5.4 %copy-start.8 = (bf16[5120,80]{0,1:T(8,128)(2,1)S(1)}, bf16[5120,80]{0,1:T(8,128)(2,1)}, u32[]{:S(2)}) copy-start(bf16[5120,80]{0,1:T(8,128)(2,1)} %param.15) | copy-start | bytes 2457604
  34.5 15.2 %collective-permute-start.7 = (bf16[384,1280]{1,0:T(8,128)(2,1)S(1)}, bf16[384,1280]{1,0:T(8,128)(2,1)S(1)}, u32[]{:S(2)}, u32[]{:S(2)}) collective-permute-start(bf16[384,1280]{1,0:T(8,128)(2,1)S(1)} %pad_maximum_fusion), channel_id=1, source_target_pairs={{0,2},{1,15},{2,4},{3,1},{4,6},{5,3},{6,8},{7,5},{8,10},{9,7},{10,... | collective-permute-start | bytes 2949128 | tf_op jit(solution)/shard_map/ppermute | solution.py:212
  37.0 12.7 %collective-permute-start.6 = (bf16[160,1280]{1,0:T(8,128)(2,1)S(1)}, bf16[160,1280]{1,0:T(8,128)(2,1)S(1)}, u32[]{:S(2)}, u32[]{:S(2)}) collective-permute-start(bf16[160,1280]{1,0:T(8,128)(2,1)S(1)} %slice.25), channel_id=1, source_target_pairs={{0,16},{16,0},{1,17},{17,1},{2,18},{18,2},{3,19},{19,3},{4,20},{20... | collective-permute-start | bytes 1228808 | tf_op jit(solution)/shard_map/ppermute | solution.py:19
  39.7 12.9 %collective-permute-start.8 = (bf16[320,1280]{1,0:T(8,128)(2,1)S(1)}, bf16[320,1280]{1,0:T(8,128)(2,1)S(1)}, u32[]{:S(2)}, u32[]{:S(2)}) collective-permute-start(bf16[320,1280]{1,0:T(8,128)(2,1)S(1)} %get-tuple-element.53.refs_6_.refs_4_), channel_id=1, source_target_pairs={{0,1},{1,0},{2,3},{3,2},{4,5},{5,4},{6,7},{7,6},{8,9},{9,8},{10,11... | collective-permute-start | bytes 2457608 | tf_op jit(solution)/shard_map/ppermute | solution.py:19
  39.8 21.0 %collective-permute-start.12 = (bf16[80,5120]{1,0:T(8,128)(2,1)S(1)}, bf16[80,5120]{1,0:T(8,128)(2,1)S(1)}, u32[]{:S(2)}, u32[]{:S(2)}) collective-permute-start(bf16[80,5120]{1,0:T(8,128)(2,1)S(1)} %bitcast.46), channel_id=1, source_target_pairs={{0,1},{1,0},{2,3},{3,2},{4,5},{5,4},{6,7},{7,6},{8,9},{9,8},{10,11... | collective-permute-start | bytes 2457608 | tf_op jit(solution)/shard_map/ppermute | solution.py:19
  49.8 11.0 %copy-start.5 = (bf16[160,1280]{1,0:T(8,128)(2,1)}, bf16[160,1280]{1,0:T(8,128)(2,1)S(1)}, u32[]{:S(2)}) copy-start(bf16[160,1280]{1,0:T(8,128)(2,1)S(1)} %collective-permute-done.6.refs_9_.refs_7_) | copy-start | bytes 1228804
  49.8 11.0 %copy-start = (bf16[384,1280]{1,0:T(8,128)(2,1)}, bf16[384,1280]{1,0:T(8,128)(2,1)S(1)}, u32[]{:S(2)}) copy-start(bf16[384,1280]{1,0:T(8,128)(2,1)S(1)} %collective-permute-done.7.refs_4_.refs_5_.refs_6_.refs_7_) | copy-start | bytes 2949124
  49.8 11.7 %collective-permute-start.11 = (bf16[320,1280]{1,0:T(8,128)(2,1)S(1)}, bf16[320,1280]{1,0:T(8,128)(2,1)}, u32[]{:S(2)}, u32[]{:S(2)}) collective-permute-start(bf16[320,1280]{1,0:T(8,128)(2,1)S(1)} %slice.28), channel_id=1, source_target_pairs={{0,2},{1,15},{2,4},{3,1},{4,6},{5,3},{6,8},{7,5},{8,10},{9,7},{10,... | collective-permute-start | bytes 2457608 | tf_op jit(solution)/shard_map/ppermute | solution.py:212
  51.3 2.6 %collective-permute-start.9 = (bf16[160,1280]{1,0:T(8,128)(2,1)S(1)}, bf16[160,1280]{1,0:T(8,128)(2,1)S(1)}, u32[]{:S(2)}, u32[]{:S(2)}) collective-permute-start(bf16[160,1280]{1,0:T(8,128)(2,1)S(1)} %collective-permute-done.3.refs_8_.refs_6_), channel_id=1, source_target_pairs={{0,1},{1,0},{2,3},{3,2},{4,5},{5,4},{6,7},{7,6},{8,9},{9,8},{10,11... | collective-permute-start | bytes 1228808 | tf_op jit(solution)/shard_map/ppermute | solution.py:19
  52.5 2.0 %collective-permute-start.10 = (bf16[160,1280]{1,0:T(8,128)(2,1)S(1)}, bf16[160,1280]{1,0:T(8,128)(2,1)S(1)}, u32[]{:S(2)}, u32[]{:S(2)}) collective-permute-start(bf16[160,1280]{1,0:T(8,128)(2,1)S(1)} %collective-permute-done.6.refs_9_.refs_7_), channel_id=1, source_target_pairs={{0,1},{1,0},{2,3},{3,2},{4,5},{5,4},{6,7},{7,6},{8,9},{9,8},{10,11... | collective-permute-start | bytes 1228808 | tf_op jit(solution)/shard_map/ppermute | solution.py:19
  52.6 8.2 %copy-start.3 = (bf16[320,1280]{1,0:T(8,128)(2,1)}, bf16[320,1280]{1,0:T(8,128)(2,1)S(1)}, u32[]{:S(2)}) copy-start(bf16[320,1280]{1,0:T(8,128)(2,1)S(1)} %collective-permute-done.8.refs_7_.refs_5_) | copy-start | bytes 2457604
  53.9 7.0 %copy-start.6 = (bf16[160,1280]{1,0:T(8,128)(2,1)}, bf16[160,1280]{1,0:T(8,128)(2,1)S(1)}, u32[]{:S(2)}) copy-start(bf16[160,1280]{1,0:T(8,128)(2,1)S(1)} %collective-permute-done.9.refs_10_.refs_8_) | copy-start | bytes 1228804
  54.4 6.4 %copy-start.7 = (bf16[160,1280]{1,0:T(8,128)(2,1)}, bf16[160,1280]{1,0:T(8,128)(2,1)S(1)}, u32[]{:S(2)}) copy-start(bf16[160,1280]{1,0:T(8,128)(2,1)S(1)} %collective-permute-done.10.refs_11_.refs_9_) | copy-start | bytes 1228804
  60.9 0.9 copy-start.9
  61.8 31.7 %all-to-all-start.1 = ((bf16[16,80,640]{2,1,0:T(8,128)(2,1)}), bf16[16,80,640]{2,1,0:T(8,128)(2,1)S(1)}, u32[]{:S(2)}, u32[]{:S(2)}) async-start(bf16[16,80,640]{2,1,0:T(8,128)(2,1)} %bitcast.14), calls=%async_computation.1 | async-start | bytes 3276800 | tf_op jit(solution)/shard_map/all_to_all | solution.py:246
  68.1 9.4 %copy-start.19 = (s32[128]{0:T(128)S(1)}, s32[128]{0:T(128)}, u32[]{:S(2)}) copy-start(s32[128]{0:T(128)} %constant.91.clone) | copy-start | bytes 1540
  68.1 9.4 %copy-start.20 = (s32[128]{0:T(128)S(1)}, s32[128]{0:T(128)}, u32[]{:S(2)}) copy-start(s32[128]{0:T(128)} %constant.92.clone) | copy-start | bytes 1540
  68.1 9.4 %copy-start.21 = (s32[128]{0:T(128)S(1)}, s32[128]{0:T(128)}, u32[]{:S(2)}) copy-start(s32[128]{0:T(128)} %constant.93.clone) | copy-start | bytes 1540
  71.6 6.0 %collective-permute-start.14 = (bf16[160,128]{1,0:T(8,128)(2,1)}, bf16[160,128]{1,0:T(8,128)(2,1)S(1)}, u32[]{:S(2)}, u32[]{:S(2)}) collective-permute-start(bf16[160,128]{1,0:T(8,128)(2,1)} %bitcast.50), channel_id=1, source_target_pairs={{0,1},{1,0},{2,3},{3,2},{4,5},{5,4},{6,7},{7,6},{8,9},{9,8},{10,11... | collective-permute-start | bytes 122888 | tf_op jit(solution)/shard_map/ppermute | solution.py:19
  77.4 9.7 %collective-permute-start.13 = (bf16[128,1280]{1,0:T(8,128)(2,1)S(1)}, bf16[128,1280]{1,0:T(8,128)(2,1)S(1)}, u32[]{:S(2)}, u32[]{:S(2)}) collective-permute-start(bf16[128,1280]{1,0:T(8,128)(2,1)S(1)} %slice.29), channel_id=1, source_target_pairs={{0,2},{1,15},{2,4},{3,1},{4,6},{5,3},{6,8},{7,5},{8,10},{9,7},{10,... | collective-permute-start | bytes 983048 | tf_op jit(solution)/shard_map/ppermute | solution.py:212
  78.5 14.3 %collective-permute-start.15 = (bf16[160,128]{1,0:T(8,128)(2,1)S(1)}, bf16[160,128]{1,0:T(8,128)(2,1)S(1)}, u32[]{:S(2)}, u32[]{:S(2)}) collective-permute-start(bf16[160,128]{1,0:T(8,128)(2,1)S(1)} %convolution_convert_fusion.1), channel_id=1, source_target_pairs={{0,24},{2,26},{4,28},{6,30},{8,16},{10,18},{12,20},{14,22},{16,8},... | collective-permute-start | bytes 122888 | tf_op jit(solution)/shard_map/ppermute | solution.py:272
  86.7 6.2 %collective-permute-start.16 = (bf16[160,128]{1,0:T(8,128)(2,1)S(1)}, bf16[160,128]{1,0:T(8,128)(2,1)S(1)}, u32[]{:S(2)}, u32[]{:S(2)}) collective-permute-start(bf16[160,128]{1,0:T(8,128)(2,1)S(1)} %convolution_convert_fusion.1), channel_id=1, source_target_pairs={{0,16},{16,0},{1,17},{17,1},{2,18},{18,2},{3,19},{19,3},{4,20},{20... | collective-permute-start | bytes 122888 | tf_op jit(solution)/shard_map/ppermute | solution.py:19
  86.7 6.8 %collective-permute-start.17 = (bf16[160,128]{1,0:T(8,128)(2,1)S(1)}, bf16[160,128]{1,0:T(8,128)(2,1)S(1)}, u32[]{:S(2)}, u32[]{:S(2)}) collective-permute-start(bf16[160,128]{1,0:T(8,128)(2,1)S(1)} %convolution_convert_fusion.1), channel_id=1, source_target_pairs={{0,8},{2,10},{4,12},{6,14},{8,0},{10,2},{12,4},{14,6},{1,9},{3,11}... | collective-permute-start | bytes 122888 | tf_op jit(solution)/shard_map/ppermute | solution.py:19
  87.1 0.7 copy-start.13
  93.5 23.3 %all-to-all-start.2 = ((bf16[16,48,640]{2,1,0:T(8,128)(2,1)}), bf16[16,48,640]{2,1,0:T(8,128)(2,1)S(1)}, u32[]{:S(2)}, u32[]{:S(2)}) async-start(bf16[16,48,640]{2,1,0:T(8,128)(2,1)} %bitcast.42), calls=%async_computation.2 | async-start | bytes 1966080 | tf_op jit(solution)/shard_map/all_to_all | solution.py:246
  100.3 6.5 %collective-permute-start.18 = (bf16[2,2,160,128]{3,2,1,0:T(8,128)(2,1)S(1)}, bf16[2,2,160,128]{3,2,1,0:T(8,128)(2,1)S(1)}, u32[]{:S(2)}, u32[]{:S(2)}) collective-permute-start(bf16[2,2,160,128]{3,2,1,0:T(8,128)(2,1)S(1)} %pad_maximum_fusion.3.near), channel_id=1, source_target_pairs={{0,4},{2,6},{4,8},{6,10},{8,12},{10,14},{12,0},{14,2},{1,5},{3,7},... | collective-permute-start | bytes 491528 | tf_op jit(solution)/shard_map/ppermute | solution.py:19
  100.4 15.3 %collective-permute-start.19 = (bf16[2,2,160,128]{3,2,1,0:T(8,128)(2,1)S(1)}, bf16[2,2,160,128]{3,2,1,0:T(8,128)(2,1)S(1)}, u32[]{:S(2)}, u32[]{:S(2)}) collective-permute-start(bf16[2,2,160,128]{3,2,1,0:T(8,128)(2,1)S(1)} %pad_maximum_fusion.3.near), channel_id=1, source_target_pairs={{0,2},{2,4},{4,6},{6,8},{8,10},{10,12},{12,14},{14,0},{1,3},{3,5},... | collective-permute-start | bytes 491528 | tf_op jit(solution)/shard_map/ppermute | solution.py:19
  102.4 13.3 %collective-permute-start.20 = (bf16[2,2,160,128]{3,2,1,0:T(8,128)(2,1)S(1)}, bf16[2,2,160,128]{3,2,1,0:T(8,128)(2,1)S(1)}, u32[]{:S(2)}, u32[]{:S(2)}) collective-permute-start(bf16[2,2,160,128]{3,2,1,0:T(8,128)(2,1)S(1)} %pad_maximum_fusion.3.near), channel_id=1, source_target_pairs={{0,14},{2,0},{4,2},{6,4},{8,6},{10,8},{12,10},{14,12},{1,15},{3,1}... | collective-permute-start | bytes 491528 | tf_op jit(solution)/shard_map/ppermute | solution.py:19
  105.0 13.0 %copy-start.14 = (s32[256]{0:T(256)S(1)}, s32[256]{0:T(256)}, u32[]{:S(2)}) copy-start(s32[256]{0:T(256)} %constant.94.clone) | copy-start | bytes 3076
  105.0 13.0 %copy-start.15 = (s32[256]{0:T(256)S(1)}, s32[256]{0:T(256)}, u32[]{:S(2)}) copy-start(s32[256]{0:T(256)} %constant.95.clone) | copy-start | bytes 3076
  105.0 12.9 %copy-start.16 = (s32[256]{0:T(256)S(1)}, s32[256]{0:T(256)}, u32[]{:S(2)}) copy-start(s32[256]{0:T(256)} %constant.96.clone) | copy-start | bytes 3076
  105.0 12.9 %copy-start.17 = (s32[256]{0:T(256)S(1)}, s32[256]{0:T(256)}, u32[]{:S(2)}) copy-start(s32[256]{0:T(256)} %constant.97.clone) | copy-start | bytes 3076
  105.0 12.9 %copy-start.18 = (s32[256]{0:T(256)S(1)}, s32[256]{0:T(256)}, u32[]{:S(2)}) copy-start(s32[256]{0:T(256)} %constant.98.clone) | copy-start | bytes 3076
  116.3 2.3 %collective-permute-start.22 = (bf16[2560,128]{1,0:T(8,128)(2,1)S(1)}, bf16[2560,128]{1,0:T(8,128)(2,1)S(1)}, u32[]{:S(2)}, u32[]{:S(2)}) collective-permute-start(bf16[2560,128]{1,0:T(8,128)(2,1)S(1)} %bitcast.40), channel_id=1, source_target_pairs={{0,1},{1,0},{2,3},{3,2},{4,5},{5,4},{6,7},{7,6},{8,9},{9,8},{10,11... | collective-permute-start | bytes 1966088 | tf_op jit(solution)/shard_map/ppermute | solution.py:19
  117.1 1.8 %collective-permute-start.21 = (bf16[128,320]{1,0:T(8,128)(2,1)S(1)}, bf16[128,320]{1,0:T(8,128)(2,1)S(1)}, u32[]{:S(2)}, u32[]{:S(2)}) collective-permute-start(bf16[128,320]{1,0:T(8,128)(2,1)S(1)} %get-tuple-element.78), channel_id=1, source_target_pairs={{0,1},{1,0},{2,3},{3,2},{4,5},{5,4},{6,7},{7,6},{8,9},{9,8},{10,11... | collective-permute-start | bytes 245768 | tf_op jit(solution)/shard_map/ppermute | solution.py:19
  121.2 5.0 %copy-start.22 = (s32[8]{0:T(128)S(1)}, s32[8]{0:T(128)}, u32[]{:S(2)}) copy-start(s32[8]{0:T(128)} %param.17) | copy-start | bytes 100
  121.2 26.3 %all-to-all-start.3 = ((bf16[8,40,2560]{2,1,0:T(8,128)(2,1)}), bf16[8,40,2560]{2,1,0:T(8,128)(2,1)S(1)}, u32[]{:S(2)}, u32[]{:S(2)}) async-start(bf16[8,40,2560]{2,1,0:T(8,128)(2,1)} %bitcast.25), calls=%async_computation.3 | async-start | bytes 3276800 | tf_op jit(solution)/shard_map/all_to_all | solution.py:308
